TPU v7x, 128 devices: a whole 4x4x4 slice. The times are simulated.
128 devices in a mesh: lat: 8 (over y, core), lon: 16 (over z, x).
Axes of the slice: x: 4, y: 4, z: 4, core: 2. Of those that a mesh axis runs over, the one named last changes fastest.
Arguments:
- tokens: bfloat16 [64, 256, 1024], P('lat', 'lon'), may hold values from -36 to 36
- shifts: int32 [2], replicated, may hold values from 1 to 7, as said below
- w_qkv: bfloat16 [1024, 3072], replicated, may hold values from -0.1875 to 0.1875
- w_out: bfloat16 [1024, 1024], replicated, may hold values from -0.1875 to 0.1875
- router: bfloat16 [1024, 64], replicated, may hold values from -0.1875 to 0.1875
- expert_ids: int32 [8, 16, 128, 2], P('lat', 'lon'), may hold values from 0 to 63, all different within a row; in each aligned block of 128 rows (0 to 127, 128 to 255, ..., all dimensions but the last counted through in order) at most 6 rows name the same one
- w_gate: bfloat16 [1024, 65536], P(None, ('lat', 'lon')), may hold values from -0.1875 to 0.1875
- w_up: bfloat16 [1024, 65536], P(None, ('lat', 'lon')), may hold values from -0.1875 to 0.1875
- w_down: bfloat16 [65536, 1024], P(('lat', 'lon')), may hold values from -0.1875 to 0.1875
Outputs:
- layer_out: bfloat16 [64, 256, 1024], P('lat', 'lon')
Inputs may be any that keep to these rules, and one draw needn't show every extreme that they name: `expert_ids`: each token names two different experts; no expert is named by more than 6 of one device's tokens, a bound that some block reaches. The two shifts differ, and one of them is 7.
All inputs are finite; a program needn't handle non-finite values.
Results may differ from a plain program's by a relative error of at most 0.0095.
Values may be sent and summed in bfloat16 or wider, within the bound.
No kernel may reach another device: no remote copies, remote signals or barrier semaphores. Data moves between devices by JAX's collectives and lax.ppermute only.
A program may use at most 64 MiB of HBM per device.

v0:
```python
import jax
import jax.numpy as jnp
from jax import lax
from jax.sharding import PartitionSpec as P

HEAD = 64
FF = 1024
TOP = 2
WIN = 8
MOST = 6


def padded(x, sides, width):
    for axis, dim in sides:
        size, length = (lax.axis_size(axis), x.shape[dim])
        up = [(i, (i + 1) % size) for i in range(size)]
        down = [(j, i) for i, j in up]
        last = lax.slice_in_dim(x, length - width, length, axis=dim)
        leading = lax.slice_in_dim(x, 0, width, axis=dim)
        before = lax.ppermute(last, axis, up)
        after = lax.ppermute(leading, axis, down)
        x = jnp.concatenate([before, x, after], axis=dim)
    return x


def rms_rows(x):
    xf = x.astype(jnp.float32)
    return xf * lax.rsqrt(jnp.mean(xf * xf, axis=-1, keepdims=True) + 1e-05)


def window_attention(qkv, key_valid):
    query = qkv[:, :, 0]
    keys = qkv[:, :, 1]
    values = qkv[:, :, 2]
    qn = rms_rows(query).astype(jnp.bfloat16)
    kn = rms_rows(keys).astype(jnp.bfloat16)
    scores = jnp.einsum("wqhd,wkhd->whqk", qn, kn, preferred_element_type=jnp.float32) / jnp.sqrt(
        jnp.float32(HEAD)
    )
    expd = jnp.exp(scores) * key_valid[:, None, None, :]
    total = jnp.sum(expd, axis=-1, keepdims=True)
    total = jnp.where(total > 0, total, 1.0)
    weights = (expd / total).astype(jnp.bfloat16)
    return jnp.einsum(
        "whqk,wkhd->wqhd", weights, values, preferred_element_type=jnp.float32
    ).astype(jnp.bfloat16)


def body(tokens, shifts, w_qkv, w_out, router, expert_ids, w_gate, w_up, w_down):
    n_lat = lax.axis_size("lat")
    n_lon = lax.axis_size("lon")
    devices = n_lat * n_lon
    rows, cols, width = tokens.shape
    heads = width // HEAD
    s_lat = shifts[0]
    s_lon = shifts[1]
    normed = rms_rows(tokens).astype(jnp.bfloat16)
    extended = padded(normed, (("lat", 0), ("lon", 1)), WIN)
    window_cells = lax.dynamic_slice(
        extended, (WIN - s_lat, WIN - s_lon, 0), (rows + WIN, cols + WIN, width)
    )
    qkv = jnp.dot(
        window_cells.reshape(-1, width), w_qkv, preferred_element_type=jnp.float32
    ).astype(jnp.bfloat16)
    win_lat = rows // WIN + 1
    win_lon = cols // WIN + 1
    windows = qkv.reshape(win_lat, WIN, win_lon, WIN, 3, heads, HEAD).transpose(0, 2, 1, 3, 4, 5, 6)
    windows = windows.reshape(win_lat * win_lon, WIN * WIN, 3, heads, HEAD)
    global_rows = lax.axis_index("lat") * rows - s_lat + jnp.arange(rows + WIN, dtype=jnp.int32)
    row_valid = ((global_rows >= 0) & (global_rows < rows * n_lat)).astype(jnp.float32)
    key_valid = jnp.broadcast_to(
        row_valid.reshape(win_lat, WIN)[:, None, :, None], (win_lat, win_lon, WIN, WIN)
    )
    key_valid = key_valid.reshape(win_lat * win_lon, WIN * WIN)
    attended = window_attention(windows, key_valid)
    attended = (
        attended.reshape(win_lat, win_lon, WIN, WIN, width)
        .transpose(0, 2, 1, 3, 4)
        .reshape(rows + WIN, cols + WIN, width)
    )
    mine = lax.dynamic_slice(attended, (s_lat, s_lon, 0), (rows, cols, width))
    projected = jnp.dot(mine.reshape(-1, width), w_out, preferred_element_type=jnp.float32)
    mixed = (tokens.reshape(-1, width).astype(jnp.float32) + projected).astype(jnp.bfloat16)
    normed2 = rms_rows(mixed).astype(jnp.bfloat16)
    logits = jnp.dot(normed2, router, preferred_element_type=jnp.float32)
    experts = router.shape[1]
    ids = expert_ids.reshape(-1, TOP)
    expert_iota = jnp.arange(experts, dtype=jnp.int32)
    picks = ids[:, :, None] == expert_iota[None, None, :]
    chosen = jnp.sum(jnp.where(picks, logits[:, None, :], 0.0), axis=-1)
    sig = jax.nn.sigmoid(chosen)
    gates = sig / jnp.sum(sig, axis=1, keepdims=True)
    flat = ids.reshape(-1)
    onehot = (flat[:, None] == expert_iota[None, :]).astype(jnp.int32)
    rank = jnp.sum(jnp.cumsum(onehot, axis=0) * onehot, axis=1) - 1
    share = w_gate.shape[1]
    piece = min(FF, share)
    repl = FF // piece
    group = share // piece
    most = MOST
    cap = group * most
    token_of = jnp.arange(flat.shape[0], dtype=jnp.int32) // TOP
    slot = flat % group * most + rank
    slot_index = jnp.stack(
        [(flat // group * repl + copy) * cap + slot for copy in range(repl)], axis=0
    )
    routed = normed2[token_of]
    send = (
        jnp.zeros((devices * cap, width), jnp.bfloat16)
        .at[slot_index.reshape(-1)]
        .set(jnp.tile(routed, (repl, 1)))
    )
    send = send.reshape(devices, group, most, width)
    received = lax.all_to_all(send, ("lat", "lon"), split_axis=0, concat_axis=0, tiled=True)
    block = received[:, 0].reshape(-1, width)
    gate = jnp.dot(block, w_gate, preferred_element_type=jnp.float32)
    upper = jnp.dot(block, w_up, preferred_element_type=jnp.float32)
    hidden = (jax.nn.silu(gate) * upper).astype(jnp.bfloat16)
    part = jnp.dot(hidden, w_down, preferred_element_type=jnp.float32).astype(jnp.bfloat16)
    results = [part.reshape(received.shape[0], received.shape[2], width)]
    back = lax.all_to_all(
        jnp.stack(results, axis=1), ("lat", "lon"), split_axis=0, concat_axis=0, tiled=True
    )
    back_flat = back.reshape(devices * cap, width)
    combined = jnp.zeros((flat.shape[0], width), jnp.float32)
    for copy in range(repl):
        combined = combined + back_flat[slot_index[copy]].astype(jnp.float32)
    combined = combined.reshape(-1, TOP, width)
    moe = jnp.sum(gates[:, :, None] * combined, axis=1)
    layer_out = (mixed.astype(jnp.float32) + moe).astype(jnp.bfloat16)
    return layer_out.reshape(rows, cols, width)


def solution(mesh):
    placed = (
        P("lat", "lon", None),
        P(),
        P(),
        P(),
        P(),
        P("lat", "lon", None, None),
        P(None, ("lat", "lon")),
        P(None, ("lat", "lon")),
        P(("lat", "lon"), None),
    )
    return jax.shard_map(
        body, mesh=mesh, in_specs=placed, out_specs=P("lat", "lon", None), check_vma=False
    )
```

profile of v0, /device:TPU:1, one launch (start us, length us, event | category | flops | bytes accessed | tf_op | source)
XLA Modules:
  0.0 194.8 jit_solution(3023414176218099438)
XLA Ops:
  0.0 1.2 multiply_reduce_fusion.2
  1.2 1.1 multiply_convert_fusion.2
  2.3 1.4 collective-permute-start.1
  3.7 1.3 collective-permute-start
  5.0 0.7 broadcast_multiply_fusion
  5.7 0.8 copy.59
  6.8 1.3 fusion.28
  8.6 0.6 reduce-window.6
  9.2 0.2 slice_reduce_fusion
  15.9 0.8 fusion.26
  16.7 6.0 %collective-permute-start.3 = (bf16[24,8,1024]{2,1,0:T(8,128)(2,1)}, bf16[24,8,1024]{2,1,0:T(8,128)(2,1)}, u32[]{:S(2)}, u32[]{:S(2)}) collective-permute-start(bf16[24,8,1024]{2,1,0:T(8,128)(2,1)} %get-tuple-element.9), channel_id=1, source_target_pairs={{1,0},{2,1},{3,2},{4,3},{5,4},{6,5},{7,6},{8,7},{9,8},{10,9},{11,1... | collective-permute-start | bytes 1179656 | tf_op jit(solution)/shard_map/ppermute | solution.py:21
  24.0 6.1 %collective-permute-done.3 = bf16[24,8,1024]{2,1,0:T(8,128)(2,1)} collective-permute-done((bf16[24,8,1024]{2,1,0:T(8,128)(2,1)}, bf16[24,8,1024]{2,1,0:T(8,128)(2,1)}, u32[]{:S(2)}, u32[]{:S(2)}) %collective-permute-start.3) | collective-permute-done | bytes 393248 | tf_op jit(solution)/shard_map/ppermute | solution.py:21
  30.1 5.0 %collective-permute-done.2 = bf16[24,8,1024]{2,1,0:T(8,128)(2,1)} collective-permute-done((bf16[24,8,1024]{2,1,0:T(8,128)(2,1)S(1)}, bf16[24,8,1024]{2,1,0:T(8,128)(2,1)}, u32[]{:S(2)}, u32[]{:S(2)}) %collective-permute-start.2) | collective-permute-done | bytes 393248 | tf_op jit(solution)/shard_map/ppermute | solution.py:20
  35.2 2.7 %fusion.15 = bf16[16,24,1024]{2,1,0:T(8,128)(2,1)S(1)} fusion(s32[]{:T(128)S(6)} %select_n.104, s32[]{:T(128)S(6)} %select_n.105, bf16[24,8,1024]{2,1,0:T(8,128)(2,1)} %collective-permute-done.2, bf16[8,16,1024]{2,1,0:T(8,128)(2,1)S(1)} %collective-permute-done, bf16[8,16,1024]{2,1,0:T(8,128)(2,1)S(1)} %multiply_convert_fusion.2, ...), kind=kLoop, calls=%fused_computation.37 | loop fusion | flops 3932160 | bytes 2359304 | tf_op jit(solution)/shard_map/concatenate | solution.py:22
  37.9 6.8 %convolution_convert_fusion = bf16[384,3072]{1,0:T(8,128)(2,1)} fusion(bf16[384,1024]{1,0:T(8,128)(2,1)S(1)} %bitcast.101, bf16[1024,3072]{1,0:T(8,128)(2,1)} %param.11), kind=kOutput, calls=%fused_computation.4 | convolution fusion | flops 2417098752 | bytes 9437184 | tf_op jit(solution)/shard_map/dot_general | solution.py:62
  44.7 6.7 %reshape.341 = bf16[2,8,3,8,3,16,64]{6,5,4,3,2,1,0:T(8,128)(2,1)} reshape(bf16[384,3072]{1,0:T(8,128)(2,1)} %convolution_convert_fusion) | data formatting | bytes 4718592 | tf_op jit(solution)/shard_map/reshape | solution.py:67
  51.4 3.3 %copy.50 = bf16[2,8,3,8,3,16,64]{6,5,4,3,1,2,0:T(8,128)(2,1)S(1)} copy(bf16[2,8,3,8,3,16,64]{6,5,4,3,2,1,0:T(8,128)(2,1)} %reshape.341) | data formatting | bytes 4718592 | tf_op jit(solution)/shard_map/reshape | solution.py:67
  54.7 1.7 fusion
  56.4 0.4 copy-done.1
  56.8 1.4 slice.44
  58.2 3.3 %copy.68 = bf16[6,64,1,16,64]{1,4,3,0,2:T(8,128)(2,1)} copy(bf16[6,64,1,16,64]{4,3,2,1,0:T(8,128)(2,1)} %slice.44) | data formatting | bytes 1572864
  61.6 3.8 %fusion.1 = (bf16[6,64,16,64]{3,2,1,0:T(8,128)(2,1)S(1)}, bf16[6,64,16,64]{3,2,1,0:T(8,128)(2,1)S(1)}) fusion(f32[6,64,16]{2,1,0:T(8,128)S(1)} %get-tuple-element.25, bf16[6,64,3,16,64]{4,3,2,1,0:T(8,128)(2,1)} %bitcast.93, f32[6,64,16]{2,1,0:T(8,128)S(1)} %get-tuple-element.24), kind=kLoop, calls=%fused_computation.10 | loop fusion | flops 2359296 | bytes 3194880 | tf_op jit(solution)/shard_map/convert_element_type | solution.py:35
  65.4 1.2 fusion.4
  66.7 0.2 copy-done.3
  66.8 2.0 %fusion.9 = bf16[6,64,16,64]{1,3,2,0:T(8,128)(2,1)} fusion(f32[6,16,64,64]{2,3,1,0:T(8,128)S(1)} %get-tuple-element.20, f32[6,16,64]{2,1,0:T(8,128)S(1)} %compare_select_fusion, f32[6,64]{1,0:T(8,128)S(1)} %mul.168, bf16[6,64,1,16,64]{1,4,3,0,2:T(8,128)(2,1)S(1)} %copy-done.3), kind=kOutput, calls=%fused_computation.30 | convolution fusion | flops 52297728 | bytes 3171840 | tf_op jit(solution)/shard_map/whqk,wkhd->wqhd/dot_general | solution.py:44
  68.8 3.2 %copy.55 = bf16[6,64,16,64]{3,2,1,0:T(8,128)(2,1)} copy(bf16[6,64,16,64]{1,3,2,0:T(8,128)(2,1)} %fusion.9) | data formatting | bytes 1572864 | tf_op jit(solution)/shard_map/convert_element_type | solution.py:46
  72.0 2.7 %reshape.343 = bf16[2,3,8,8,1024]{4,3,2,1,0:T(8,128)(2,1)S(1)} reshape(bf16[6,64,16,64]{3,2,1,0:T(8,128)(2,1)} %copy.55) | data formatting | bytes 1572864 | tf_op jit(solution)/shard_map/reshape | solution.py:77
  74.9 0.8 copy-done.2
  75.7 0.5 multiply_reduce_fusion.1
  76.3 1.2 gather_fusion
  77.5 1.1 tile.4
  78.6 4.7 %scatter_custom_fusion = bf16[768,1024]{1,0:T(8,128)(2,1)} fusion(s32[512]{0:T(512)S(1)} %bitcast.109, bf16[512,1024]{1,0:T(8,128)(2,1)} %bitcast.99, bf16[]{:T(256)} %constant.107.clone.1), kind=kCustom, calls=%fused_computation.42 | custom fusion | bytes 1573376 | tf_op jit(solution)/shard_map/scatter | solution.py:111
  83.3 3.7 %reshape.348 = bf16[128,1,6,1024]{3,2,0,1:T(8,128)(2,1)} reshape(bf16[768,1024]{1,0:T(8,128)(2,1)} %scatter_custom_fusion) | data formatting | bytes 3145728 | tf_op jit(solution)/shard_map/reshape | solution.py:113
  87.0 36.4 %all_to_all.10 = bf16[128,1,6,1024]{3,2,1,0:T(8,128)(2,1)} all-to-all(bf16[128,1,6,1024]{3,2,1,0:T(8,128)(2,1)} %bitcast.95), channel_id=1, replica_groups=mesh['lat'=8,'lon'=16] {'lat','lon'}, dimensions={0} | all-to-all | bytes 3145728 | tf_op jit(solution)/shard_map/all_to_all | solution.py:114
  123.5 3.7 %reshape_squeeze.3 = bf16[768,1024]{1,0:T(8,128)(2,1)} reshape(bf16[128,1,6,1024]{3,2,1,0:T(8,128)(2,1)} %all_to_all.10) | data formatting | bytes 3145728 | tf_op jit(solution)/shard_map/reshape;squeeze | solution.py:115
  127.2 3.8 %fusion.30 = f32[768,512]{1,0:T(8,128)} fusion(bf16[768,1024]{1,0:T(8,128)(2,1)} %reshape_squeeze.3, bf16[1024,512]{1,0:T(8,128)(2,1)} %param.15), kind=kOutput, calls=%fused_computation.90 | convolution fusion | flops 805306368 | bytes 4194304 | tf_op jit(solution)/shard_map/dot_general | solution.py:116
  131.0 5.5 %convolution_convert_fusion.1 = bf16[768,1024]{1,0:T(8,128)(2,1)} fusion(bf16[512,1024]{1,0:T(8,128)(2,1)} %param.17, f32[768,512]{1,0:T(8,128)} %fusion.30, bf16[768,1024]{1,0:T(8,128)(2,1)} %reshape_squeeze.3, bf16[1024,512]{1,0:T(8,128)(2,1)} %param.16), kind=kOutput, calls=%fused_computation.16 | convolution fusion | flops 1613758464 | bytes 6815744 | tf_op jit(solution)/shard_map/dot_general | solution.py:119
  136.6 3.7 %stack_reshape.3 = bf16[128,1,6,1024]{3,2,0,1:T(8,128)(2,1)} reshape(bf16[768,1024]{1,0:T(8,128)(2,1)} %convolution_convert_fusion.1) | data formatting | bytes 3145728 | tf_op jit(solution)/shard_map/stack;reshape | solution.py:122
  140.3 5.9 %all-to-all-start.1 = ((bf16[128,1,6,1024]{3,2,1,0:T(8,128)(2,1)}), bf16[128,1,6,1024]{3,2,1,0:T(8,128)(2,1)}, u32[]{:S(2)}, u32[]{:S(2)}) async-start(bf16[128,1,6,1024]{3,2,1,0:T(8,128)(2,1)} %bitcast.94), calls=%async_computation.1 | async-start | bytes 4194304 | tf_op jit(solution)/shard_map/all_to_all | solution.py:121
  146.2 0.2 fusion.29
  146.6 28.8 %all-to-all-done.1 = bf16[128,1,6,1024]{3,2,1,0:T(8,128)(2,1)} async-done(((bf16[128,1,6,1024]{3,2,1,0:T(8,128)(2,1)}), bf16[128,1,6,1024]{3,2,1,0:T(8,128)(2,1)}, u32[]{:S(2)}, u32[]{:S(2)}) %all-to-all-start.1) | async-done | bytes 1572896 | tf_op jit(solution)/shard_map/all_to_all | solution.py:121
  175.5 3.7 %reshape.349 = bf16[768,1024]{1,0:T(8,128)(2,1)} reshape(bf16[128,1,6,1024]{3,2,1,0:T(8,128)(2,1)} %all-to-all-done.1) | data formatting | bytes 3145728 | tf_op jit(solution)/shard_map/reshape | solution.py:124
  179.2 3.2 %gather_fusion.2 = bf16[256,1024]{1,0:T(8,128)(2,1)S(1)} fusion(bf16[768,1024]{1,0:T(8,128)(2,1)} %reshape.349, s32[1024]{0:T(1024)S(1)} %pad_clamp_fusion), kind=kCustom, calls=%fused_computation.2 | custom fusion | bytes 1049600 | tf_op jit(solution)/shard_map/gather | solution.py:127
  182.3 4.0 %gather_fusion.1 = bf16[256,1024]{1,0:T(8,128)(2,1)} fusion(bf16[768,1024]{1,0:T(8,128)(2,1)} %reshape.349, s32[1024]{0:T(1024)S(1)} %pad_clamp_fusion.1), kind=kCustom, calls=%fused_computation.1 | custom fusion | bytes 1049600 | tf_op jit(solution)/shard_map/gather | solution.py:127
  186.3 2.2 %convert_add_fusion = f32[256,1024]{1,0:T(8,128)} fusion(bf16[256,1024]{1,0:T(8,128)(2,1)S(1)} %gather_fusion.2, bf16[256,1024]{1,0:T(8,128)(2,1)} %gather_fusion.1), kind=kLoop, calls=%fused_computation.35 | loop fusion | flops 786432 | bytes 2097152 | tf_op jit(solution)/shard_map/add | solution.py:127
  188.5 2.9 %add.278 = f32[128,2,1024]{2,1,0:T(2,128)} reshape(f32[256,1024]{1,0:T(8,128)} %convert_add_fusion) | data formatting | bytes 2097152 | tf_op jit(solution)/shard_map/add | solution.py:127
  191.4 2.6 %multiply_reduce_fusion = f32[128,1024]{1,0:T(8,128)S(1)} fusion(f32[128,2,1024]{2,1,0:T(2,128)} %add.278, f32[128,2]{1,0:T(8,128)S(1)} %copy.57), kind=kLoop, calls=%fused_computation.34 | loop fusion | flops 393216 | bytes 1573888 | tf_op jit(solution)/shard_map/reduce_sum | solution.py:129
  194.0 0.8 add_convert_fusion
  (48 shorter events, 2.1 us)
Async XLA Ops:
  0.0 74.9 %copy-start = (bf16[1024,1024]{1,0:T(8,128)(2,1)S(1)}, bf16[1024,1024]{1,0:T(8,128)(2,1)}, u32[]{:S(2)}) copy-start(bf16[1024,1024]{1,0:T(8,128)(2,1)} %param.12) | copy-start | bytes 6291460
  2.3 13.5 %collective-permute-start.1 = (bf16[8,16,1024]{2,1,0:T(8,128)(2,1)S(1)}, bf16[8,16,1024]{2,1,0:T(8,128)(2,1)S(1)}, u32[]{:S(2)}, u32[]{:S(2)}) collective-permute-start(bf16[8,16,1024]{2,1,0:T(8,128)(2,1)S(1)} %multiply_convert_fusion.2), channel_id=1, source_target_pairs={{16,0},{32,16},{48,32},{64,48},{80,64},{96,80},{112,96},{0,112},{1... | collective-permute-start | bytes 786440 | tf_op jit(solution)/shard_map/ppermute | solution.py:21
  3.7 12.0 %collective-permute-start = (bf16[8,16,1024]{2,1,0:T(8,128)(2,1)S(1)}, bf16[8,16,1024]{2,1,0:T(8,128)(2,1)S(1)}, u32[]{:S(2)}, u32[]{:S(2)}) collective-permute-start(bf16[8,16,1024]{2,1,0:T(8,128)(2,1)S(1)} %multiply_convert_fusion.2), channel_id=1, source_target_pairs={{0,16},{16,32},{32,48},{48,64},{64,80},{80,96},{96,112},{112,0},{1... | collective-permute-start | bytes 786440 | tf_op jit(solution)/shard_map/ppermute | solution.py:20
  16.7 13.4 %collective-permute-start.3 = (bf16[24,8,1024]{2,1,0:T(8,128)(2,1)}, bf16[24,8,1024]{2,1,0:T(8,128)(2,1)}, u32[]{:S(2)}, u32[]{:S(2)}) collective-permute-start(bf16[24,8,1024]{2,1,0:T(8,128)(2,1)} %get-tuple-element.9), channel_id=1, source_target_pairs={{1,0},{2,1},{3,2},{4,3},{5,4},{6,5},{7,6},{8,7},{9,8},{10,9},{11,1... | collective-permute-start | bytes 1179656 | tf_op jit(solution)/shard_map/ppermute | solution.py:21
  22.6 12.5 %collective-permute-start.2 = (bf16[24,8,1024]{2,1,0:T(8,128)(2,1)S(1)}, bf16[24,8,1024]{2,1,0:T(8,128)(2,1)}, u32[]{:S(2)}, u32[]{:S(2)}) collective-permute-start(bf16[24,8,1024]{2,1,0:T(8,128)(2,1)S(1)} %get-tuple-element.10), channel_id=1, source_target_pairs={{0,1},{1,2},{2,3},{3,4},{4,5},{5,6},{6,7},{7,8},{8,9},{9,10},{10,1... | collective-permute-start | bytes 1179656 | tf_op jit(solution)/shard_map/ppermute | solution.py:20
  54.7 2.1 %copy-start.1 = (bf16[2,8,3,8,3,16,64]{6,5,4,3,1,2,0:T(8,128)(2,1)}, bf16[2,8,3,8,3,16,64]{6,5,4,3,1,2,0:T(8,128)(2,1)S(1)}, u32[]{:S(2)}) copy-start(bf16[2,8,3,8,3,16,64]{6,5,4,3,1,2,0:T(8,128)(2,1)S(1)} %copy.50) | copy-start | bytes 7077892
  65.4 1.4 copy-start.3
  74.7 1.0 copy-start.2
  140.3 5.9 %copy-start.4 = (bf16[1024,64]{0,1:T(8,128)(2,1)S(1)}, bf16[1024,64]{0,1:T(8,128)(2,1)}, u32[]{:S(2)}) copy-start(bf16[1024,64]{0,1:T(8,128)(2,1)} %param.13) | copy-start | bytes 393220
  140.3 6.2 %copy-start.5 = (s32[1,1,128,2]{2,3,1,0:T(2,128)S(1)}, s32[1,1,128,2]{2,3,1,0:T(2,128)}, u32[]{:S(2)}) copy-start(s32[1,1,128,2]{2,3,1,0:T(2,128)} %param.14) | copy-start | bytes 3076
  140.3 35.2 %all-to-all-start.1 = ((bf16[128,1,6,1024]{3,2,1,0:T(8,128)(2,1)}), bf16[128,1,6,1024]{3,2,1,0:T(8,128)(2,1)}, u32[]{:S(2)}, u32[]{:S(2)}) async-start(bf16[128,1,6,1024]{3,2,1,0:T(8,128)(2,1)} %bitcast.94), calls=%async_computation.1 | async-start | bytes 4194304 | tf_op jit(solution)/shard_map/all_to_all | solution.py:121
where the time goes:
time: 196 us; the launch traced here: 195 us
  local copies, waits for them, and re-layouts  58.3 us (30%)
  waiting for transfers between devices  40 us (20%)
  blocking collectives  36.4 us (19%)
  matrix products  20.1 us (10%)
  other arithmetic  18 us (9%)
  starting transfers between devices  14.6 us (7%)
  between operations  7.32 us (4%)
    all_to_all x1, blocking collectives, body(): lax.all_to_all(send, ('lat', 'lon'), split_axis=0, concat_axis=0, tiled=T...  36.4 us
    all_to_all x1, waiting for transfers between devices, body(): lax.all_to_all(jnp.stack(results, axis=1), ('lat', 'lon'), split_axis=0,...  28.8 us
    reshape x2, local copies, waits for them, and re-layouts, body(): qkv.reshape(win_lat, WIN, win_lon, WIN, 3, heads, HEAD)  10 us
    ppermute x2, starting transfers between devices, padded(): after = lax.ppermute(leading, axis, down)  7.39 us
    gather x2, local copies, waits for them, and re-layouts, body(): combined = combined + back_flat[slot_index[copy]].astype(jnp.float32)  7.15 us
    dot_general x1, matrix products, body(): jnp.dot(window_cells.reshape(-1, width), w_qkv, preferred_element_type=jn...  6.82 us
    ppermute x2, waiting for transfers between devices, padded(): after = lax.ppermute(leading, axis, down)  6.14 us
    all_to_all x1, starting transfers between devices, body(): lax.all_to_all(jnp.stack(results, axis=1), ('lat', 'lon'), split_axis=0,...  5.91 us
  transfers between devices with their start and end apart: 5, of which 3 were waited for; matrix products, arithmetic and copies ran while one was open for 3% of the time, Pallas kernels for 0%

commit v1 on v0

v1 whole, which is shorter than its diff:
```python
import functools

import jax
import jax.numpy as jnp
from jax import lax
from jax.experimental import pallas as pl
from jax.experimental.pallas import tpu as pltpu
from jax.sharding import PartitionSpec as P

HEAD = 64
WIN = 8
MOST = 6
D = 1024
MAIN = 768
TAIL = 256
BLK = 256
BF16 = jnp.bfloat16
F32 = jnp.float32
AXES = ("lat", "lon")


def iota(shape, dim):
    return lax.broadcasted_iota(jnp.int32, shape, dim)


def dot(a, b):
    return jnp.dot(a, b, preferred_element_type=F32)


def rms(x):
    return x * lax.rsqrt(jnp.mean(x * x, axis=-1, keepdims=True) + 1e-05)


def head_norm(y):
    n = y.shape[1]
    square = y * y
    high = square.astype(BF16)
    low = (square - high.astype(F32)).astype(BF16)
    same = jnp.where(iota((n, n), 0) // HEAD == iota((n, n), 1) // HEAD, 1.0, 0.0).astype(BF16)
    total = dot(high, same) + dot(low, same)
    return (y * lax.rsqrt(total * (1.0 / HEAD) + 1e-05)).astype(BF16)


def own_kernel(x_ref, wq_ref, wk_ref, wv_ref, q_ref, k_ref, v_ref, xn):
    @pl.when(pl.program_id(0) == 0)
    def _():
        xn[...] = rms(x_ref[...].astype(F32)).astype(BF16)

    x = xn[...]
    q_ref[...] = head_norm(dot(x, wq_ref[...]).astype(BF16).astype(F32))
    k_ref[...] = head_norm(dot(x, wk_ref[...]).astype(BF16).astype(F32))
    v_ref[...] = dot(x, wv_ref[...]).astype(BF16)


def own_qkv(x, w_qkv):
    n = x.shape[0]
    steps = D // BLK
    col = lambda part: pl.BlockSpec((D, BLK), lambda i: (0, part * steps + i))
    out = pl.BlockSpec((n, BLK), lambda i: (0, i))
    return pl.pallas_call(
        own_kernel,
        grid=(steps,),
        in_specs=[pl.BlockSpec((n, D), lambda i: (0, 0)), col(0), col(1), col(2)],
        out_specs=[out, out, out],
        out_shape=[jax.ShapeDtypeStruct((n, D), BF16)] * 3,
        scratch_shapes=[pltpu.VMEM((n, D), BF16)],
        compiler_params=pltpu.CompilerParams(vmem_limit_bytes=32 << 20),
        cost_estimate=pl.CostEstimate(
            flops=2 * n * D * 3 * D, bytes_accessed=7 << 20, transcendentals=0
        ),
        name="own_qkv",
    )(x, w_qkv, w_qkv, w_qkv)


def route_kernel(experts, ids_ref, idt_ref, pack_ref, pick_ref, spread_ref, gather_ref):
    n = ids_ref.shape[0]
    expert = iota((experts, n), 0)
    first = idt_ref[0:1, :] == expert
    second = idt_ref[1:2, :] == expert
    both = jnp.where(first | second, 1.0, 0.0)
    before = jnp.where(iota((n, n), 0) < iota((n, n), 1), 1.0, 0.0).astype(BF16)
    count = dot(both.astype(BF16), before)
    codes = [
        jnp.sum(jnp.where(hit, count + 8.0 * expert.astype(F32), 0.0), axis=0, keepdims=True)
        for hit in (first, second)
    ]
    rows = 8 * experts
    slot = iota((rows, n), 0)
    base = slot // 8 * 8
    rank = slot % 8
    slot_f = slot.astype(F32)
    main = jnp.where((slot_f == codes[0]) | (slot_f == codes[1]), 1.0, 0.0).astype(BF16)
    for j in range(3):
        want = jnp.where(rank == 6, base + j, jnp.where(rank == 7, base + 3 + j, -1)).astype(F32)
        pack_ref[j, :, 0:n] = main
        pack_ref[j, :, n : 2 * n] = jnp.where(
            (want == codes[0]) | (want == codes[1]), 1.0, 0.0
        ).astype(BF16)
    expert = iota((n, experts), 1)
    first = ids_ref[:, 0:1] == expert
    second = ids_ref[:, 1:2] == expert
    both = jnp.where(first | second, 1.0, 0.0)
    before = jnp.where(iota((n, n), 1) < iota((n, n), 0), 1.0, 0.0).astype(BF16)
    count = dot(before, both.astype(BF16))
    lanes = 16 * experts
    slot = iota((1, lanes), 1)
    base = slot // 16 * 8
    rank = slot % 8
    for k, hit in enumerate((first, second)):
        code = jnp.sum(jnp.where(hit, count + 8.0 * expert.astype(F32), 0.0), axis=1, keepdims=True)
        wants = [jnp.where(rank < MOST, base + rank, -1)]
        for j in range(3):
            wants.append(jnp.where(rank == 6, base + j, jnp.where(rank == 7, base + 3 + j, -1)))
        for j, want in enumerate(wants):
            pick_ref[j, k * n : (k + 1) * n, :] = jnp.where(
                want.astype(F32) == code, 1.0, 0.0
            ).astype(BF16)
    row = iota((BLK, BLK), 0)
    column = iota((BLK, BLK), 1)
    rank = row % 8
    base = row - rank
    for j in range(3):
        source = jnp.where(
            rank == j, base + 6, jnp.where(rank == 3 + j, base + 7, -1)
        )
        spread_ref[:, j * BLK : (j + 1) * BLK] = jnp.where(source == column, 1.0, 0.0).astype(BF16)
        source = jnp.where(rank == 6, base + j, jnp.where(rank == 7, base + 3 + j, -1))
        gather_ref[j * BLK : (j + 1) * BLK, :] = jnp.where(source == column, 1.0, 0.0).astype(BF16)


def route(ids, experts):
    n = ids.shape[0]
    return pl.pallas_call(
        functools.partial(route_kernel, experts),
        out_shape=[
            jax.ShapeDtypeStruct((3, 8 * experts, 2 * n), BF16),
            jax.ShapeDtypeStruct((4, 2 * n, 16 * experts), BF16),
            jax.ShapeDtypeStruct((BLK, 3 * BLK), BF16),
            jax.ShapeDtypeStruct((3 * BLK, BLK), BF16),
        ],
        compiler_params=pltpu.CompilerParams(vmem_limit_bytes=32 << 20),
        cost_estimate=pl.CostEstimate(flops=1 << 28, bytes_accessed=4 << 20, transcendentals=0),
        name="route",
    )(ids, ids.T)


def attend_kernel(
    meta_ref, x_ref, up_ref, down_ref, left_ref, right_ref, ul_ref, ur_ref, dl_ref, dr_ref,
    q_ref, k_ref, v_ref, wk_ref, wv_ref, wo_ref, router_ref, ids_ref, pack_ref,
    mixed_ref, gates_ref, send_ref, xh, acc, mask,
):
    step = pl.program_id(0)
    cut_lat = WIN - meta_ref[0]
    cut_lon = WIN - meta_ref[1]
    n = x_ref.shape[0]
    cols = 16

    @pl.when(step == 0)
    def _():
        def normed(a):
            return rms(a).astype(BF16)

        band = iota((n, 1), 0) // cols >= cut_lat
        xh[0:n, :] = normed(
            jnp.where(band, up_ref[...].astype(F32), down_ref[...].astype(F32))
        )
        cell = iota((64, 1), 0)
        from_left = cell % WIN >= cut_lon
        xh[n : n + 64, :] = normed(
            jnp.where(from_left, left_ref[...].astype(F32), right_ref[...].astype(F32))
        )
        upper = jnp.where(from_left, ul_ref[...].astype(F32), ur_ref[...].astype(F32))
        lower = jnp.where(from_left, dl_ref[...].astype(F32), dr_ref[...].astype(F32))
        xh[n + 64 :, :] = normed(jnp.where(cell // WIN >= cut_lat, upper, lower))
        cell = iota((n, 3 * n), 0)
        row_of = (cell // cols >= cut_lat).astype(jnp.int32)
        col_of = (cell % cols + (WIN - cut_lon)) // WIN
        query = row_of * 3 + col_of
        key = iota((n, 3 * n), 1)
        in_band = (key >= n) & (key < 2 * n)
        in_side = (key >= 2 * n) & (key < 2 * n + 64)
        in_corner = key >= 2 * n + 64
        local = key % n
        small = key % 64
        row = jnp.where(in_side | in_corner, small // WIN, local // cols)
        past = row >= cut_lat
        halo_row = in_band | in_corner
        key_row = jnp.where(past != halo_row, 1, 0)
        edge_low = meta_ref[2] == 0
        edge_high = meta_ref[2] == meta_ref[3] - 1
        outside = halo_row & ((past & edge_low) | (~past & edge_high))
        key_col = jnp.where(
            in_side | in_corner,
            jnp.where(small % WIN >= cut_lon, 0, 2),
            (local % cols + (WIN - cut_lon)) // WIN,
        )
        same = (key_row * 3 + key_col == query) & ~outside
        valid = jnp.where(same, 1.0, 0.0)
        mask[0:n, :] = valid
        mask[n : 2 * n, :] = valid
        acc[...] = jnp.zeros_like(acc)

    x = xh[...]
    keys = jnp.concatenate(
        [k_ref[...], head_norm(dot(x, wk_ref[...]).astype(BF16).astype(F32))], axis=0
    )
    values = jnp.concatenate([v_ref[...], dot(x, wv_ref[...]).astype(BF16)], axis=0)
    low_half = iota((1, 128), 1) < HEAD
    first = jnp.where(low_half, 1.0, 0.0).astype(BF16)
    second = jnp.where(low_half, 0.0, 1.0).astype(BF16)
    outs = []
    for pair in range(BLK // 128):
        lanes = slice(pair * 128, (pair + 1) * 128)
        q = q_ref[:, lanes]
        qq = jnp.concatenate([q * first, q * second], axis=0)
        scores = lax.dot_general(
            qq, keys[:, lanes], (((1,), (1,)), ((), ())), preferred_element_type=F32
        )
        weight = jnp.exp(scores * 0.125) * mask[...]
        weight = weight * (1.0 / jnp.sum(weight, axis=1, keepdims=True))
        out = dot(weight.astype(BF16), values[:, lanes])
        outs.append(jnp.where(low_half, out[0:n], out[n:]).astype(BF16))
    acc[...] += dot(jnp.concatenate(outs, axis=1), wo_ref[...])

    @pl.when(step == pl.num_programs(0) - 1)
    def _():
        mixed = (x_ref[...].astype(F32) + acc[...]).astype(BF16)
        mixed_ref[...] = mixed
        normed = rms(mixed.astype(F32)).astype(BF16)
        logits = dot(normed, router_ref[...])
        expert = iota(logits.shape, 1)
        sig = [
            jax.nn.sigmoid(
                jnp.sum(
                    jnp.where(ids_ref[:, k : k + 1] == expert, logits, 0.0), axis=1, keepdims=True
                )
            )
            for k in range(2)
        ]
        total = sig[0] + sig[1]
        gates_ref[...] = jnp.where(iota((n, 128), 1) == 0, sig[0] / total, sig[1] / total)
        tail = normed[:, MAIN:]
        experts = logits.shape[1]
        for j in range(3):
            lanes = slice(j * BLK, (j + 1) * BLK)
            rows = dot(pack_ref[j], jnp.concatenate([normed[:, lanes], tail], axis=0))
            rows = jnp.broadcast_to(rows.reshape(experts, 1, 8, BLK), (experts, 2, 8, BLK))
            send_ref[:, lanes] = rows.reshape(experts * 16, BLK).astype(BF16)


def attend(meta, x, halo, qkv, w_qkv, w_out, router, ids, pack):
    n = x.shape[0]
    steps = D // BLK
    experts = router.shape[1]
    whole = lambda a: pl.BlockSpec(a.shape, lambda i: (0,) * a.ndim)
    block = pl.BlockSpec((n, BLK), lambda i: (0, i))
    col = lambda part: pl.BlockSpec((D, BLK), lambda i: (0, part * steps + i))
    return pl.pallas_call(
        attend_kernel,
        grid=(steps,),
        in_specs=[
            pl.BlockSpec(memory_space=pltpu.SMEM),
            whole(x),
            *[whole(h) for h in halo],
            block, block, block,
            col(1), col(2),
            pl.BlockSpec((BLK, D), lambda i: (i, 0)),
            whole(router), whole(ids), whole(pack),
        ],
        out_specs=[
            pl.BlockSpec((n, D), lambda i: (0, 0)),
            pl.BlockSpec((n, 128), lambda i: (0, 0)),
            pl.BlockSpec((16 * experts, MAIN), lambda i: (0, 0)),
        ],
        out_shape=[
            jax.ShapeDtypeStruct((n, D), BF16),
            jax.ShapeDtypeStruct((n, 128), F32),
            jax.ShapeDtypeStruct((16 * experts, MAIN), BF16),
        ],
        scratch_shapes=[
            pltpu.VMEM((2 * n, D), BF16),
            pltpu.VMEM((n, D), F32),
            pltpu.VMEM((2 * n, 3 * n), F32),
        ],
        compiler_params=pltpu.CompilerParams(vmem_limit_bytes=40 << 20),
        cost_estimate=pl.CostEstimate(flops=3 << 30, bytes_accessed=10 << 20, transcendentals=1 << 20),
        name="attend",
    )(meta, x, *halo, *qkv, w_qkv, w_qkv, w_out, router, ids, pack)


def expert_kernel(r_ref, wg_ref, wu_ref, wd_ref, spread_ref, gather_ref, out_ref):
    tail = dot(spread_ref[:, 0:BLK], r_ref[:, 0:BLK])
    for j in range(1, 3):
        lanes = slice(j * BLK, (j + 1) * BLK)
        tail = tail + dot(spread_ref[:, lanes], r_ref[:, lanes])
    x = jnp.concatenate([r_ref[...], tail.astype(BF16)], axis=1)
    gate = dot(x, wg_ref[...])
    upper = dot(x, wu_ref[...])
    hidden = (jax.nn.silu(gate) * upper).astype(BF16)
    part = dot(hidden, wd_ref[...]).astype(BF16)
    packed = dot(gather_ref[...], part[:, MAIN:])
    kept = iota((BLK, 1), 0) % 8 < MOST
    for j in range(3):
        lanes = slice(j * BLK, (j + 1) * BLK)
        out_ref[:, lanes] = jnp.where(
            kept, part[:, lanes].astype(F32), packed[lanes, :]
        ).astype(BF16)


def run_experts(received, w_gate, w_up, w_down, spread, gather):
    rows = received.shape[0]
    whole = lambda a: pl.BlockSpec(a.shape, lambda i: (0, 0))
    block = pl.BlockSpec((BLK, MAIN), lambda i: (i, 0))
    return pl.pallas_call(
        expert_kernel,
        grid=(rows // BLK,),
        in_specs=[block, *[whole(a) for a in (w_gate, w_up, w_down, spread, gather)]],
        out_specs=block,
        out_shape=jax.ShapeDtypeStruct(received.shape, BF16),
        compiler_params=pltpu.CompilerParams(vmem_limit_bytes=40 << 20),
        cost_estimate=pl.CostEstimate(flops=4 << 30, bytes_accessed=7 << 20, transcendentals=1 << 19),
        name="experts",
    )(received, w_gate, w_up, w_down, spread, gather)


def combine_kernel(back_ref, pick_ref, gates_ref, mixed_ref, out_ref):
    n = mixed_ref.shape[0]
    gates = [gates_ref[:, 0:1], gates_ref[:, 1:2]]

    def finish(lanes, both):
        moe = gates[0] * both[0:n] + gates[1] * both[n:]
        out_ref[:, lanes] = (mixed_ref[:, lanes].astype(F32) + moe).astype(BF16)

    tail = None
    for j in range(3):
        lanes = slice(j * BLK, (j + 1) * BLK)
        back = back_ref[:, lanes]
        finish(lanes, dot(pick_ref[0], back))
        more = dot(pick_ref[1 + j], back)
        tail = more if tail is None else tail + more
    finish(slice(MAIN, D), tail)


def combine(back, pick, gates, mixed):
    return pl.pallas_call(
        combine_kernel,
        out_shape=jax.ShapeDtypeStruct(mixed.shape, BF16),
        compiler_params=pltpu.CompilerParams(vmem_limit_bytes=40 << 20),
        cost_estimate=pl.CostEstimate(flops=1 << 30, bytes_accessed=5 << 20, transcendentals=0),
        name="combine",
    )(back, pick, gates, mixed)


def halo_of(tokens):
    n_lat, n_lon = lax.axis_size("lat"), lax.axis_size("lon")
    low, high = tokens[:, :WIN], tokens[:, WIN:]

    def moved(x, down, right):
        pairs = [
            (i * n_lon + j, (i + down) % n_lat * n_lon + (j + right) % n_lon)
            for i in range(n_lat)
            for j in range(n_lon)
        ]
        return lax.ppermute(x, AXES, pairs).reshape(-1, x.shape[-1])

    return [
        moved(tokens, 1, 0),
        moved(tokens, -1, 0),
        moved(high, 0, 1),
        moved(low, 0, -1),
        moved(high, 1, 1),
        moved(low, 1, -1),
        moved(high, -1, 1),
        moved(low, -1, -1),
    ]


def body(tokens, shifts, w_qkv, w_out, router, expert_ids, w_gate, w_up, w_down):
    rows, cols, width = tokens.shape
    x = tokens.reshape(-1, width)
    ids = expert_ids.reshape(-1, 2)
    halo = halo_of(tokens)
    meta = jnp.concatenate(
        [shifts, jnp.stack([lax.axis_index("lat"), jnp.int32(lax.axis_size("lat"))])]
    ).astype(jnp.int32)
    pack, pick, spread, gather = route(ids, router.shape[1])
    qkv = own_qkv(x, w_qkv)
    mixed, gates, send = attend(meta, x, halo, qkv, w_qkv, w_out, router, ids, pack)
    received = lax.all_to_all(send, AXES, split_axis=0, concat_axis=0, tiled=True)
    part = run_experts(received, w_gate, w_up, w_down, spread, gather)
    back = lax.all_to_all(part, AXES, split_axis=0, concat_axis=0, tiled=True)
    return combine(back, pick, gates, mixed).reshape(rows, cols, width)


def solution(mesh):
    placed = (
        P("lat", "lon", None),
        P(),
        P(),
        P(),
        P(),
        P("lat", "lon", None, None),
        P(None, ("lat", "lon")),
        P(None, ("lat", "lon")),
        P(("lat", "lon"), None),
    )
    return jax.shard_map(
        body, mesh=mesh, in_specs=placed, out_specs=P("lat", "lon", None), check_vma=False
    )
```

time: 196 us -> 112 us (0.57)
  local copies, waits for them, and re-layouts: 58.3 us -> 6.69 us
  waiting for transfers between devices: 40 us -> 11.1 us
  Pallas kernels: 0 us -> 22.3 us
  matrix products: 20.1 us -> 0 us
  blocking collectives: 36.4 us -> 56.5 us
  other arithmetic: 18 us -> 0.08 us
  between operations: 7.32 us -> 0.13 us
    all_to_all x1 -> x0, waiting for transfers between devices: 28.8 us -> none  [body(): lax.all_to_all(jnp.stack(results, axis=1), ('lat', 'lon'), split_axis=0,...]
    pallas_call x0 -> x5, Pallas kernels: none -> 22.3 us  [the longest x1 8.4 us: attend(): pl.pallas_call(attend_kernel, grid=(steps,), in_specs=[pl.BlockSpec(memor...]
    dot_general x7 -> x0, matrix products: 20.1 us -> none  [the longest x1 6.82 us: body(): jnp.dot(window_cells.reshape(-1, width), w_qkv, preferred_element_type=jn...]
    reshape x5 -> x0, local copies, waits for them, and re-layouts: 20.1 us -> none  [the longest x2 10 us: body(): qkv.reshape(win_lat, WIN, win_lon, WIN, 3, heads, HEAD)]
    all_to_all x1 -> x2, blocking collectives: 36.4 us -> 56.5 us  [the longest x1 28.4 us: body(): back = lax.all_to_all(part, AXES, split_axis=0, concat_axis=0, tiled=True)]
    another operation x4 -> x0, local copies, waits for them, and re-layouts: 8.53 us -> none  [the longest x1 3.73 us: body(): block = received[:, 0].reshape(-1, width)]
    gather x3 -> x0, local copies, waits for them, and re-layouts: 8.32 us -> none  [the longest x2 7.15 us: body(): combined = combined + back_flat[slot_index[copy]].astype(jnp.float32)]
    ppermute x4 -> x8, starting transfers between devices: 8.68 us -> 15.3 us  [moved(): return lax.ppermute(x, AXES, pairs).reshape(-1, x.shape[-1])]
  transfers between devices with their start and end apart: 5 -> 8, of which waited for: 3 -> 3; matrix products, arithmetic and copies ran while one was open for 3% -> 2% of each run, Pallas kernels for 0% -> 5%
where the time goes in v1:
time: 112 us
  blocking collectives  56.5 us (50%)
  Pallas kernels  22.3 us (20%)
  starting transfers between devices  15.3 us (14%)
  waiting for transfers between devices  11.1 us (10%)
  local copies, waits for them, and re-layouts  6.69 us (6%)
    all_to_all x1, blocking collectives, body(): back = lax.all_to_all(part, AXES, split_axis=0, concat_axis=0, tiled=True)  28.4 us
    all_to_all x1, blocking collectives, body(): lax.all_to_all(send, AXES, split_axis=0, concat_axis=0, tiled=True)  28.1 us
    ppermute x8, starting transfers between devices, moved(): return lax.ppermute(x, AXES, pairs).reshape(-1, x.shape[-1])  15.3 us
    ppermute x8, waiting for transfers between devices, moved(): return lax.ppermute(x, AXES, pairs).reshape(-1, x.shape[-1])  11.1 us
    pallas_call x1, Pallas kernels, attend(): pl.pallas_call(attend_kernel, grid=(steps,), in_specs=[pl.BlockSpec(memor...  8.4 us
    pallas_call x1, Pallas kernels, run_experts(): pl.pallas_call(expert_kernel, grid=(rows // BLK,), in_specs=[block, *[who...  6.31 us
    unnamed x20, local copies, waits for them, and re-layouts  5.64 us
    pallas_call x1, Pallas kernels, own_qkv(): pl.pallas_call(own_kernel, grid=(steps,), in_specs=[pl.BlockSpec((n, D),...  4.51 us
  transfers between devices with their start and end apart: 8, of which 3 were waited for; matrix products, arithmetic and copies ran while one was open for 2% of the time, Pallas kernels for 5%

profile of v1, /device:TPU:1, one launch (start us, length us, event | category | flops | bytes accessed | tf_op | source)
XLA Modules:
  0.0 112.2 jit_solution(13658289543284226213)
XLA Ops:
  0.0 1.0 fusion
  1.0 7.4 %collective-permute-start.7 = (bf16[8,8,1024]{2,1,0:T(8,128)(2,1)S(1)}, bf16[8,8,1024]{2,1,0:T(8,128)(2,1)S(1)}, u32[]{:S(2)}, u32[]{:S(2)}) collective-permute-start(bf16[8,8,1024]{2,1,0:T(8,128)(2,1)S(1)} %get-tuple-element.25), channel_id=1, source_target_pairs={{0,127},{1,112},{2,113},{3,114},{4,115},{5,116},{6,117},{7,118},{8... | collective-permute-start | bytes 393224 | tf_op jit(solution)/shard_map/ppermute | solution.py:364
  8.4 1.2 %collective-permute-start.5 = (bf16[8,8,1024]{2,1,0:T(8,128)(2,1)S(1)}, bf16[8,8,1024]{2,1,0:T(8,128)(2,1)S(1)}, u32[]{:S(2)}, u32[]{:S(2)}) collective-permute-start(bf16[8,8,1024]{2,1,0:T(8,128)(2,1)S(1)} %get-tuple-element.25), channel_id=1, source_target_pairs={{0,31},{1,16},{2,17},{3,18},{4,19},{5,20},{6,21},{7,22},{8,23},{9,... | collective-permute-start | bytes 393224 | tf_op jit(solution)/shard_map/ppermute | solution.py:364
  9.6 0.5 collective-permute-start.3
  10.0 1.0 collective-permute-start
  11.1 0.5 collective-permute-start.1
  11.5 0.8 copy.10
  12.3 0.1 copy.11.idt_ref
  12.4 1.1 copy.12.router_ref
  13.5 0.0 copy-start
  13.5 2.8 %copy-done = bf16[1024,3072]{1,0:T(8,128)(2,1)S(1)} copy-done((bf16[1024,3072]{1,0:T(8,128)(2,1)S(1)}, bf16[1024,3072]{1,0:T(8,128)(2,1)}, u32[]{:S(2)}) %copy-start) | copy-done | bytes 6291480
  16.3 0.0 copy-start.2
  16.3 0.9 copy-done.2
  17.2 0.0 copy-start.8
  17.2 0.0 copy-start.1
  17.2 0.0 copy-start.3
  17.2 0.0 copy-start.4
  17.2 4.5 %own_qkv.1 = (bf16[128,1024]{1,0:T(8,128)(2,1)S(1)}, bf16[128,1024]{1,0:T(8,128)(2,1)S(1)}, bf16[128,1024]{1,0:T(8,128)(2,1)S(1)}) custom-call(bf16[128,1024]{1,0:T(8,128)(2,1)S(1)} %bitcast.19, bf16[1024,3072]{1,0:T(8,128)(2,1)S(1)} %copy-done, bf16[1024,3072]{1,0:T(8,128)(2,1)S(1)} %copy-done, bf16[1024,3072]{1,0:T(8,128)(2,1)S(1)} %copy-done), custom_call_target="tpu_custom_call" | custom-call | flops 805306368 | bytes 7340032 | tf_op jit(solution)/shard_map/own_qkv/pallas_call | solution.py:60
  21.7 0.0 collective-permute-done.7
  21.7 3.8 %collective-permute-start.6 = (bf16[8,8,1024]{2,1,0:T(8,128)(2,1)S(1)}, bf16[8,8,1024]{2,1,0:T(8,128)(2,1)S(1)}, u32[]{:S(2)}, u32[]{:S(2)}) collective-permute-start(bf16[8,8,1024]{2,1,0:T(8,128)(2,1)S(1)} %get-tuple-element.26), channel_id=1, source_target_pairs={{0,113},{1,114},{2,115},{3,116},{4,117},{5,118},{6,119},{7,120},{8... | collective-permute-start | bytes 393224 | tf_op jit(solution)/shard_map/ppermute | solution.py:364
  25.6 0.0 collective-permute-done.5
  25.6 0.0 collective-permute-start.4
  25.6 0.0 collective-permute-done.3
  25.6 1.0 collective-permute-start.2
  26.6 1.4 %route.1 = (bf16[3,512,256]{2,1,0:T(8,128)(2,1)S(1)}, bf16[4,256,1024]{2,1,0:T(8,128)(2,1)S(1)}, bf16[256,768]{1,0:T(8,128)(2,1)S(1)}, bf16[768,256]{1,0:T(8,128)(2,1)S(1)}) custom-call(s32[128,2]{1,0:T(8,128)S(1)} %bitcast.25, s32[2,128]{1,0:T(2,128)S(1)} %copy.11.idt_ref), custom_call_target="tpu_custom_call" | custom-call | flops 268435456 | bytes 4194304 | tf_op jit(solution)/shard_map/route/pallas_call | solution.py:133
  27.9 0.0 copy-done.8
  27.9 0.1 pad_add_fusion.meta_ref
  28.0 3.8 %collective-permute-done.6 = bf16[8,8,1024]{2,1,0:T(8,128)(2,1)S(1)} collective-permute-done((bf16[8,8,1024]{2,1,0:T(8,128)(2,1)S(1)}, bf16[8,8,1024]{2,1,0:T(8,128)(2,1)S(1)}, u32[]{:S(2)}, u32[]{:S(2)}) %collective-permute-start.6) | collective-permute-done | bytes 131104 | tf_op jit(solution)/shard_map/ppermute | solution.py:364
  31.9 4.7 %collective-permute-done.4 = bf16[8,8,1024]{2,1,0:T(8,128)(2,1)S(1)} collective-permute-done((bf16[8,8,1024]{2,1,0:T(8,128)(2,1)S(1)}, bf16[8,8,1024]{2,1,0:T(8,128)(2,1)S(1)}, u32[]{:S(2)}, u32[]{:S(2)}) %collective-permute-start.4) | collective-permute-done | bytes 131104 | tf_op jit(solution)/shard_map/ppermute | solution.py:364
  36.5 2.6 %collective-permute-done.2 = bf16[8,8,1024]{2,1,0:T(8,128)(2,1)S(1)} collective-permute-done((bf16[8,8,1024]{2,1,0:T(8,128)(2,1)S(1)}, bf16[8,8,1024]{2,1,0:T(8,128)(2,1)S(1)}, u32[]{:S(2)}, u32[]{:S(2)}) %collective-permute-start.2) | collective-permute-done | bytes 131104 | tf_op jit(solution)/shard_map/ppermute | solution.py:364
  39.2 0.0 collective-permute-done
  39.2 0.0 collective-permute-done.1
  39.2 0.0 copy-done.1
  39.2 0.0 copy-done.3
  39.2 0.0 copy-done.4
  39.2 8.4 %attend.1 = (bf16[128,1024]{1,0:T(8,128)(2,1)S(1)}, f32[128,128]{1,0:T(8,128)S(1)}, bf16[1024,768]{1,0:T(8,128)(2,1)S(1)}) custom-call(s32[4]{0:T(128)S(1)} %pad_add_fusion.meta_ref, bf16[128,1024]{1,0:T(8,128)(2,1)S(1)} %bitcast.20, bf16[128,1024]{1,0:T(8,128)(2,1)S(1)} %bitcast.27, bf16[128,1024]{1,0:T(8,128)(2,1)S(1)} %bitcast.28, ...), custom_call_target="tpu_custom_call" | custom-call | flops 3221225472 | bytes 10485760 | tf_op jit(solution)/shard_map/attend/pallas_call | solution.py:258
  47.6 0.0 copy-start.5
  47.6 0.0 copy-start.6
  47.6 0.0 copy-start.7
  47.6 28.1 %all_to_all.22 = bf16[128,8,768]{2,1,0:T(8,128)(2,1)S(1)} all-to-all(bf16[128,8,768]{2,1,0:T(8,128)(2,1)S(1)} %bitcast.21), channel_id=1, replica_groups=mesh['lat'=8,'lon'=16] {'lat','lon'}, dimensions={0} | all-to-all | bytes 3145728 | tf_op jit(solution)/shard_map/all_to_all | solution.py:389
  75.7 0.0 copy-done.5
  75.7 0.0 copy-done.6
  75.7 0.0 copy-done.7
  75.7 6.3 %experts.1 = bf16[1024,768]{1,0:T(8,128)(2,1)S(1)} custom-call(bf16[1024,768]{1,0:T(8,128)(2,1)S(1)} %bitcast.22, bf16[1024,512]{1,0:T(8,128)(2,1)S(1)} %copy-done.5, bf16[1024,512]{1,0:T(8,128)(2,1)S(1)} %copy-done.6, bf16[512,1024]{1,0:T(8,128)(2,1)S(1)} %copy-done.7, bf16[256,768]{1,0:T(8,128)(2,1)S(1)} %get-tuple-element.20.spread_ref, ...), custom_call_target="tpu_custom_call" | custom-call | flops 4294967296 | bytes 7340032 | tf_op jit(solution)/shard_map/experts/pallas_call | solution.py:314
  82.0 28.4 %all_to_all.23 = bf16[128,8,768]{2,1,0:T(8,128)(2,1)S(1)} all-to-all(bf16[128,8,768]{2,1,0:T(8,128)(2,1)S(1)} %bitcast.23), channel_id=1, replica_groups=mesh['lat'=8,'lon'=16] {'lat','lon'}, dimensions={0} | all-to-all | bytes 3145728 | tf_op jit(solution)/shard_map/all_to_all | solution.py:391
  110.4 1.7 %combine.1 = bf16[128,1024]{1,0:T(8,128)(2,1)} custom-call(bf16[1024,768]{1,0:T(8,128)(2,1)S(1)} %bitcast.18, bf16[4,256,1024]{2,1,0:T(8,128)(2,1)S(1)} %get-tuple-element.22.pick_ref, f32[128,128]{1,0:T(8,128)S(1)} %get-tuple-element.23.gates_ref, bf16[128,1024]{1,0:T(8,128)(2,1)S(1)} %get-tuple-element.24.mixed_ref), custom_call_target="tpu_custom_call" | custom-call | flops 1073741824 | bytes 5242880 | tf_op jit(solution)/shard_map/combine/pallas_call | solution.py:345
Async XLA Ops:
  1.0 20.7 %collective-permute-start.7 = (bf16[8,8,1024]{2,1,0:T(8,128)(2,1)S(1)}, bf16[8,8,1024]{2,1,0:T(8,128)(2,1)S(1)}, u32[]{:S(2)}, u32[]{:S(2)}) collective-permute-start(bf16[8,8,1024]{2,1,0:T(8,128)(2,1)S(1)} %get-tuple-element.25), channel_id=1, source_target_pairs={{0,127},{1,112},{2,113},{3,114},{4,115},{5,116},{6,117},{7,118},{8... | collective-permute-start | bytes 393224 | tf_op jit(solution)/shard_map/ppermute | solution.py:364
  8.4 17.2 %collective-permute-start.5 = (bf16[8,8,1024]{2,1,0:T(8,128)(2,1)S(1)}, bf16[8,8,1024]{2,1,0:T(8,128)(2,1)S(1)}, u32[]{:S(2)}, u32[]{:S(2)}) collective-permute-start(bf16[8,8,1024]{2,1,0:T(8,128)(2,1)S(1)} %get-tuple-element.25), channel_id=1, source_target_pairs={{0,31},{1,16},{2,17},{3,18},{4,19},{5,20},{6,21},{7,22},{8,23},{9,... | collective-permute-start | bytes 393224 | tf_op jit(solution)/shard_map/ppermute | solution.py:364
  9.6 16.0 %collective-permute-start.3 = (bf16[8,8,1024]{2,1,0:T(8,128)(2,1)S(1)}, bf16[8,8,1024]{2,1,0:T(8,128)(2,1)S(1)}, u32[]{:S(2)}, u32[]{:S(2)}) collective-permute-start(bf16[8,8,1024]{2,1,0:T(8,128)(2,1)S(1)} %get-tuple-element.25), channel_id=1, source_target_pairs={{0,15},{1,0},{2,1},{3,2},{4,3},{5,4},{6,5},{7,6},{8,7},{9,8},{10,9... | collective-permute-start | bytes 393224 | tf_op jit(solution)/shard_map/ppermute | solution.py:364
  10.0 29.1 %collective-permute-start = (bf16[8,16,1024]{2,1,0:T(8,128)(2,1)}, bf16[8,16,1024]{2,1,0:T(8,128)(2,1)S(1)}, u32[]{:S(2)}, u32[]{:S(2)}) collective-permute-start(bf16[8,16,1024]{2,1,0:T(8,128)(2,1)} %param.9), channel_id=1, source_target_pairs={{0,16},{1,17},{2,18},{3,19},{4,20},{5,21},{6,22},{7,23},{8,24},{9,... | collective-permute-start | bytes 786440 | tf_op jit(solution)/shard_map/ppermute | solution.py:364
  11.1 28.1 %collective-permute-start.1 = (bf16[8,16,1024]{2,1,0:T(8,128)(2,1)}, bf16[8,16,1024]{2,1,0:T(8,128)(2,1)S(1)}, u32[]{:S(2)}, u32[]{:S(2)}) collective-permute-start(bf16[8,16,1024]{2,1,0:T(8,128)(2,1)} %param.9), channel_id=1, source_target_pairs={{0,112},{1,113},{2,114},{3,115},{4,116},{5,117},{6,118},{7,119},{8... | collective-permute-start | bytes 786440 | tf_op jit(solution)/shard_map/ppermute | solution.py:364
  13.5 2.8 %copy-start = (bf16[1024,3072]{1,0:T(8,128)(2,1)S(1)}, bf16[1024,3072]{1,0:T(8,128)(2,1)}, u32[]{:S(2)}) copy-start(bf16[1024,3072]{1,0:T(8,128)(2,1)} %wv_ref.3) | copy-start | bytes 18874372
  16.3 0.9 copy-start.2
  17.2 10.7 %copy-start.8 = (s32[2]{0:T(128)S(1)}, s32[2]{0:T(128)}, u32[]{:S(2)}) copy-start(s32[2]{0:T(128)} %param.10) | copy-start | bytes 28
  17.2 22.0 %copy-start.1 = (bf16[1024,3072]{1,0:T(8,128)(2,1)S(1)}, bf16[1024,3072]{1,0:T(8,128)(2,1)}, u32[]{:S(2)}) copy-start(bf16[1024,3072]{1,0:T(8,128)(2,1)} %wv_ref.3) | copy-start | bytes 18874372
  17.2 22.0 %copy-start.3 = (bf16[8,16,1024]{2,1,0:T(8,128)(2,1)S(1)}, bf16[8,16,1024]{2,1,0:T(8,128)(2,1)}, u32[]{:S(2)}) copy-start(bf16[8,16,1024]{2,1,0:T(8,128)(2,1)} %param.9) | copy-start | bytes 786436
  17.2 22.0 %copy-start.4 = (bf16[1024,1024]{1,0:T(8,128)(2,1)S(1)}, bf16[1024,1024]{1,0:T(8,128)(2,1)}, u32[]{:S(2)}) copy-start(bf16[1024,1024]{1,0:T(8,128)(2,1)} %wo_ref.1) | copy-start | bytes 6291460
  21.7 10.1 %collective-permute-start.6 = (bf16[8,8,1024]{2,1,0:T(8,128)(2,1)S(1)}, bf16[8,8,1024]{2,1,0:T(8,128)(2,1)S(1)}, u32[]{:S(2)}, u32[]{:S(2)}) collective-permute-start(bf16[8,8,1024]{2,1,0:T(8,128)(2,1)S(1)} %get-tuple-element.26), channel_id=1, source_target_pairs={{0,113},{1,114},{2,115},{3,116},{4,117},{5,118},{6,119},{7,120},{8... | collective-permute-start | bytes 393224 | tf_op jit(solution)/shard_map/ppermute | solution.py:364
  25.6 10.9 %collective-permute-start.4 = (bf16[8,8,1024]{2,1,0:T(8,128)(2,1)S(1)}, bf16[8,8,1024]{2,1,0:T(8,128)(2,1)S(1)}, u32[]{:S(2)}, u32[]{:S(2)}) collective-permute-start(bf16[8,8,1024]{2,1,0:T(8,128)(2,1)S(1)} %get-tuple-element.26), channel_id=1, source_target_pairs={{0,17},{1,18},{2,19},{3,20},{4,21},{5,22},{6,23},{7,24},{8,25},{9,... | collective-permute-start | bytes 393224 | tf_op jit(solution)/shard_map/ppermute | solution.py:364
  25.6 13.6 %collective-permute-start.2 = (bf16[8,8,1024]{2,1,0:T(8,128)(2,1)S(1)}, bf16[8,8,1024]{2,1,0:T(8,128)(2,1)S(1)}, u32[]{:S(2)}, u32[]{:S(2)}) collective-permute-start(bf16[8,8,1024]{2,1,0:T(8,128)(2,1)S(1)} %get-tuple-element.26), channel_id=1, source_target_pairs={{0,1},{1,2},{2,3},{3,4},{4,5},{5,6},{6,7},{7,8},{8,9},{9,10},{10,1... | collective-permute-start | bytes 393224 | tf_op jit(solution)/shard_map/ppermute | solution.py:364
  47.6 28.1 %copy-start.5 = (bf16[1024,512]{1,0:T(8,128)(2,1)S(1)}, bf16[1024,512]{1,0:T(8,128)(2,1)}, u32[]{:S(2)}) copy-start(bf16[1024,512]{1,0:T(8,128)(2,1)} %wg_ref.1) | copy-start | bytes 3145732
  47.6 28.1 %copy-start.6 = (bf16[1024,512]{1,0:T(8,128)(2,1)S(1)}, bf16[1024,512]{1,0:T(8,128)(2,1)}, u32[]{:S(2)}) copy-start(bf16[1024,512]{1,0:T(8,128)(2,1)} %wu_ref.1) | copy-start | bytes 3145732
  47.6 28.1 %copy-start.7 = (bf16[512,1024]{1,0:T(8,128)(2,1)S(1)}, bf16[512,1024]{1,0:T(8,128)(2,1)}, u32[]{:S(2)}) copy-start(bf16[512,1024]{1,0:T(8,128)(2,1)} %wd_ref.1) | copy-start | bytes 3145732

commit v2 on v0

v2 whole, which is shorter than its diff:
```python
import functools

import jax
import jax.numpy as jnp
from jax import lax
from jax.experimental import pallas as pl
from jax.experimental.pallas import tpu as pltpu
from jax.sharding import PartitionSpec as P

HEAD = 64
WIN = 8
MOST = 6
D = 1024
MAIN = 768
TAIL = 256
BLK = 256
BF16 = jnp.bfloat16
F32 = jnp.float32
AXES = ("lat", "lon")


def iota(shape, dim):
    return lax.broadcasted_iota(jnp.int32, shape, dim)


def dot(a, b):
    return jnp.dot(a, b, preferred_element_type=F32)


def rms(x):
    return x * lax.rsqrt(jnp.mean(x * x, axis=-1, keepdims=True) + 1e-05)


def head_norm(y):
    n = y.shape[1]
    square = y * y
    high = square.astype(BF16)
    low = (square - high.astype(F32)).astype(BF16)
    same = jnp.where(iota((n, n), 0) // HEAD == iota((n, n), 1) // HEAD, 1.0, 0.0).astype(BF16)
    total = dot(high, same) + dot(low, same)
    return (y * lax.rsqrt(total * (1.0 / HEAD) + 1e-05)).astype(BF16)


def vmem_call(kernel, name, out_shape, operands, flops, scratch=(), spaces=None):
    spaces = spaces or {}
    specs = [
        pl.BlockSpec(memory_space=spaces.get(i, pltpu.VMEM)) for i in range(len(operands))
    ]
    count = sum(a.size * a.dtype.itemsize for a in operands)
    outs = jax.tree.map(lambda _: pl.BlockSpec(memory_space=pltpu.VMEM), out_shape)
    return pl.pallas_call(
        kernel,
        in_specs=specs,
        out_specs=outs,
        out_shape=out_shape,
        scratch_shapes=list(scratch),
        compiler_params=pltpu.CompilerParams(vmem_limit_bytes=16 << 20),
        cost_estimate=pl.CostEstimate(flops=flops, bytes_accessed=count, transcendentals=0),
        name=name,
    )(*operands)


def contract_last(a, b):
    return lax.dot_general(a, b, (((1,), (1,)), ((), ())), preferred_element_type=F32)


def tail_source(rank, base, j):
    return jnp.where(rank == 6, base + j, jnp.where(rank == 7, base + 3 + j, -1))


def split_kernel(x_ref, low_ref, high_ref):
    halves = x_ref[...].astype(F32).reshape(-1, 2, WIN, D)
    low_ref[...] = halves[:, 0].reshape(-1, D).astype(BF16)
    high_ref[...] = halves[:, 1].reshape(-1, D).astype(BF16)


def plan_kernel(
    experts, shifts_ref, idt_ref, pack_ref, cols_ref, mask_ref, pick_ref, spread_ref, gather_ref
):
    n = idt_ref.shape[1]
    cut_lat = WIN - shifts_ref[0]
    cut_lon = WIN - shifts_ref[1]
    expert = iota((experts, n), 0)
    hits = [idt_ref[k : k + 1, :] == expert for k in range(2)]
    both = jnp.where(hits[0] | hits[1], 1.0, 0.0)
    before = jnp.where(iota((n, n), 0) < iota((n, n), 1), 1.0, 0.0).astype(BF16)
    count = dot(both.astype(BF16), before)
    ranks = [jnp.sum(jnp.where(hit, count, 0.0), axis=0, keepdims=True) for hit in hits]
    ids = idt_ref[...].astype(F32)
    codes = [ids[k : k + 1] * 8.0 + ranks[k] for k in range(2)]
    eye = jnp.where(iota((n, n), 0) == iota((n, n), 1), 1.0, 0.0).astype(BF16)
    cell = iota((1, n), 1)
    flags = [
        jnp.where(flag, 1.0, 0.0)
        for flag in (cell >> 4 >= cut_lat, cell & 7 >= cut_lon, cell >> 3 >= cut_lat)
    ]
    lines = jnp.concatenate([ids, *ranks, *flags, jnp.zeros((1, n), F32)], axis=0)
    lined = contract_last(eye, lines.astype(BF16))
    cols_ref[...] = lined
    rows = 8 * experts
    slot = iota((rows, n), 0)
    rank = slot & 7
    base = slot - rank

    def chosen(want):
        want = want.astype(F32)
        return jnp.where((want == codes[0]) | (want == codes[1]), 1.0, 0.0).astype(BF16)

    main = chosen(slot)
    for j in range(3):
        pack_ref[j, :, 0:n] = main
        pack_ref[j, :, n : 2 * n] = chosen(tail_source(rank, base, j))
    cell = iota((n, 1), 0)
    query = jnp.where(cell >> 4 >= cut_lat, 3, 0) + ((cell & 15) + shifts_ref[1] >> 3)
    key = iota((1, 3 * n), 1)
    narrow = key >= 2 * n
    halo_row = ((key >= n) & (key < 2 * n)) | (key >= 2 * n + WIN * WIN)
    past = jnp.where(narrow, key >> 3 & 7, key >> 4 & 7) >= cut_lat
    lat = lax.axis_index("lat")
    first, final = lat == 0, lat == lax.axis_size("lat") - 1
    beyond = halo_row & ((past & first) | (~past & final))
    window = jnp.where(past != halo_row, 3, 0) + jnp.where(
        narrow, jnp.where(key & 7 >= cut_lon, 0, 2), (key & 15) + shifts_ref[1] >> 3
    )
    valid = jnp.where(query == jnp.where(beyond, -1, window), 1.0, 0.0).astype(BF16)
    mask_ref[0:n, :] = valid
    mask_ref[n : 2 * n, :] = valid
    lanes = 16 * experts
    slot = iota((1, lanes), 1)
    base = (slot >> 4) * 8
    rank = slot & 7
    wants = [jnp.where(rank < MOST, base + rank, -1)]
    wants += [tail_source(rank, base, j) for j in range(3)]
    for k in range(2):
        code = lined[:, k : k + 1] * 8.0 + lined[:, 2 + k : 3 + k]
        for j, want in enumerate(wants):
            pick_ref[j, k * n : (k + 1) * n, :] = jnp.where(
                want.astype(F32) == code, 1.0, 0.0
            ).astype(BF16)
    row = iota((BLK, BLK), 0)
    column = iota((BLK, BLK), 1)
    rank = row & 7
    base = row - rank
    for j in range(3):
        lanes = slice(j * BLK, (j + 1) * BLK)
        source = jnp.where(rank == j, base + 6, jnp.where(rank == 3 + j, base + 7, -1))
        spread_ref[:, lanes] = jnp.where(source == column, 1.0, 0.0).astype(BF16)
        source = tail_source(rank, base, j)
        gather_ref[lanes, :] = jnp.where(source == column, 1.0, 0.0).astype(BF16)


def attend_keys(queries, keys, values, mask):
    n = queries.shape[0] // 2
    low_half = iota((1, 128), 1) < HEAD
    weight = jnp.exp(contract_last(queries, keys)).astype(BF16) * mask
    both = dot(weight, jnp.concatenate([values, jnp.ones_like(values)], axis=1))
    return (
        jnp.where(low_half, both[0:n, 0:128], both[n:, 0:128]),
        jnp.where(low_half, both[0:n, 128:], both[n:, 128:]),
    )


def own_kernel(x_ref, w_ref, mask_ref, qq_ref, num_ref, den_ref):
    n = x_ref.shape[0]
    x = rms(x_ref[...].astype(F32)).astype(BF16)
    mask = mask_ref[:, 0:n]
    low_half = iota((1, 128), 1) < HEAD
    for i in range(D // BLK):
        lanes = slice(i * BLK, (i + 1) * BLK)
        q, k, v = [
            dot(x, w_ref[:, part * D + i * BLK : part * D + (i + 1) * BLK]).astype(BF16)
            for part in range(3)
        ]
        q = head_norm(q.astype(F32)).astype(F32) * 0.125
        k = head_norm(k.astype(F32))
        for pair in range(BLK // 128):
            some = slice(pair * 128, (pair + 1) * 128)
            qq = jnp.concatenate(
                [jnp.where(low_half, q[:, some], 0.0), jnp.where(low_half, 0.0, q[:, some])], axis=0
            ).astype(BF16)
            num, den = attend_keys(qq, k[:, some], v[:, some], mask)
            lanes = slice(i * BLK + pair * 128, i * BLK + (pair + 1) * 128)
            qq_ref[:, lanes] = qq
            num_ref[:, lanes] = num
            den_ref[:, lanes] = den


def side_kernel(left_ref, right_ref, cols_ref, side_ref):
    n = side_ref.shape[0]
    side_ref[...] = jnp.where(
        cols_ref[0:n, 5:6] > 0.5, left_ref[...].astype(F32), right_ref[...].astype(F32)
    ).astype(BF16)


def near_kernel(
    up_ref, down_ref, side_ref, w_ref, mask_ref, cols_ref, qq_ref, num_in, den_in, num_ref, den_ref
):
    n = up_ref.shape[0]
    past = cols_ref[:, 4:5] > 0.5
    band = jnp.where(past, up_ref[...].astype(F32), down_ref[...].astype(F32))
    x = jnp.concatenate(
        [rms(band).astype(BF16), rms(side_ref[...].astype(F32)).astype(BF16)], axis=0
    )
    mask = mask_ref[:, n : n + x.shape[0]]
    for i in range(D // BLK):
        k, v = [
            dot(x, w_ref[:, part * D + i * BLK : part * D + (i + 1) * BLK]).astype(BF16)
            for part in (1, 2)
        ]
        k = head_norm(k.astype(F32))
        for pair in range(BLK // 128):
            some = slice(pair * 128, (pair + 1) * 128)
            lanes = slice(i * BLK + pair * 128, i * BLK + (pair + 1) * 128)
            num, den = attend_keys(qq_ref[:, lanes], k[:, some], v[:, some], mask)
            num_ref[:, lanes] = num_in[:, lanes] + num
            den_ref[:, lanes] = den_in[:, lanes] + den


def last_kernel(
    x_ref, up_ref, down_ref, w_ref, mask_ref, qq_ref, num_ref, den_ref,
    wo_ref, router_ref, cols_ref, pack_ref, mixed_ref, gates_ref, send_ref,
):
    n = x_ref.shape[0]
    m = up_ref.shape[0]
    past = cols_ref[0:m, 6:7] > 0.5
    corner = jnp.where(past, up_ref[...].astype(F32), down_ref[...].astype(F32))
    x = rms(corner).astype(BF16)
    mask = mask_ref[:, 3 * n - m :]
    total = None
    for i in range(D // BLK):
        k, v = [
            dot(x, w_ref[:, part * D + i * BLK : part * D + (i + 1) * BLK]).astype(BF16)
            for part in (1, 2)
        ]
        k = head_norm(k.astype(F32))
        outs = []
        for pair in range(BLK // 128):
            some = slice(pair * 128, (pair + 1) * 128)
            lanes = slice(i * BLK + pair * 128, i * BLK + (pair + 1) * 128)
            num, den = attend_keys(qq_ref[:, lanes], k[:, some], v[:, some], mask)
            outs.append(((num_ref[:, lanes] + num) / (den_ref[:, lanes] + den)).astype(BF16))
        more = dot(jnp.concatenate(outs, axis=1), wo_ref[i * BLK : (i + 1) * BLK, :])
        total = more if total is None else total + more
    mixed = (x_ref[...].astype(F32) + total).astype(BF16)
    mixed_ref[...] = mixed
    normed = rms(mixed.astype(F32)).astype(BF16)
    logits = contract_last(normed, router_ref[...])
    experts = logits.shape[1]
    expert = iota(logits.shape, 1).astype(F32)
    sig = [
        jax.nn.sigmoid(
            jnp.sum(jnp.where(cols_ref[:, k : k + 1] == expert, logits, 0.0), axis=1, keepdims=True)
        )
        for k in range(2)
    ]
    gates_ref[...] = jnp.where(iota((n, 128), 1) == 0, sig[0], sig[1]) / (sig[0] + sig[1])
    for j in range(3):
        lanes = slice(j * BLK, (j + 1) * BLK)
        rows = dot(pack_ref[j], jnp.concatenate([normed[:, lanes], normed[:, MAIN:]], axis=0))
        rows = jnp.broadcast_to(rows.reshape(experts, 1, 8, BLK), (experts, 2, 8, BLK))
        send_ref[:, lanes] = rows.reshape(experts * 16, BLK).astype(BF16)


def expert_kernel(r_ref, wg_ref, wu_ref, wd_ref, spread_ref, gather_ref, out_ref):
    for block in range(r_ref.shape[0] // BLK):
        rows = slice(block * BLK, (block + 1) * BLK)
        tail = None
        for j in range(3):
            lanes = slice(j * BLK, (j + 1) * BLK)
            more = dot(spread_ref[:, lanes], r_ref[rows, lanes])
            tail = more if tail is None else tail + more
        x = jnp.concatenate([r_ref[rows, :], tail.astype(BF16)], axis=1)
        gate = dot(x, wg_ref[...])
        upper = dot(x, wu_ref[...])
        hidden = (jax.nn.silu(gate) * upper).astype(BF16)
        part = dot(hidden, wd_ref[...]).astype(BF16)
        packed = dot(gather_ref[...], part[:, MAIN:])
        kept = (iota((BLK, 1), 0) & 7) < MOST
        for j in range(3):
            lanes = slice(j * BLK, (j + 1) * BLK)
            out_ref[rows, lanes] = jnp.where(
                kept, part[:, lanes].astype(F32), packed[lanes, :]
            ).astype(BF16)


def combine_kernel(back_ref, pick_ref, gates_ref, mixed_ref, out_ref):
    n = mixed_ref.shape[0]
    gates = [gates_ref[:, 0:1], gates_ref[:, 1:2]]

    def finish(lanes, both):
        moe = gates[0] * both[0:n] + gates[1] * both[n:]
        out_ref[:, lanes] = (mixed_ref[:, lanes].astype(F32) + moe).astype(BF16)

    tail = None
    for j in range(3):
        lanes = slice(j * BLK, (j + 1) * BLK)
        back = back_ref[:, lanes]
        finish(lanes, dot(pick_ref[0], back))
        more = dot(pick_ref[1 + j], back)
        tail = more if tail is None else tail + more
    finish(slice(MAIN, D), tail)


def moved(x, down, right):
    n_lat, n_lon = lax.axis_size("lat"), lax.axis_size("lon")
    pairs = [
        (i * n_lon + j, (i + down) % n_lat * n_lon + (j + right) % n_lon)
        for i in range(n_lat)
        for j in range(n_lon)
    ]
    return lax.ppermute(x, AXES, pairs)


def body(tokens, shifts, w_qkv, w_out, router, expert_ids, w_gate, w_up, w_down):
    rows, cols, width = tokens.shape
    n = rows * cols
    experts = router.shape[1]
    shape = jax.ShapeDtypeStruct
    half = shape((n // 2, width), BF16)
    x = tokens.reshape(n, width)
    low, high = vmem_call(split_kernel, "split", [half, half], (x,), 1 << 20)
    left = moved(high, 0, 1)
    right = moved(low, 0, -1)
    up = moved(x, 1, 0)
    down = moved(x, -1, 0)
    sums = [shape((n, width), F32)] * 2
    pack, cells, mask, pick, spread, gather = vmem_call(
        functools.partial(plan_kernel, experts),
        "plan",
        [
            shape((3, 8 * experts, 2 * n), BF16),
            shape((n, 8), F32),
            shape((2 * n, 3 * n), BF16),
            shape((4, 2 * n, 16 * experts), BF16),
            shape((BLK, MAIN), BF16),
            shape((MAIN, BLK), BF16),
        ],
        (shifts, expert_ids.reshape(n, 2).T),
        3 << 30,
        spaces={0: pltpu.SMEM},
    )
    qq, num, den = vmem_call(
        own_kernel,
        "own",
        [shape((2 * n, width), BF16), *sums],
        (x, w_qkv, mask),
        8 * n * width * width,
    )
    left, right, num = lax.optimization_barrier((left, right, num))
    side = vmem_call(side_kernel, "side", half, (left, right, cells), 1 << 10)
    up_side = moved(side, 1, 0)
    down_side = moved(side, -1, 0)
    num, den = vmem_call(
        near_kernel,
        "near",
        sums,
        (up, down, side, w_qkv, mask, cells, qq, num, den),
        8 * n * width * width,
    )
    mixed, gates, send = vmem_call(
        last_kernel,
        "last",
        [shape((n, width), BF16), shape((n, 128), F32), shape((16 * experts, MAIN), BF16)],
        (x, up_side, down_side, w_qkv, mask, qq, num, den, w_out, router.T, cells, pack),
        6 * n * width * width,
    )
    received = lax.all_to_all(send, AXES, split_axis=0, concat_axis=0, tiled=True)
    part = vmem_call(
        expert_kernel,
        "experts",
        shape(received.shape, BF16),
        (received, w_gate, w_up, w_down, spread, gather),
        1 << 32,
    )
    back = lax.all_to_all(part, AXES, split_axis=0, concat_axis=0, tiled=True)
    out = vmem_call(
        combine_kernel, "combine", shape((n, width), BF16), (back, pick, gates, mixed), 1 << 30
    )
    return out.reshape(rows, cols, width)


def solution(mesh):
    placed = (
        P("lat", "lon", None),
        P(),
        P(),
        P(),
        P(),
        P("lat", "lon", None, None),
        P(None, ("lat", "lon")),
        P(None, ("lat", "lon")),
        P(("lat", "lon"), None),
    )
    return jax.shard_map(
        body, mesh=mesh, in_specs=placed, out_specs=P("lat", "lon", None), check_vma=False
    )
```

time: 196 us -> 93.1 us (0.47)
  local copies, waits for them, and re-layouts: 58.3 us -> 2.36 us
  waiting for transfers between devices: 40 us -> 0.27 us
  blocking collectives: 36.4 us -> 60.5 us
  matrix products: 20.1 us -> 0 us
  Pallas kernels: 0 us -> 19.1 us
  other arithmetic: 18 us -> 0.01 us
  between operations: 7.32 us -> 0.14 us
  starting transfers between devices: 14.6 us -> 10.5 us
    all_to_all x1 -> x0, waiting for transfers between devices: 28.8 us -> none  [body(): lax.all_to_all(jnp.stack(results, axis=1), ('lat', 'lon'), split_axis=0,...]
    all_to_all x1 -> x2, blocking collectives: 36.4 us -> 60.5 us  [the longest x1 32.1 us: body(): lax.all_to_all(send, AXES, split_axis=0, concat_axis=0, tiled=True)]
    dot_general x7 -> x0, matrix products: 20.1 us -> none  [the longest x1 6.82 us: body(): jnp.dot(window_cells.reshape(-1, width), w_qkv, preferred_element_type=jn...]
    reshape x5 -> x0, local copies, waits for them, and re-layouts: 20.1 us -> none  [the longest x2 10 us: body(): qkv.reshape(win_lat, WIN, win_lon, WIN, 3, heads, HEAD)]
    pallas_call x0 -> x8, Pallas kernels: none -> 19.1 us  [vmem_call(): pl.pallas_call(kernel, in_specs=specs, out_specs=outs, out_shape=out_shap...]
    ppermute x4 -> x6, waiting for transfers between devices: 11.2 us -> 0.27 us  [moved(): return lax.ppermute(x, AXES, pairs)]
    another operation x4 -> x0, local copies, waits for them, and re-layouts: 8.53 us -> none  [the longest x1 3.73 us: body(): block = received[:, 0].reshape(-1, width)]
    gather x3 -> x0, local copies, waits for them, and re-layouts: 8.32 us -> none  [the longest x2 7.15 us: body(): combined = combined + back_flat[slot_index[copy]].astype(jnp.float32)]
  transfers between devices with their start and end apart: 5 -> 6, of which waited for: 3 -> 1; matrix products, arithmetic and copies ran while one was open for 3% -> 0% of each run, Pallas kernels for 0% -> 9%
where the time goes in v2:
time: 93.1 us; the launch traced here: 92.9 us
  blocking collectives  60.5 us (65%)
  Pallas kernels  19.1 us (21%)
  starting transfers between devices  10.5 us (11%)
  local copies, waits for them, and re-layouts  2.36 us (3%)
    all_to_all x1, blocking collectives, body(): lax.all_to_all(send, AXES, split_axis=0, concat_axis=0, tiled=True)  32.1 us
    all_to_all x1, blocking collectives, body(): back = lax.all_to_all(part, AXES, split_axis=0, concat_axis=0, tiled=True)  28.4 us
    pallas_call x8, Pallas kernels, vmem_call(): pl.pallas_call(kernel, in_specs=specs, out_specs=outs, out_shape=out_shap...  19.1 us
    ppermute x6, starting transfers between devices, moved(): return lax.ppermute(x, AXES, pairs)  10.5 us
    unnamed x22, local copies, waits for them, and re-layouts  2.36 us
  transfers between devices with their start and end apart: 6, of which 1 were waited for; matrix products, arithmetic and copies ran while one was open for 0% of the time, Pallas kernels for 9%

profile of v2, /device:TPU:1, one launch (start us, length us, event | category | flops | bytes accessed | tf_op | source)
XLA Modules:
  0.0 92.9 jit_solution(144810866860671767)
XLA Ops:
  0.0 1.4 %collective-permute-start.5 = (bf16[128,1024]{1,0:T(8,128)(2,1)}, bf16[128,1024]{1,0:T(8,128)(2,1)S(1)}, u32[]{:S(2)}, u32[]{:S(2)}) collective-permute-start(bf16[128,1024]{1,0:T(8,128)(2,1)} %bitcast.13), channel_id=1, source_target_pairs={{0,112},{1,113},{2,114},{3,115},{4,116},{5,117},{6,118},{7,119},{8... | collective-permute-start | bytes 786440 | tf_op jit(solution)/shard_map/ppermute | solution.py:311
  1.4 1.3 %collective-permute-start.4 = (bf16[128,1024]{1,0:T(8,128)(2,1)}, bf16[128,1024]{1,0:T(8,128)(2,1)S(1)}, u32[]{:S(2)}, u32[]{:S(2)}) collective-permute-start(bf16[128,1024]{1,0:T(8,128)(2,1)} %bitcast.14), channel_id=1, source_target_pairs={{0,16},{1,17},{2,18},{3,19},{4,20},{5,21},{6,22},{7,23},{8,24},{9,... | collective-permute-start | bytes 786440 | tf_op jit(solution)/shard_map/ppermute | solution.py:311
  2.7 0.0 copy-start
  2.7 1.0 %copy-done = bf16[8,16,1024]{2,1,0:T(8,128)(2,1)S(1)} copy-done((bf16[8,16,1024]{2,1,0:T(8,128)(2,1)S(1)}, bf16[8,16,1024]{2,1,0:T(8,128)(2,1)}, u32[]{:S(2)}) %copy-start) | copy-done | bytes 262168
  3.7 0.0 slice-start
  3.7 1.3 %collective-permute-start = (bf16[64,1024]{1,0:T(8,128)(2,1)S(1)}, bf16[64,1024]{1,0:T(8,128)(2,1)S(1)}, u32[]{:S(2)}, u32[]{:S(2)}) collective-permute-start(bf16[64,1024]{1,0:T(8,128)(2,1)S(1)} %get-tuple-element.24), channel_id=1, source_target_pairs={{0,1},{1,2},{2,3},{3,4},{4,5},{5,6},{6,7},{7,8},{8,9},{9,10},{10,1... | collective-permute-start | bytes 393224 | tf_op jit(solution)/shard_map/ppermute | solution.py:311
  5.0 4.8 %collective-permute-start.1 = (bf16[64,1024]{1,0:T(8,128)(2,1)S(1)}, bf16[64,1024]{1,0:T(8,128)(2,1)S(1)}, u32[]{:S(2)}, u32[]{:S(2)}) collective-permute-start(bf16[64,1024]{1,0:T(8,128)(2,1)S(1)} %get-tuple-element.25), channel_id=1, source_target_pairs={{0,15},{1,0},{2,1},{3,2},{4,3},{5,4},{6,5},{7,6},{8,7},{9,8},{10,9... | collective-permute-start | bytes 393224 | tf_op jit(solution)/shard_map/ppermute | solution.py:311
  9.8 0.0 copy-start.7
  9.8 0.7 copy-done.7
  10.5 0.0 copy-start.8
  10.5 0.7 copy-done.8
  11.1 0.0 slice-start.1
  11.1 0.0 copy-start.1
  11.1 1.9 %plan.1 = (bf16[3,512,256]{2,1,0:T(8,128)(2,1)S(1)}, f32[128,8]{1,0:T(8,128)S(1)}, bf16[256,384]{1,0:T(8,128)(2,1)S(1)}, bf16[4,256,1024]{2,1,0:T(8,128)(2,1)S(1...) custom-call(s32[2]{0:T(128)S(1)} %copy-done.8, s32[2,128]{1,0:T(2,128)S(1)} %bitcast.22), custom_call_target="tpu_custom_call" | custom-call | flops 3221225472 | bytes 1032 | tf_op jit(solution)/shard_map/plan/pallas_call | solution.py:51
  13.1 0.0 slice-done
  13.1 0.0 slice-done.1
  13.1 0.0 copy-done.1
  13.1 3.1 %own.1 = (bf16[256,1024]{1,0:T(8,128)(2,1)S(1)}, f32[128,1024]{1,0:T(8,128)S(1)}, f32[128,1024]{1,0:T(8,128)S(1)}) custom-call(bf16[128,1024]{1,0:T(8,128)(2,1)S(1)} %bitcast.16, bf16[1024,3072]{1,0:T(8,128)(2,1)S(1)} %bitcast.11, bf16[256,384]{1,0:T(8,128)(2,1)S(1)} %get-tuple-element.26.mask_ref), custom_call_target="tpu_custom_call" | custom-call | flops 1073741824 | bytes 6750208 | tf_op jit(solution)/shard_map/own/pallas_call | solution.py:51
  16.2 0.0 collective-permute-done.left_ref
  16.2 0.0 collective-permute-done.1.right_ref
  16.2 0.1 side.1.side_ref
  16.3 1.6 %collective-permute-start.3 = (bf16[64,1024]{1,0:T(8,128)(2,1)S(1)}, bf16[64,1024]{1,0:T(8,128)(2,1)S(1)}, u32[]{:S(2)}, u32[]{:S(2)}) collective-permute-start(bf16[64,1024]{1,0:T(8,128)(2,1)S(1)} %side.1.side_ref), channel_id=1, source_target_pairs={{0,112},{1,113},{2,114},{3,115},{4,116},{5,117},{6,118},{7,119},{8... | collective-permute-start | bytes 393224 | tf_op jit(solution)/shard_map/ppermute | solution.py:311
  17.9 0.2 collective-permute-start.2
  18.1 0.0 collective-permute-done.5.down_ref
  18.1 0.0 collective-permute-done.4.up_ref
  18.1 0.0 copy-start.2
  18.1 0.0 copy-start.3
  18.1 3.0 %near.1 = (f32[128,1024]{1,0:T(8,128)S(1)}, f32[128,1024]{1,0:T(8,128)S(1)}) custom-call(bf16[128,1024]{1,0:T(8,128)(2,1)S(1)} %collective-permute-done.4.up_ref, bf16[128,1024]{1,0:T(8,128)(2,1)S(1)} %collective-permute-done.5.down_ref, bf16[64,1024]{1,0:T(8,128)(2,1)S(1)} %side.1.side_ref, bf16[1024,3072]{1,0:T(8,128)(2,1)S(1)} %bitcast.11, ...), custom_call_target="tpu_custom_call" | custom-call | flops 1073741824 | bytes 8720384 | tf_op jit(solution)/shard_map/near/pallas_call | solution.py:51
  21.1 0.0 collective-permute-done.3.down_ref
  21.1 0.3 collective-permute-done.2.up_ref
  21.4 0.0 copy-done.2
  21.4 0.0 copy-done.3
  21.4 4.0 %last.1 = (bf16[128,1024]{1,0:T(8,128)(2,1)S(1)}, f32[128,128]{1,0:T(8,128)S(1)}, bf16[1024,768]{1,0:T(8,128)(2,1)S(1)}) custom-call(bf16[128,1024]{1,0:T(8,128)(2,1)S(1)} %bitcast.17, bf16[64,1024]{1,0:T(8,128)(2,1)S(1)} %collective-permute-done.2.up_ref, bf16[64,1024]{1,0:T(8,128)(2,1)S(1)} %collective-permute-done.3.down_ref, ...), custom_call_target="tpu_custom_call" | custom-call | flops 805306368 | bytes 11603968 | tf_op jit(solution)/shard_map/last/pallas_call | solution.py:51
  25.4 0.0 copy-start.4
  25.5 0.0 copy-start.5
  25.5 0.0 copy-start.6
  25.5 32.1 %all_to_all.22 = bf16[128,8,768]{2,1,0:T(8,128)(2,1)S(1)} all-to-all(bf16[128,8,768]{2,1,0:T(8,128)(2,1)S(1)} %bitcast.18), channel_id=1, replica_groups=mesh['lat'=8,'lon'=16] {'lat','lon'}, dimensions={0} | all-to-all | bytes 3145728 | tf_op jit(solution)/shard_map/all_to_all | solution.py:367
  57.6 0.0 copy-done.4
  57.6 0.0 copy-done.5
  57.6 0.0 copy-done.6
  57.6 5.2 %experts.1 = bf16[1024,768]{1,0:T(8,128)(2,1)S(1)} custom-call(bf16[1024,768]{1,0:T(8,128)(2,1)S(1)} %bitcast.19, bf16[1024,512]{1,0:T(8,128)(2,1)S(1)} %copy-done.4, bf16[1024,512]{1,0:T(8,128)(2,1)S(1)} %copy-done.5, bf16[512,1024]{1,0:T(8,128)(2,1)S(1)} %copy-done.6, bf16[256,768]{1,0:T(8,128)(2,1)S(1)} %get-tuple-element.38.spread_ref, ...), custom_call_target="tpu_custom_call" | custom-call | flops 4294967296 | bytes 5505024 | tf_op jit(solution)/shard_map/experts/pallas_call | solution.py:51
  62.8 28.4 %all_to_all.23 = bf16[128,8,768]{2,1,0:T(8,128)(2,1)S(1)} all-to-all(bf16[128,8,768]{2,1,0:T(8,128)(2,1)S(1)} %bitcast.20), channel_id=1, replica_groups=mesh['lat'=8,'lon'=16] {'lat','lon'}, dimensions={0} | all-to-all | bytes 3145728 | tf_op jit(solution)/shard_map/all_to_all | solution.py:375
  91.2 1.7 %combine.1 = bf16[128,1024]{1,0:T(8,128)(2,1)} custom-call(bf16[1024,768]{1,0:T(8,128)(2,1)S(1)} %bitcast.12, bf16[4,256,1024]{2,1,0:T(8,128)(2,1)S(1)} %get-tuple-element.40.pick_ref, f32[128,128]{1,0:T(8,128)S(1)} %get-tuple-element.41.gates_ref, bf16[128,1024]{1,0:T(8,128)(2,1)S(1)} %get-tuple-element.42.mixed_ref), custom_call_target="tpu_custom_call" | custom-call | flops 1073741824 | bytes 3997696 | tf_op jit(solution)/shard_map/combine/pallas_call | solution.py:51
  (2 shorter events, 0.0 us)
Async XLA Ops:
  0.0 18.1 %collective-permute-start.5 = (bf16[128,1024]{1,0:T(8,128)(2,1)}, bf16[128,1024]{1,0:T(8,128)(2,1)S(1)}, u32[]{:S(2)}, u32[]{:S(2)}) collective-permute-start(bf16[128,1024]{1,0:T(8,128)(2,1)} %bitcast.13), channel_id=1, source_target_pairs={{0,112},{1,113},{2,114},{3,115},{4,116},{5,117},{6,118},{7,119},{8... | collective-permute-start | bytes 786440 | tf_op jit(solution)/shard_map/ppermute | solution.py:311
  1.4 16.7 %collective-permute-start.4 = (bf16[128,1024]{1,0:T(8,128)(2,1)}, bf16[128,1024]{1,0:T(8,128)(2,1)S(1)}, u32[]{:S(2)}, u32[]{:S(2)}) collective-permute-start(bf16[128,1024]{1,0:T(8,128)(2,1)} %bitcast.14), channel_id=1, source_target_pairs={{0,16},{1,17},{2,18},{3,19},{4,20},{5,21},{6,22},{7,23},{8,24},{9,... | collective-permute-start | bytes 786440 | tf_op jit(solution)/shard_map/ppermute | solution.py:311
  2.7 1.0 %copy-start = (bf16[8,16,1024]{2,1,0:T(8,128)(2,1)S(1)}, bf16[8,16,1024]{2,1,0:T(8,128)(2,1)}, u32[]{:S(2)}) copy-start(bf16[8,16,1024]{2,1,0:T(8,128)(2,1)} %param.9) | copy-start | bytes 786436
  3.7 9.4 %slice-start = ((s8[6291456]{0:T(1024)(128)(4,1)}), s8[4194304]{0:T(1024)(128)(4,1)S(1)}, s32[]{:S(2)}) async-start(s8[6291456]{0:T(1024)(128)(4,1)} %bitcast.10), calls=%async_computation.2 | async-start | bytes 8388608
  3.7 12.5 %collective-permute-start = (bf16[64,1024]{1,0:T(8,128)(2,1)S(1)}, bf16[64,1024]{1,0:T(8,128)(2,1)S(1)}, u32[]{:S(2)}, u32[]{:S(2)}) collective-permute-start(bf16[64,1024]{1,0:T(8,128)(2,1)S(1)} %get-tuple-element.24), channel_id=1, source_target_pairs={{0,1},{1,2},{2,3},{3,4},{4,5},{5,6},{6,7},{7,8},{8,9},{9,10},{10,1... | collective-permute-start | bytes 393224 | tf_op jit(solution)/shard_map/ppermute | solution.py:311
  5.0 11.2 %collective-permute-start.1 = (bf16[64,1024]{1,0:T(8,128)(2,1)S(1)}, bf16[64,1024]{1,0:T(8,128)(2,1)S(1)}, u32[]{:S(2)}, u32[]{:S(2)}) collective-permute-start(bf16[64,1024]{1,0:T(8,128)(2,1)S(1)} %get-tuple-element.25), channel_id=1, source_target_pairs={{0,15},{1,0},{2,1},{3,2},{4,3},{5,4},{6,5},{7,6},{8,7},{9,8},{10,9... | collective-permute-start | bytes 393224 | tf_op jit(solution)/shard_map/ppermute | solution.py:311
  9.8 0.7 copy-start.7
  10.5 0.7 copy-start.8
  11.1 2.0 %slice-start.1 = ((s8[6291456]{0:T(1024)(128)(4,1)}), s8[2097152]{0:T(1024)(128)(4,1)S(1)}, s32[]{:S(2)}) async-start(s8[6291456]{0:T(1024)(128)(4,1)} %bitcast.10), calls=%async_computation.3 | async-start | bytes 4194304
  11.1 2.0 %copy-start.1 = (bf16[8,16,1024]{2,1,0:T(8,128)(2,1)S(1)}, bf16[8,16,1024]{2,1,0:T(8,128)(2,1)}, u32[]{:S(2)}) copy-start(bf16[8,16,1024]{2,1,0:T(8,128)(2,1)} %param.9) | copy-start | bytes 786436
  16.3 4.8 %collective-permute-start.3 = (bf16[64,1024]{1,0:T(8,128)(2,1)S(1)}, bf16[64,1024]{1,0:T(8,128)(2,1)S(1)}, u32[]{:S(2)}, u32[]{:S(2)}) collective-permute-start(bf16[64,1024]{1,0:T(8,128)(2,1)S(1)} %side.1.side_ref), channel_id=1, source_target_pairs={{0,112},{1,113},{2,114},{3,115},{4,116},{5,117},{6,118},{7,119},{8... | collective-permute-start | bytes 393224 | tf_op jit(solution)/shard_map/ppermute | solution.py:311
  17.9 3.5 %collective-permute-start.2 = (bf16[64,1024]{1,0:T(8,128)(2,1)S(1)}, bf16[64,1024]{1,0:T(8,128)(2,1)S(1)}, u32[]{:S(2)}, u32[]{:S(2)}) collective-permute-start(bf16[64,1024]{1,0:T(8,128)(2,1)S(1)} %side.1.side_ref), channel_id=1, source_target_pairs={{0,16},{1,17},{2,18},{3,19},{4,20},{5,21},{6,22},{7,23},{8,24},{9,... | collective-permute-start | bytes 393224 | tf_op jit(solution)/shard_map/ppermute | solution.py:311
  18.1 3.3 %copy-start.2 = (bf16[1024,1024]{1,0:T(8,128)(2,1)S(1)}, bf16[1024,1024]{1,0:T(8,128)(2,1)}, u32[]{:S(2)}) copy-start(bf16[1024,1024]{1,0:T(8,128)(2,1)} %wo_ref.1) | copy-start | bytes 6291460
  18.1 3.3 %copy-start.3 = (bf16[1024,64]{0,1:T(8,128)(2,1)S(1)}, bf16[1024,64]{0,1:T(8,128)(2,1)}, u32[]{:S(2)}) copy-start(bf16[1024,64]{0,1:T(8,128)(2,1)} %param.13) | copy-start | bytes 393220
  25.4 32.1 %copy-start.4 = (bf16[1024,512]{1,0:T(8,128)(2,1)S(1)}, bf16[1024,512]{1,0:T(8,128)(2,1)}, u32[]{:S(2)}) copy-start(bf16[1024,512]{1,0:T(8,128)(2,1)} %wg_ref.1) | copy-start | bytes 3145732
  25.5 32.1 %copy-start.5 = (bf16[1024,512]{1,0:T(8,128)(2,1)S(1)}, bf16[1024,512]{1,0:T(8,128)(2,1)}, u32[]{:S(2)}) copy-start(bf16[1024,512]{1,0:T(8,128)(2,1)} %wu_ref.1) | copy-start | bytes 3145732
  25.5 32.1 %copy-start.6 = (bf16[512,1024]{1,0:T(8,128)(2,1)S(1)}, bf16[512,1024]{1,0:T(8,128)(2,1)}, u32[]{:S(2)}) copy-start(bf16[512,1024]{1,0:T(8,128)(2,1)} %wd_ref.1) | copy-start | bytes 3145732

commit v3 on v2

v3 whole, which is shorter than its diff:
```python
import functools

import jax
import jax.numpy as jnp
from jax import lax
from jax.experimental import pallas as pl
from jax.experimental.pallas import tpu as pltpu
from jax.sharding import PartitionSpec as P

HEAD = 64
WIN = 8
MOST = 6
D = 1024
BLK = 256
BF16 = jnp.bfloat16
F32 = jnp.float32
AXES = ("lat", "lon")


def iota(shape, dim):
    return lax.broadcasted_iota(jnp.int32, shape, dim)


def dot(a, b):
    return jnp.dot(a, b, preferred_element_type=F32)


def rms(x):
    return x * lax.rsqrt(jnp.mean(x * x, axis=-1, keepdims=True) + 1e-05)


def head_norm(y):
    n = y.shape[1]
    same = jnp.where(iota((n, n), 0) // HEAD == iota((n, n), 1) // HEAD, 1.0, 0.0).astype(BF16)
    total = dot((y * y).astype(BF16), same)
    return (y * lax.rsqrt(total * (1.0 / HEAD) + 1e-05)).astype(BF16)


def vmem_call(kernel, name, out_shape, operands, flops, scratch=(), spaces=None):
    spaces = spaces or {}
    specs = [
        pl.BlockSpec(memory_space=spaces.get(i, pltpu.VMEM)) for i in range(len(operands))
    ]
    count = sum(a.size * a.dtype.itemsize for a in operands)
    outs = jax.tree.map(lambda _: pl.BlockSpec(memory_space=pltpu.VMEM), out_shape)
    return pl.pallas_call(
        kernel,
        in_specs=specs,
        out_specs=outs,
        out_shape=out_shape,
        scratch_shapes=list(scratch),
        compiler_params=pltpu.CompilerParams(vmem_limit_bytes=16 << 20),
        cost_estimate=pl.CostEstimate(flops=flops, bytes_accessed=count, transcendentals=0),
        name=name,
    )(*operands)


def contract_last(a, b):
    return lax.dot_general(a, b, (((1,), (1,)), ((), ())), preferred_element_type=F32)


def split_kernel(tokens_ref, x_ref, low_ref, high_ref):
    x = tokens_ref[...]
    x_ref[...] = x
    halves = x.astype(F32).reshape(-1, 2, WIN, D)
    low_ref[...] = halves[:, 0].reshape(-1, D).astype(BF16)
    high_ref[...] = halves[:, 1].reshape(-1, D).astype(BF16)


def plan_kernel(experts, shifts_ref, ids_ref, pack_ref, cells_ref, mask_ref, pick_ref):
    n = ids_ref.shape[1]
    shift_lat, shift_lon = shifts_ref[0], shifts_ref[1]
    cut_lat = WIN - shift_lat
    cut_lon = WIN - shift_lon
    expert = iota((experts, n), 0)
    hits = [ids_ref[k : k + 1, :] == expert for k in range(2)]
    both = jnp.where(hits[0] | hits[1], 1.0, 0.0)
    before = jnp.where(iota((n, n), 0) < iota((n, n), 1), 1.0, 0.0).astype(BF16)
    count = dot(both.astype(BF16), before)
    ranks = [jnp.sum(jnp.where(hit, count, 0.0), axis=0, keepdims=True) for hit in hits]
    ids = ids_ref[...].astype(F32)
    cell = iota((1, n), 1)
    flags = [
        jnp.where(flag, 1.0, 0.0)
        for flag in (cell >> 4 >= cut_lat, cell & 7 >= cut_lon, cell >> 3 >= cut_lat)
    ]
    lines = jnp.concatenate([ids, *ranks, *flags, jnp.zeros((1, n), F32)], axis=0)
    eye = jnp.where(iota((n, n), 0) == iota((n, n), 1), 1.0, 0.0).astype(BF16)
    cells = contract_last(eye, lines.astype(BF16))
    cells_ref[...] = cells
    slot = iota((MOST * experts, n), 0).astype(F32)
    codes = [ids[k : k + 1] * MOST + ranks[k] for k in range(2)]
    pack_ref[...] = jnp.where((slot == codes[0]) | (slot == codes[1]), 1.0, 0.0).astype(BF16)
    slot = iota((1, 2 * MOST * experts), 1)
    slot = (slot // (2 * MOST) * MOST + slot % MOST).astype(F32)
    for k in range(2):
        code = cells[:, k : k + 1] * MOST + cells[:, 2 + k : 3 + k]
        pick_ref[k * n : (k + 1) * n, :] = jnp.where(slot == code, 1.0, 0.0).astype(BF16)
    cell = iota((n, 1), 0)
    query = jnp.where(cell >> 4 >= cut_lat, 3, 0) + ((cell & 15) + shift_lon >> 3)
    key = iota((1, 3 * n), 1)
    narrow = key >= 2 * n
    halo_row = ((key >= n) & (key < 2 * n)) | (key >= 2 * n + WIN * WIN)
    past = jnp.where(narrow, key >> 3 & 7, key >> 4 & 7) >= cut_lat
    lat = lax.axis_index("lat")
    first, final = lat == 0, lat == lax.axis_size("lat") - 1
    beyond = halo_row & ((past & first) | (~past & final))
    window = jnp.where(past != halo_row, 3, 0) + jnp.where(
        narrow, jnp.where(key & 7 >= cut_lon, 0, 2), (key & 15) + shift_lon >> 3
    )
    valid = jnp.where(query == jnp.where(beyond, -1, window), 1.0, 0.0).astype(BF16)
    mask_ref[0:n, :] = valid
    mask_ref[n : 2 * n, :] = valid


def attend_keys(queries, keys, values, mask):
    n = queries.shape[0] // 2
    low_half = iota((1, 128), 1) < HEAD
    weight = jnp.exp(contract_last(queries, keys)).astype(BF16) * mask
    both = dot(weight, jnp.concatenate([values, jnp.ones_like(values)], axis=1))
    return (
        jnp.where(low_half, both[0:n, 0:128], both[n:, 0:128]),
        jnp.where(low_half, both[0:n, 128:], both[n:, 128:]),
    )


def own_kernel(x_ref, w_ref, mask_ref, qq_ref, num_ref, den_ref):
    n = x_ref.shape[0]
    x = rms(x_ref[...].astype(F32)).astype(BF16)
    mask = mask_ref[:, 0:n]
    low_half = iota((1, 128), 1) < HEAD
    for i in range(D // BLK):
        lanes = slice(i * BLK, (i + 1) * BLK)
        q, k, v = [
            dot(x, w_ref[:, part * D + i * BLK : part * D + (i + 1) * BLK]).astype(BF16)
            for part in range(3)
        ]
        q = head_norm(q.astype(F32)).astype(F32) * 0.125
        k = head_norm(k.astype(F32))
        for pair in range(BLK // 128):
            some = slice(pair * 128, (pair + 1) * 128)
            qq = jnp.concatenate(
                [jnp.where(low_half, q[:, some], 0.0), jnp.where(low_half, 0.0, q[:, some])], axis=0
            ).astype(BF16)
            num, den = attend_keys(qq, k[:, some], v[:, some], mask)
            lanes = slice(i * BLK + pair * 128, i * BLK + (pair + 1) * 128)
            qq_ref[:, lanes] = qq
            num_ref[:, lanes] = num
            den_ref[:, lanes] = den


def side_kernel(left_ref, right_ref, cells_ref, side_ref):
    n = side_ref.shape[0]
    side_ref[...] = jnp.where(
        cells_ref[0:n, 5:6] > 0.5, left_ref[...].astype(F32), right_ref[...].astype(F32)
    ).astype(BF16)


def near_kernel(
    up_ref, down_ref, side_ref, w_ref, mask_ref, cells_ref, qq_ref, num_in, den_in, num_ref, den_ref
):
    n = up_ref.shape[0]
    past = cells_ref[:, 4:5] > 0.5
    band = jnp.where(past, up_ref[...].astype(F32), down_ref[...].astype(F32))
    x = jnp.concatenate(
        [rms(band).astype(BF16), rms(side_ref[...].astype(F32)).astype(BF16)], axis=0
    )
    mask = mask_ref[:, n : n + x.shape[0]]
    for i in range(D // BLK):
        k, v = [
            dot(x, w_ref[:, part * D + i * BLK : part * D + (i + 1) * BLK]).astype(BF16)
            for part in (1, 2)
        ]
        k = head_norm(k.astype(F32))
        for pair in range(BLK // 128):
            some = slice(pair * 128, (pair + 1) * 128)
            lanes = slice(i * BLK + pair * 128, i * BLK + (pair + 1) * 128)
            num, den = attend_keys(qq_ref[:, lanes], k[:, some], v[:, some], mask)
            num_ref[:, lanes] = num_in[:, lanes] + num
            den_ref[:, lanes] = den_in[:, lanes] + den


def last_kernel(
    x_ref, up_ref, down_ref, w_ref, mask_ref, qq_ref, num_ref, den_ref,
    wo_ref, router_ref, cells_ref, pack_ref, mixed_ref, gates_ref, send_ref,
):
    n = x_ref.shape[0]
    m = up_ref.shape[0]
    past = cells_ref[0:m, 6:7] > 0.5
    corner = jnp.where(past, up_ref[...].astype(F32), down_ref[...].astype(F32))
    x = rms(corner).astype(BF16)
    mask = mask_ref[:, 3 * n - m :]
    total = None
    for i in range(D // BLK):
        k, v = [
            dot(x, w_ref[:, part * D + i * BLK : part * D + (i + 1) * BLK]).astype(BF16)
            for part in (1, 2)
        ]
        k = head_norm(k.astype(F32))
        outs = []
        for pair in range(BLK // 128):
            some = slice(pair * 128, (pair + 1) * 128)
            lanes = slice(i * BLK + pair * 128, i * BLK + (pair + 1) * 128)
            num, den = attend_keys(qq_ref[:, lanes], k[:, some], v[:, some], mask)
            outs.append(((num_ref[:, lanes] + num) / (den_ref[:, lanes] + den)).astype(BF16))
        more = dot(jnp.concatenate(outs, axis=1), wo_ref[i * BLK : (i + 1) * BLK, :])
        total = more if total is None else total + more
    mixed = (x_ref[...].astype(F32) + total).astype(BF16)
    mixed_ref[...] = mixed
    normed = rms(mixed.astype(F32)).astype(BF16)
    logits = contract_last(normed, router_ref[...])
    experts = logits.shape[1]
    expert = iota(logits.shape, 1).astype(F32)
    sig = [
        jax.nn.sigmoid(
            jnp.sum(jnp.where(cells_ref[:, k : k + 1] == expert, logits, 0.0), axis=1, keepdims=True)
        )
        for k in range(2)
    ]
    gates_ref[...] = jnp.where(iota((n, 128), 1) == 0, sig[0], sig[1]) / (sig[0] + sig[1])
    rows = dot(pack_ref[...], normed).astype(BF16).reshape(-1, 8, 128)
    rows = rows.reshape(experts, MOST, 8, 128)
    send_ref[:, 0] = rows
    send_ref[:, 1] = rows


def expert_kernel(rows_ref, wg_ref, wu_ref, wd_ref, out_ref):
    x = rows_ref[...].reshape(-1, D)
    gate = dot(x, wg_ref[...])
    upper = dot(x, wu_ref[...])
    hidden = (jax.nn.silu(gate) * upper).astype(BF16)
    out_ref[...] = dot(hidden, wd_ref[...]).astype(BF16).reshape(out_ref.shape)


def combine_kernel(back_ref, pick_ref, gates_ref, mixed_ref, out_ref):
    n = mixed_ref.shape[0]
    both = dot(pick_ref[...], back_ref[...].reshape(-1, D))
    moe = gates_ref[:, 0:1] * both[0:n] + gates_ref[:, 1:2] * both[n:]
    out_ref[...] = (mixed_ref[...].astype(F32) + moe).astype(BF16)


def moved(x, down, right):
    n_lat, n_lon = lax.axis_size("lat"), lax.axis_size("lon")
    pairs = [
        (i * n_lon + j, (i + down) % n_lat * n_lon + (j + right) % n_lon)
        for i in range(n_lat)
        for j in range(n_lon)
    ]
    return lax.ppermute(x, AXES, pairs)


def body(tokens, shifts, w_qkv, w_out, router, expert_ids, w_gate, w_up, w_down):
    rows, cols, width = tokens.shape
    n = rows * cols
    experts = router.shape[1]
    shape = jax.ShapeDtypeStruct
    half = shape((n // 2, width), BF16)
    cells, ids, shifts = lax.optimization_barrier(
        (tokens.reshape(n, width), expert_ids.reshape(n, 2).T, shifts)
    )
    x, low, high = vmem_call(
        split_kernel, "split", [shape((n, width), BF16), half, half], (cells,), 1 << 20
    )
    left = moved(high, 0, 1)
    right = moved(low, 0, -1)
    up = moved(x, 1, 0)
    down = moved(x, -1, 0)
    sums = [shape((n, width), F32)] * 2
    pack, cells, mask, pick = vmem_call(
        functools.partial(plan_kernel, experts),
        "plan",
        [
            shape((MOST * experts, n), BF16),
            shape((n, 8), F32),
            shape((2 * n, 3 * n), BF16),
            shape((2 * n, 2 * MOST * experts), BF16),
        ],
        (shifts, ids),
        3 << 30,
        spaces={0: pltpu.SMEM},
    )
    qq, num, den = vmem_call(
        own_kernel,
        "own",
        [shape((2 * n, width), BF16), *sums],
        (x, w_qkv, mask),
        8 * n * width * width,
    )
    left, right, num = lax.optimization_barrier((left, right, num))
    side = vmem_call(side_kernel, "side", half, (left, right, cells), 1 << 10)
    up_side = moved(side, 1, 0)
    down_side = moved(side, -1, 0)
    num, den = vmem_call(
        near_kernel,
        "near",
        sums,
        (up, down, side, w_qkv, mask, cells, qq, num, den),
        8 * n * width * width,
    )
    mixed, gates, send = vmem_call(
        last_kernel,
        "last",
        [
            shape((n, width), BF16),
            shape((n, 128), F32),
            shape((experts, 2, MOST, 8, width // 8), BF16),
        ],
        (x, up_side, down_side, w_qkv, mask, qq, num, den, w_out, router.T, cells, pack),
        6 * n * width * width,
    )
    send = send.reshape(2 * experts * MOST, 8, width // 8)
    received = lax.all_to_all(send, AXES, split_axis=0, concat_axis=0, tiled=True)
    part = vmem_call(
        expert_kernel, "experts", shape(received.shape, BF16), (received, w_gate, w_up, w_down), 1 << 32
    )
    back = lax.all_to_all(part, AXES, split_axis=0, concat_axis=0, tiled=True)
    out = vmem_call(
        combine_kernel, "combine", shape((n, width), BF16), (back, pick, gates, mixed), 1 << 30
    )
    return out.reshape(rows, cols, width)


def solution(mesh):
    placed = (
        P("lat", "lon", None),
        P(),
        P(),
        P(),
        P(),
        P("lat", "lon", None, None),
        P(None, ("lat", "lon")),
        P(None, ("lat", "lon")),
        P(("lat", "lon"), None),
    )
    return jax.shard_map(
        body, mesh=mesh, in_specs=placed, out_specs=P("lat", "lon", None), check_vma=False
    )
```

time: 93.1 us -> 88.8 us (0.954)
  Pallas kernels: 19.1 us -> 14.8 us
    pallas_call x8, Pallas kernels: 19.1 us -> 14.8 us  [vmem_call(): pl.pallas_call(kernel, in_specs=specs, out_specs=outs, out_shape=out_shap...]
    unnamed x22 -> x20, local copies, waits for them, and re-layouts: 2.36 us -> 2.32 us
  transfers between devices with their start and end apart: 6 -> 6, of which waited for: 1 -> 1; matrix products, arithmetic and copies ran while one was open for 0% -> 0% of each run, Pallas kernels for 9% -> 8%
where the time goes in v3:
time: 88.8 us; the launch traced here: 88.6 us
  blocking collectives  60.5 us (68%)
  Pallas kernels  14.8 us (17%)
  starting transfers between devices  10.4 us (12%)
  local copies, waits for them, and re-layouts  2.32 us (3%)
    all_to_all x1, blocking collectives, body(): lax.all_to_all(send, AXES, split_axis=0, concat_axis=0, tiled=True)  32.1 us
    all_to_all x1, blocking collectives, body(): back = lax.all_to_all(part, AXES, split_axis=0, concat_axis=0, tiled=True)  28.4 us
    pallas_call x8, Pallas kernels, vmem_call(): pl.pallas_call(kernel, in_specs=specs, out_specs=outs, out_shape=out_shap...  14.8 us
    ppermute x6, starting transfers between devices, moved(): return lax.ppermute(x, AXES, pairs)  10.4 us
    unnamed x20, local copies, waits for them, and re-layouts  2.32 us
  transfers between devices with their start and end apart: 6, of which 1 were waited for; matrix products, arithmetic and copies ran while one was open for 0% of the time, Pallas kernels for 8%

profile of v3, /device:TPU:1, one launch (start us, length us, event | category | flops | bytes accessed | tf_op | source)
XLA Modules:
  0.0 88.6 jit_solution(11476082084741513571)
XLA Ops:
  0.0 0.0 copy-start.1
  0.0 0.9 %copy-done.1 = bf16[8,16,1024]{2,1,0:T(8,128)(2,1)S(1)} copy-done((bf16[8,16,1024]{2,1,0:T(8,128)(2,1)S(1)}, bf16[8,16,1024]{2,1,0:T(8,128)(2,1)}, u32[]{:S(2)}) %copy-start.1) | copy-done | bytes 262168
  1.0 0.0 slice-start
  1.0 1.4 %collective-permute-start.5 = (bf16[128,1024]{1,0:T(8,128)(2,1)S(1)}, bf16[128,1024]{1,0:T(8,128)(2,1)S(1)}, u32[]{:S(2)}, u32[]{:S(2)}) collective-permute-start(bf16[128,1024]{1,0:T(8,128)(2,1)S(1)} %get-tuple-element.27.x_ref), channel_id=1, source_target_pairs={{0,112},{1,113},{2,114},{3,115},{4,116},{5,117},{6,118},{7,119},{8... | collective-permute-start | bytes 786440 | tf_op jit(solution)/shard_map/ppermute | solution.py:249
  2.4 1.3 %collective-permute-start.4 = (bf16[128,1024]{1,0:T(8,128)(2,1)S(1)}, bf16[128,1024]{1,0:T(8,128)(2,1)S(1)}, u32[]{:S(2)}, u32[]{:S(2)}) collective-permute-start(bf16[128,1024]{1,0:T(8,128)(2,1)S(1)} %get-tuple-element.27.x_ref), channel_id=1, source_target_pairs={{0,16},{1,17},{2,18},{3,19},{4,20},{5,21},{6,22},{7,23},{8,24},{9,... | collective-permute-start | bytes 786440 | tf_op jit(solution)/shard_map/ppermute | solution.py:249
  3.7 1.2 %collective-permute-start = (bf16[64,1024]{1,0:T(8,128)(2,1)S(1)}, bf16[64,1024]{1,0:T(8,128)(2,1)S(1)}, u32[]{:S(2)}, u32[]{:S(2)}) collective-permute-start(bf16[64,1024]{1,0:T(8,128)(2,1)S(1)} %get-tuple-element.28), channel_id=1, source_target_pairs={{0,1},{1,2},{2,3},{3,4},{4,5},{5,6},{6,7},{7,8},{8,9},{9,10},{10,1... | collective-permute-start | bytes 393224 | tf_op jit(solution)/shard_map/ppermute | solution.py:249
  4.9 0.0 slice-start.1
  4.9 4.7 %collective-permute-start.1 = (bf16[64,1024]{1,0:T(8,128)(2,1)S(1)}, bf16[64,1024]{1,0:T(8,128)(2,1)S(1)}, u32[]{:S(2)}, u32[]{:S(2)}) collective-permute-start(bf16[64,1024]{1,0:T(8,128)(2,1)S(1)} %get-tuple-element.29), channel_id=1, source_target_pairs={{0,15},{1,0},{2,1},{3,2},{4,3},{5,4},{6,5},{7,6},{8,7},{9,8},{10,9... | collective-permute-start | bytes 393224 | tf_op jit(solution)/shard_map/ppermute | solution.py:249
  9.7 0.0 copy-start.6
  9.7 0.7 copy-done.6
  10.4 0.0 copy-start.7
  10.4 0.7 copy-done.7
  11.0 1.0 %plan.1 = (bf16[384,128]{1,0:T(8,128)(2,1)S(1)}, f32[128,8]{1,0:T(8,128)S(1)}, bf16[256,384]{1,0:T(8,128)(2,1)S(1)}, bf16[256,768]{1,0:T(8,128)(2,1)S(1)}) custom-call(s32[2]{0:T(128)S(1)} %copy-done.7, s32[2,128]{1,0:T(2,128)S(1)} %bitcast.12), custom_call_target="tpu_custom_call" | custom-call | flops 3221225472 | bytes 1032 | tf_op jit(solution)/shard_map/plan/pallas_call | solution.py:46
  12.1 0.0 slice-done
  12.1 0.0 slice-done.1
  12.1 2.8 %own.1 = (bf16[256,1024]{1,0:T(8,128)(2,1)S(1)}, f32[128,1024]{1,0:T(8,128)S(1)}, f32[128,1024]{1,0:T(8,128)S(1)}) custom-call(bf16[128,1024]{1,0:T(8,128)(2,1)S(1)} %get-tuple-element.27.x_ref, bf16[1024,3072]{1,0:T(8,128)(2,1)S(1)} %bitcast.8, bf16[256,384]{1,0:T(8,128)(2,1)S(1)} %get-tuple-element.32.mask_ref), custom_call_target="tpu_custom_call" | custom-call | flops 1073741824 | bytes 6750208 | tf_op jit(solution)/shard_map/own/pallas_call | solution.py:46
  14.9 0.0 collective-permute-done.left_ref
  14.9 0.0 collective-permute-done.1.right_ref
  14.9 0.1 side.1.side_ref
  15.0 1.6 %collective-permute-start.3 = (bf16[64,1024]{1,0:T(8,128)(2,1)S(1)}, bf16[64,1024]{1,0:T(8,128)(2,1)S(1)}, u32[]{:S(2)}, u32[]{:S(2)}) collective-permute-start(bf16[64,1024]{1,0:T(8,128)(2,1)S(1)} %side.1.side_ref), channel_id=1, source_target_pairs={{0,112},{1,113},{2,114},{3,115},{4,116},{5,117},{6,118},{7,119},{8... | collective-permute-start | bytes 393224 | tf_op jit(solution)/shard_map/ppermute | solution.py:249
  16.6 0.1 collective-permute-start.2
  16.8 0.0 collective-permute-done.5.down_ref
  16.8 0.0 collective-permute-done.4.up_ref
  16.8 0.0 copy-start
  16.8 0.0 copy-start.2
  16.8 2.9 %near.1 = (f32[128,1024]{1,0:T(8,128)S(1)}, f32[128,1024]{1,0:T(8,128)S(1)}) custom-call(bf16[128,1024]{1,0:T(8,128)(2,1)S(1)} %collective-permute-done.4.up_ref, bf16[128,1024]{1,0:T(8,128)(2,1)S(1)} %collective-permute-done.5.down_ref, bf16[64,1024]{1,0:T(8,128)(2,1)S(1)} %side.1.side_ref, bf16[1024,3072]{1,0:T(8,128)(2,1)S(1)} %bitcast.8, ...), custom_call_target="tpu_custom_call" | custom-call | flops 1073741824 | bytes 8720384 | tf_op jit(solution)/shard_map/near/pallas_call | solution.py:46
  19.7 0.0 collective-permute-done.3.down_ref
  19.7 0.4 collective-permute-done.2.up_ref
  20.1 0.0 copy-done
  20.1 0.0 copy-done.2
  20.1 4.0 %last.1 = (bf16[128,1024]{1,0:T(8,128)(2,1)S(1)}, f32[128,128]{1,0:T(8,128)S(1)}, bf16[64,2,6,8,128]{4,3,2,1,0:T(8,128)(2,1)S(1)}) custom-call(bf16[128,1024]{1,0:T(8,128)(2,1)S(1)} %get-tuple-element.27.x_ref, bf16[64,1024]{1,0:T(8,128)(2,1)S(1)} %collective-permute-done.2.up_ref, bf16[64,1024]{1,0:T(8,128)(2,1)S(1)} %collective-permute-done.3.down_ref, ...), custom_call_target="tpu_custom_call" | custom-call | flops 805306368 | bytes 10915840 | tf_op jit(solution)/shard_map/last/pallas_call | solution.py:46
  24.1 0.0 copy-start.3
  24.1 0.0 copy-start.4
  24.1 0.0 copy-start.5
  24.2 32.1 %all_to_all.10.rows_ref = bf16[768,8,128]{2,1,0:T(8,128)(2,1)S(1)} all-to-all(bf16[768,8,128]{2,1,0:T(8,128)(2,1)S(1)} %bitcast.9), channel_id=1, replica_groups=mesh['lat'=8,'lon'=16] {'lat','lon'}, dimensions={0} | all-to-all | bytes 3145728 | tf_op jit(solution)/shard_map/all_to_all | solution.py:312
  56.3 0.0 copy-done.3
  56.3 0.0 copy-done.4
  56.3 0.0 copy-done.5
  56.3 2.6 %experts.1 = bf16[768,8,128]{2,1,0:T(8,128)(2,1)S(1)} custom-call(bf16[768,8,128]{2,1,0:T(8,128)(2,1)S(1)} %all_to_all.10.rows_ref, bf16[1024,512]{1,0:T(8,128)(2,1)S(1)} %copy-done.3, bf16[1024,512]{1,0:T(8,128)(2,1)S(1)} %copy-done.4, bf16[512,1024]{1,0:T(8,128)(2,1)S(1)} %copy-done.5), custom_call_target="tpu_custom_call" | custom-call | flops 4294967296 | bytes 4718592 | tf_op jit(solution)/shard_map/experts/pallas_call | solution.py:46
  58.9 28.4 %all_to_all.11.back_ref = bf16[768,8,128]{2,1,0:T(8,128)(2,1)S(1)} all-to-all(bf16[768,8,128]{2,1,0:T(8,128)(2,1)S(1)} %experts.1), channel_id=1, replica_groups=mesh['lat'=8,'lon'=16] {'lat','lon'}, dimensions={0} | all-to-all | bytes 3145728 | tf_op jit(solution)/shard_map/all_to_all | solution.py:316
  87.3 1.3 %combine.1 = bf16[128,1024]{1,0:T(8,128)(2,1)} custom-call(bf16[768,8,128]{2,1,0:T(8,128)(2,1)S(1)} %all_to_all.11.back_ref, bf16[256,768]{1,0:T(8,128)(2,1)S(1)} %get-tuple-element.44.pick_ref, f32[128,128]{1,0:T(8,128)S(1)} %get-tuple-element.45.gates_ref, bf16[128,1024]{1,0:T(8,128)(2,1)S(1)} %get-tuple-element.46.mixed_ref), custom_call_target="tpu_custom_call" | custom-call | flops 1073741824 | bytes 2293760 | tf_op jit(solution)/shard_map/combine/pallas_call | solution.py:46
  (2 shorter events, 0.0 us)
Async XLA Ops:
  0.0 0.9 %copy-start.1 = (bf16[8,16,1024]{2,1,0:T(8,128)(2,1)S(1)}, bf16[8,16,1024]{2,1,0:T(8,128)(2,1)}, u32[]{:S(2)}) copy-start(bf16[8,16,1024]{2,1,0:T(8,128)(2,1)} %param.9) | copy-start | bytes 786436
  1.0 11.1 %slice-start = ((s8[6291456]{0:T(1024)(128)(4,1)}), s8[4194304]{0:T(1024)(128)(4,1)S(1)}, s32[]{:S(2)}) async-start(s8[6291456]{0:T(1024)(128)(4,1)} %bitcast.7), calls=%async_computation.2 | async-start | bytes 8388608
  1.0 15.8 %collective-permute-start.5 = (bf16[128,1024]{1,0:T(8,128)(2,1)S(1)}, bf16[128,1024]{1,0:T(8,128)(2,1)S(1)}, u32[]{:S(2)}, u32[]{:S(2)}) collective-permute-start(bf16[128,1024]{1,0:T(8,128)(2,1)S(1)} %get-tuple-element.27.x_ref), channel_id=1, source_target_pairs={{0,112},{1,113},{2,114},{3,115},{4,116},{5,117},{6,118},{7,119},{8... | collective-permute-start | bytes 786440 | tf_op jit(solution)/shard_map/ppermute | solution.py:249
  2.4 14.4 %collective-permute-start.4 = (bf16[128,1024]{1,0:T(8,128)(2,1)S(1)}, bf16[128,1024]{1,0:T(8,128)(2,1)S(1)}, u32[]{:S(2)}, u32[]{:S(2)}) collective-permute-start(bf16[128,1024]{1,0:T(8,128)(2,1)S(1)} %get-tuple-element.27.x_ref), channel_id=1, source_target_pairs={{0,16},{1,17},{2,18},{3,19},{4,20},{5,21},{6,22},{7,23},{8,24},{9,... | collective-permute-start | bytes 786440 | tf_op jit(solution)/shard_map/ppermute | solution.py:249
  3.7 11.2 %collective-permute-start = (bf16[64,1024]{1,0:T(8,128)(2,1)S(1)}, bf16[64,1024]{1,0:T(8,128)(2,1)S(1)}, u32[]{:S(2)}, u32[]{:S(2)}) collective-permute-start(bf16[64,1024]{1,0:T(8,128)(2,1)S(1)} %get-tuple-element.28), channel_id=1, source_target_pairs={{0,1},{1,2},{2,3},{3,4},{4,5},{5,6},{6,7},{7,8},{8,9},{9,10},{10,1... | collective-permute-start | bytes 393224 | tf_op jit(solution)/shard_map/ppermute | solution.py:249
  4.9 7.1 %slice-start.1 = ((s8[6291456]{0:T(1024)(128)(4,1)}), s8[2097152]{0:T(1024)(128)(4,1)S(1)}, s32[]{:S(2)}) async-start(s8[6291456]{0:T(1024)(128)(4,1)} %bitcast.7), calls=%async_computation.3 | async-start | bytes 4194304
  4.9 10.0 %collective-permute-start.1 = (bf16[64,1024]{1,0:T(8,128)(2,1)S(1)}, bf16[64,1024]{1,0:T(8,128)(2,1)S(1)}, u32[]{:S(2)}, u32[]{:S(2)}) collective-permute-start(bf16[64,1024]{1,0:T(8,128)(2,1)S(1)} %get-tuple-element.29), channel_id=1, source_target_pairs={{0,15},{1,0},{2,1},{3,2},{4,3},{5,4},{6,5},{7,6},{8,7},{9,8},{10,9... | collective-permute-start | bytes 393224 | tf_op jit(solution)/shard_map/ppermute | solution.py:249
  9.7 0.7 copy-start.6
  10.4 0.7 copy-start.7
  15.0 4.6 %collective-permute-start.3 = (bf16[64,1024]{1,0:T(8,128)(2,1)S(1)}, bf16[64,1024]{1,0:T(8,128)(2,1)S(1)}, u32[]{:S(2)}, u32[]{:S(2)}) collective-permute-start(bf16[64,1024]{1,0:T(8,128)(2,1)S(1)} %side.1.side_ref), channel_id=1, source_target_pairs={{0,112},{1,113},{2,114},{3,115},{4,116},{5,117},{6,118},{7,119},{8... | collective-permute-start | bytes 393224 | tf_op jit(solution)/shard_map/ppermute | solution.py:249
  16.6 3.5 %collective-permute-start.2 = (bf16[64,1024]{1,0:T(8,128)(2,1)S(1)}, bf16[64,1024]{1,0:T(8,128)(2,1)S(1)}, u32[]{:S(2)}, u32[]{:S(2)}) collective-permute-start(bf16[64,1024]{1,0:T(8,128)(2,1)S(1)} %side.1.side_ref), channel_id=1, source_target_pairs={{0,16},{1,17},{2,18},{3,19},{4,20},{5,21},{6,22},{7,23},{8,24},{9,... | collective-permute-start | bytes 393224 | tf_op jit(solution)/shard_map/ppermute | solution.py:249
  16.8 3.3 %copy-start = (bf16[1024,1024]{1,0:T(8,128)(2,1)S(1)}, bf16[1024,1024]{1,0:T(8,128)(2,1)}, u32[]{:S(2)}) copy-start(bf16[1024,1024]{1,0:T(8,128)(2,1)} %wo_ref.1) | copy-start | bytes 6291460
  16.8 3.3 %copy-start.2 = (bf16[1024,64]{0,1:T(8,128)(2,1)S(1)}, bf16[1024,64]{0,1:T(8,128)(2,1)}, u32[]{:S(2)}) copy-start(bf16[1024,64]{0,1:T(8,128)(2,1)} %param.13) | copy-start | bytes 393220
  24.1 32.1 %copy-start.3 = (bf16[1024,512]{1,0:T(8,128)(2,1)S(1)}, bf16[1024,512]{1,0:T(8,128)(2,1)}, u32[]{:S(2)}) copy-start(bf16[1024,512]{1,0:T(8,128)(2,1)} %wg_ref.1) | copy-start | bytes 3145732
  24.1 32.1 %copy-start.4 = (bf16[1024,512]{1,0:T(8,128)(2,1)S(1)}, bf16[1024,512]{1,0:T(8,128)(2,1)}, u32[]{:S(2)}) copy-start(bf16[1024,512]{1,0:T(8,128)(2,1)} %wu_ref.1) | copy-start | bytes 3145732
  24.1 32.1 %copy-start.5 = (bf16[512,1024]{1,0:T(8,128)(2,1)S(1)}, bf16[512,1024]{1,0:T(8,128)(2,1)}, u32[]{:S(2)}) copy-start(bf16[512,1024]{1,0:T(8,128)(2,1)} %wd_ref.1) | copy-start | bytes 3145732

commit v4 on v3

--- a/solution.py
+++ b/solution.py
@@ -113,40 +113,46 @@
     mask_ref[n : 2 * n, :] = valid
 
 
-def attend_keys(queries, keys, values, mask):
-    n = queries.shape[0] // 2
+def blocks(width):
+    return [slice(i, i + width) for i in range(0, D, width)]
+
+
+def keys_values(x, w_ref):
+    keys = dot(x, w_ref[:, D : 2 * D]).astype(BF16).astype(F32)
+    values = dot(x, w_ref[:, 2 * D :]).astype(BF16)
+    return jnp.concatenate([head_norm(keys[:, lanes]) for lanes in blocks(BLK)], axis=1), values
+
+
+def attend_keys(queries_ref, keys, values, mask):
+    n = queries_ref.shape[0] // 2
     low_half = iota((1, 128), 1) < HEAD
-    weight = jnp.exp(contract_last(queries, keys)).astype(BF16) * mask
-    both = dot(weight, jnp.concatenate([values, jnp.ones_like(values)], axis=1))
-    return (
-        jnp.where(low_half, both[0:n, 0:128], both[n:, 0:128]),
-        jnp.where(low_half, both[0:n, 128:], both[n:, 128:]),
-    )
-
-
-def own_kernel(x_ref, w_ref, mask_ref, qq_ref, num_ref, den_ref):
+    pairs = blocks(128)
+    ones = jnp.ones((keys.shape[0], 128), BF16)
+    scores = [contract_last(queries_ref[:, lanes], keys[:, lanes]) for lanes in pairs]
+    weights = [jnp.exp(score).astype(BF16) * mask for score in scores]
+    sums = [
+        dot(weight, jnp.concatenate([values[:, lanes], ones], axis=1))
+        for weight, lanes in zip(weights, pairs, strict=True)
+    ]
+    return [
+        (
+            jnp.where(low_half, both[0:n, 0:128], both[n:, 0:128]),
+            jnp.where(low_half, both[0:n, 128:], both[n:, 128:]),
+        )
+        for both in sums
+    ]
+
+
+def own_kernel(x_ref, w_ref, qq_ref, k_ref, v_ref):
     n = x_ref.shape[0]
     x = rms(x_ref[...].astype(F32)).astype(BF16)
-    mask = mask_ref[:, 0:n]
-    low_half = iota((1, 128), 1) < HEAD
-    for i in range(D // BLK):
-        lanes = slice(i * BLK, (i + 1) * BLK)
-        q, k, v = [
-            dot(x, w_ref[:, part * D + i * BLK : part * D + (i + 1) * BLK]).astype(BF16)
-            for part in range(3)
-        ]
-        q = head_norm(q.astype(F32)).astype(F32) * 0.125
-        k = head_norm(k.astype(F32))
-        for pair in range(BLK // 128):
-            some = slice(pair * 128, (pair + 1) * 128)
-            qq = jnp.concatenate(
-                [jnp.where(low_half, q[:, some], 0.0), jnp.where(low_half, 0.0, q[:, some])], axis=0
-            ).astype(BF16)
-            num, den = attend_keys(qq, k[:, some], v[:, some], mask)
-            lanes = slice(i * BLK + pair * 128, i * BLK + (pair + 1) * 128)
-            qq_ref[:, lanes] = qq
-            num_ref[:, lanes] = num
-            den_ref[:, lanes] = den
+    queries = dot(x, w_ref[:, 0:D]).astype(BF16).astype(F32)
+    k_ref[...], v_ref[...] = keys_values(x, w_ref)
+    low_half = (iota((1, BLK), 1) & 127) < HEAD
+    for lanes in blocks(BLK):
+        q = head_norm(queries[:, lanes]).astype(F32) * 0.125
+        qq_ref[0:n, lanes] = jnp.where(low_half, q, 0.0).astype(BF16)
+        qq_ref[n:, lanes] = jnp.where(low_half, 0.0, q).astype(BF16)
 
 
 def side_kernel(left_ref, right_ref, cells_ref, side_ref):
@@ -157,7 +163,7 @@
 
 
 def near_kernel(
-    up_ref, down_ref, side_ref, w_ref, mask_ref, cells_ref, qq_ref, num_in, den_in, num_ref, den_ref
+    up_ref, down_ref, side_ref, w_ref, mask_ref, cells_ref, qq_ref, k_ref, v_ref, num_ref, den_ref
 ):
     n = up_ref.shape[0]
     past = cells_ref[:, 4:5] > 0.5
@@ -165,19 +171,13 @@
     x = jnp.concatenate(
         [rms(band).astype(BF16), rms(side_ref[...].astype(F32)).astype(BF16)], axis=0
     )
-    mask = mask_ref[:, n : n + x.shape[0]]
-    for i in range(D // BLK):
-        k, v = [
-            dot(x, w_ref[:, part * D + i * BLK : part * D + (i + 1) * BLK]).astype(BF16)
-            for part in (1, 2)
-        ]
-        k = head_norm(k.astype(F32))
-        for pair in range(BLK // 128):
-            some = slice(pair * 128, (pair + 1) * 128)
-            lanes = slice(i * BLK + pair * 128, i * BLK + (pair + 1) * 128)
-            num, den = attend_keys(qq_ref[:, lanes], k[:, some], v[:, some], mask)
-            num_ref[:, lanes] = num_in[:, lanes] + num
-            den_ref[:, lanes] = den_in[:, lanes] + den
+    keys, values = keys_values(x, w_ref)
+    keys = jnp.concatenate([k_ref[...], keys], axis=0)
+    values = jnp.concatenate([v_ref[...], values], axis=0)
+    sums = attend_keys(qq_ref, keys, values, mask_ref[:, 0 : keys.shape[0]])
+    for lanes, (num, den) in zip(blocks(128), sums, strict=True):
+        num_ref[:, lanes] = num
+        den_ref[:, lanes] = den
 
 
 def last_kernel(
@@ -188,23 +188,13 @@
     m = up_ref.shape[0]
     past = cells_ref[0:m, 6:7] > 0.5
     corner = jnp.where(past, up_ref[...].astype(F32), down_ref[...].astype(F32))
-    x = rms(corner).astype(BF16)
-    mask = mask_ref[:, 3 * n - m :]
-    total = None
-    for i in range(D // BLK):
-        k, v = [
-            dot(x, w_ref[:, part * D + i * BLK : part * D + (i + 1) * BLK]).astype(BF16)
-            for part in (1, 2)
-        ]
-        k = head_norm(k.astype(F32))
-        outs = []
-        for pair in range(BLK // 128):
-            some = slice(pair * 128, (pair + 1) * 128)
-            lanes = slice(i * BLK + pair * 128, i * BLK + (pair + 1) * 128)
-            num, den = attend_keys(qq_ref[:, lanes], k[:, some], v[:, some], mask)
-            outs.append(((num_ref[:, lanes] + num) / (den_ref[:, lanes] + den)).astype(BF16))
-        more = dot(jnp.concatenate(outs, axis=1), wo_ref[i * BLK : (i + 1) * BLK, :])
-        total = more if total is None else total + more
+    keys, values = keys_values(rms(corner).astype(BF16), w_ref)
+    sums = attend_keys(qq_ref, keys, values, mask_ref[:, 3 * n - m :])
+    attended = [
+        ((num_ref[:, lanes] + num) / (den_ref[:, lanes] + den)).astype(BF16)
+        for lanes, (num, den) in zip(blocks(128), sums, strict=True)
+    ]
+    total = dot(jnp.concatenate(attended, axis=1), wo_ref[...])
     mixed = (x_ref[...].astype(F32) + total).astype(BF16)
     mixed_ref[...] = mixed
     normed = rms(mixed.astype(F32)).astype(BF16)
@@ -255,17 +245,26 @@
     experts = router.shape[1]
     shape = jax.ShapeDtypeStruct
     half = shape((n // 2, width), BF16)
-    cells, ids, shifts = lax.optimization_barrier(
-        (tokens.reshape(n, width), expert_ids.reshape(n, 2).T, shifts)
-    )
     x, low, high = vmem_call(
-        split_kernel, "split", [shape((n, width), BF16), half, half], (cells,), 1 << 20
-    )
+        split_kernel,
+        "split",
+        [shape((n, width), BF16), half, half],
+        (tokens.reshape(n, width),),
+        3 << 30,
+    )
+    up = moved(x, 1, 0)
+    down = moved(x, -1, 0)
     left = moved(high, 0, 1)
     right = moved(low, 0, -1)
-    up = moved(x, 1, 0)
-    down = moved(x, -1, 0)
-    sums = [shape((n, width), F32)] * 2
+    whole = shape((n, width), BF16)
+    qq, keys, values = vmem_call(
+        own_kernel,
+        "own",
+        [shape((2 * n, width), BF16), whole, whole],
+        (x, w_qkv),
+        6 * n * width * width,
+    )
+    shifts, ids, keys = lax.optimization_barrier((shifts, expert_ids.reshape(n, 2).T, keys))
     pack, cells, mask, pick = vmem_call(
         functools.partial(plan_kernel, experts),
         "plan",
@@ -276,25 +275,17 @@
             shape((2 * n, 2 * MOST * experts), BF16),
         ],
         (shifts, ids),
-        3 << 30,
+        1 << 30,
         spaces={0: pltpu.SMEM},
     )
-    qq, num, den = vmem_call(
-        own_kernel,
-        "own",
-        [shape((2 * n, width), BF16), *sums],
-        (x, w_qkv, mask),
-        8 * n * width * width,
-    )
-    left, right, num = lax.optimization_barrier((left, right, num))
     side = vmem_call(side_kernel, "side", half, (left, right, cells), 1 << 10)
     up_side = moved(side, 1, 0)
     down_side = moved(side, -1, 0)
     num, den = vmem_call(
         near_kernel,
         "near",
-        sums,
-        (up, down, side, w_qkv, mask, cells, qq, num, den),
+        [shape((n, width), F32)] * 2,
+        (up, down, side, w_qkv, mask, cells, qq, keys, values),
         8 * n * width * width,
     )
     mixed, gates, send = vmem_call(

time: 88.8 us -> 87.4 us (0.984)
  Pallas kernels: 14.8 us -> 11.4 us
  blocking collectives: 60.5 us -> 63.2 us
  local copies, waits for them, and re-layouts: 2.32 us -> 1.14 us
    pallas_call x8, Pallas kernels: 14.8 us -> 11.4 us  [vmem_call(): pl.pallas_call(kernel, in_specs=specs, out_specs=outs, out_shape=out_shap...]
    all_to_all x1, blocking collectives: 32.1 us -> 34.8 us  [body(): lax.all_to_all(send, AXES, split_axis=0, concat_axis=0, tiled=True)]
    unnamed x20, local copies, waits for them, and re-layouts: 2.32 us -> 1.14 us
  transfers between devices with their start and end apart: 6 -> 6, of which waited for: 1 -> 2; matrix products, arithmetic and copies ran while one was open for 0% -> 0% of each run, Pallas kernels for 8% -> 6%
where the time goes in v4:
time: 87.4 us; the launch traced here: 87.3 us
  blocking collectives  63.2 us (72%)
  Pallas kernels  11.4 us (13%)
  starting transfers between devices  10.9 us (12%)
  local copies, waits for them, and re-layouts  1.14 us (1%)
    all_to_all x1, blocking collectives, body(): lax.all_to_all(send, AXES, split_axis=0, concat_axis=0, tiled=True)  34.8 us
    all_to_all x1, blocking collectives, body(): back = lax.all_to_all(part, AXES, split_axis=0, concat_axis=0, tiled=True)  28.4 us
    pallas_call x8, Pallas kernels, vmem_call(): pl.pallas_call(kernel, in_specs=specs, out_specs=outs, out_shape=out_shap...  11.4 us
    ppermute x6, starting transfers between devices, moved(): return lax.ppermute(x, AXES, pairs)  10.9 us
  transfers between devices with their start and end apart: 6, of which 2 were waited for; matrix products, arithmetic and copies ran while one was open for 0% of the time, Pallas kernels for 6%

profile of v4, /device:TPU:1, one launch (start us, length us, event | category | flops | bytes accessed | tf_op | source)
XLA Modules:
  0.0 87.3 jit_solution(16820037051564212745)
XLA Ops:
  0.0 0.0 slice-start
  0.0 0.0 copy-start.5
  0.0 1.1 %copy-done.5 = bf16[8,16,1024]{2,1,0:T(8,128)(2,1)S(1)} copy-done((bf16[8,16,1024]{2,1,0:T(8,128)(2,1)S(1)}, bf16[8,16,1024]{2,1,0:T(8,128)(2,1)}, u32[]{:S(2)}) %copy-start.5) | copy-done | bytes 262168
  1.1 0.0 slice-start.1
  1.1 1.4 %collective-permute-start.5 = (bf16[128,1024]{1,0:T(8,128)(2,1)S(1)}, bf16[128,1024]{1,0:T(8,128)(2,1)S(1)}, u32[]{:S(2)}, u32[]{:S(2)}) collective-permute-start(bf16[128,1024]{1,0:T(8,128)(2,1)S(1)} %get-tuple-element.23.x_ref), channel_id=1, source_target_pairs={{0,112},{1,113},{2,114},{3,115},{4,116},{5,117},{6,118},{7,119},{8... | collective-permute-start | bytes 786440 | tf_op jit(solution)/shard_map/ppermute | solution.py:239
  2.6 1.3 %collective-permute-start.4 = (bf16[128,1024]{1,0:T(8,128)(2,1)S(1)}, bf16[128,1024]{1,0:T(8,128)(2,1)S(1)}, u32[]{:S(2)}, u32[]{:S(2)}) collective-permute-start(bf16[128,1024]{1,0:T(8,128)(2,1)S(1)} %get-tuple-element.23.x_ref), channel_id=1, source_target_pairs={{0,16},{1,17},{2,18},{3,19},{4,20},{5,21},{6,22},{7,23},{8,24},{9,... | collective-permute-start | bytes 786440 | tf_op jit(solution)/shard_map/ppermute | solution.py:239
  3.9 1.2 %collective-permute-start = (bf16[64,1024]{1,0:T(8,128)(2,1)S(1)}, bf16[64,1024]{1,0:T(8,128)(2,1)S(1)}, u32[]{:S(2)}, u32[]{:S(2)}) collective-permute-start(bf16[64,1024]{1,0:T(8,128)(2,1)S(1)} %get-tuple-element.24), channel_id=1, source_target_pairs={{0,1},{1,2},{2,3},{3,4},{4,5},{5,6},{6,7},{7,8},{8,9},{9,10},{10,1... | collective-permute-start | bytes 393224 | tf_op jit(solution)/shard_map/ppermute | solution.py:239
  5.1 0.0 copy-start.6
  5.1 0.0 copy-start.7
  5.1 4.7 %collective-permute-start.1 = (bf16[64,1024]{1,0:T(8,128)(2,1)S(1)}, bf16[64,1024]{1,0:T(8,128)(2,1)S(1)}, u32[]{:S(2)}, u32[]{:S(2)}) collective-permute-start(bf16[64,1024]{1,0:T(8,128)(2,1)S(1)} %get-tuple-element.25), channel_id=1, source_target_pairs={{0,15},{1,0},{2,1},{3,2},{4,3},{5,4},{6,5},{7,6},{8,7},{9,8},{10,9... | collective-permute-start | bytes 393224 | tf_op jit(solution)/shard_map/ppermute | solution.py:239
  9.8 0.0 slice-done
  9.8 0.0 slice-done.1
  9.8 1.3 %own.1 = (bf16[256,1024]{1,0:T(8,128)(2,1)S(1)}, bf16[128,1024]{1,0:T(8,128)(2,1)S(1)}, bf16[128,1024]{1,0:T(8,128)(2,1)S(1)}) custom-call(bf16[128,1024]{1,0:T(8,128)(2,1)S(1)} %get-tuple-element.23.x_ref, bf16[1024,3072]{1,0:T(8,128)(2,1)S(1)} %bitcast.8), custom_call_target="tpu_custom_call" | custom-call | flops 805306368 | bytes 6553600 | tf_op jit(solution)/shard_map/own/pallas_call | solution.py:46
  11.2 0.0 copy-done.6
  11.2 0.0 copy-done.7
  11.2 1.0 %plan.1 = (bf16[384,128]{1,0:T(8,128)(2,1)S(1)}, f32[128,8]{1,0:T(8,128)S(1)}, bf16[256,384]{1,0:T(8,128)(2,1)S(1)}, bf16[256,768]{1,0:T(8,128)(2,1)S(1)}) custom-call(s32[2]{0:T(128)S(1)} %copy-done.7, s32[2,128]{1,0:T(2,128)S(1)} %bitcast.12), custom_call_target="tpu_custom_call" | custom-call | flops 1073741824 | bytes 1032 | tf_op jit(solution)/shard_map/plan/pallas_call | solution.py:46
  12.2 0.0 collective-permute-done.left_ref
  12.3 0.0 collective-permute-done.1.right_ref
  12.3 0.1 side.1.side_ref
  12.4 2.0 %collective-permute-start.3 = (bf16[64,1024]{1,0:T(8,128)(2,1)S(1)}, bf16[64,1024]{1,0:T(8,128)(2,1)S(1)}, u32[]{:S(2)}, u32[]{:S(2)}) collective-permute-start(bf16[64,1024]{1,0:T(8,128)(2,1)S(1)} %side.1.side_ref), channel_id=1, source_target_pairs={{0,112},{1,113},{2,114},{3,115},{4,116},{5,117},{6,118},{7,119},{8... | collective-permute-start | bytes 393224 | tf_op jit(solution)/shard_map/ppermute | solution.py:239
  14.4 0.2 collective-permute-start.2
  14.6 0.0 collective-permute-done.5.down_ref
  14.6 0.0 collective-permute-done.4.up_ref
  14.6 0.0 copy-start
  14.6 0.0 copy-start.1
  14.7 2.3 %near.1 = (f32[128,1024]{1,0:T(8,128)S(1)}, f32[128,1024]{1,0:T(8,128)S(1)}) custom-call(bf16[128,1024]{1,0:T(8,128)(2,1)S(1)} %collective-permute-done.4.up_ref, bf16[128,1024]{1,0:T(8,128)(2,1)S(1)} %collective-permute-done.5.down_ref, bf16[64,1024]{1,0:T(8,128)(2,1)S(1)} %side.1.side_ref, bf16[1024,3072]{1,0:T(8,128)(2,1)S(1)} %bitcast.8, ...), custom_call_target="tpu_custom_call" | custom-call | flops 1073741824 | bytes 8196096 | tf_op jit(solution)/shard_map/near/pallas_call | solution.py:46
  17.0 0.3 collective-permute-done.3.down_ref
  17.3 0.2 collective-permute-done.2.up_ref
  17.4 0.0 copy-done
  17.4 0.0 copy-done.1
  17.4 2.6 %last.1 = (bf16[128,1024]{1,0:T(8,128)(2,1)S(1)}, f32[128,128]{1,0:T(8,128)S(1)}, bf16[64,2,6,8,128]{4,3,2,1,0:T(8,128)(2,1)S(1)}) custom-call(bf16[128,1024]{1,0:T(8,128)(2,1)S(1)} %get-tuple-element.23.x_ref, bf16[64,1024]{1,0:T(8,128)(2,1)S(1)} %collective-permute-done.2.up_ref, bf16[64,1024]{1,0:T(8,128)(2,1)S(1)} %collective-permute-done.3.down_ref, ...), custom_call_target="tpu_custom_call" | custom-call | flops 805306368 | bytes 10915840 | tf_op jit(solution)/shard_map/last/pallas_call | solution.py:46
  20.1 0.0 copy-start.2
  20.1 0.0 copy-start.3
  20.1 0.0 copy-start.4
  20.1 34.8 %all_to_all.10.rows_ref = bf16[768,8,128]{2,1,0:T(8,128)(2,1)S(1)} all-to-all(bf16[768,8,128]{2,1,0:T(8,128)(2,1)S(1)} %bitcast.9), channel_id=1, replica_groups=mesh['lat'=8,'lon'=16] {'lat','lon'}, dimensions={0} | all-to-all | bytes 3145728 | tf_op jit(solution)/shard_map/all_to_all | solution.py:303
  54.9 0.0 copy-done.2
  54.9 0.0 copy-done.3
  54.9 0.0 copy-done.4
  54.9 2.6 %experts.1 = bf16[768,8,128]{2,1,0:T(8,128)(2,1)S(1)} custom-call(bf16[768,8,128]{2,1,0:T(8,128)(2,1)S(1)} %all_to_all.10.rows_ref, bf16[1024,512]{1,0:T(8,128)(2,1)S(1)} %copy-done.2, bf16[1024,512]{1,0:T(8,128)(2,1)S(1)} %copy-done.3, bf16[512,1024]{1,0:T(8,128)(2,1)S(1)} %copy-done.4), custom_call_target="tpu_custom_call" | custom-call | flops 4294967296 | bytes 4718592 | tf_op jit(solution)/shard_map/experts/pallas_call | solution.py:46
  57.5 28.4 %all_to_all.11.back_ref = bf16[768,8,128]{2,1,0:T(8,128)(2,1)S(1)} all-to-all(bf16[768,8,128]{2,1,0:T(8,128)(2,1)S(1)} %experts.1), channel_id=1, replica_groups=mesh['lat'=8,'lon'=16] {'lat','lon'}, dimensions={0} | all-to-all | bytes 3145728 | tf_op jit(solution)/shard_map/all_to_all | solution.py:307
  86.0 1.3 %combine.1 = bf16[128,1024]{1,0:T(8,128)(2,1)} custom-call(bf16[768,8,128]{2,1,0:T(8,128)(2,1)S(1)} %all_to_all.11.back_ref, bf16[256,768]{1,0:T(8,128)(2,1)S(1)} %get-tuple-element.38.pick_ref, f32[128,128]{1,0:T(8,128)S(1)} %get-tuple-element.39.gates_ref, bf16[128,1024]{1,0:T(8,128)(2,1)S(1)} %get-tuple-element.40.mixed_ref), custom_call_target="tpu_custom_call" | custom-call | flops 1073741824 | bytes 2293760 | tf_op jit(solution)/shard_map/combine/pallas_call | solution.py:46
  (2 shorter events, 0.0 us)
Async XLA Ops:
  0.0 9.8 %slice-start = ((s8[6291456]{0:T(1024)(128)(4,1)}), s8[4194304]{0:T(1024)(128)(4,1)S(1)}, s32[]{:S(2)}) async-start(s8[6291456]{0:T(1024)(128)(4,1)} %bitcast.7), calls=%async_computation.2 | async-start | bytes 8388608
  0.0 1.1 %copy-start.5 = (bf16[8,16,1024]{2,1,0:T(8,128)(2,1)S(1)}, bf16[8,16,1024]{2,1,0:T(8,128)(2,1)}, u32[]{:S(2)}) copy-start(bf16[8,16,1024]{2,1,0:T(8,128)(2,1)} %param.9) | copy-start | bytes 786436
  1.1 8.7 %slice-start.1 = ((s8[6291456]{0:T(1024)(128)(4,1)}), s8[2097152]{0:T(1024)(128)(4,1)S(1)}, s32[]{:S(2)}) async-start(s8[6291456]{0:T(1024)(128)(4,1)} %bitcast.7), calls=%async_computation.3 | async-start | bytes 4194304
  1.1 13.5 %collective-permute-start.5 = (bf16[128,1024]{1,0:T(8,128)(2,1)S(1)}, bf16[128,1024]{1,0:T(8,128)(2,1)S(1)}, u32[]{:S(2)}, u32[]{:S(2)}) collective-permute-start(bf16[128,1024]{1,0:T(8,128)(2,1)S(1)} %get-tuple-element.23.x_ref), channel_id=1, source_target_pairs={{0,112},{1,113},{2,114},{3,115},{4,116},{5,117},{6,118},{7,119},{8... | collective-permute-start | bytes 786440 | tf_op jit(solution)/shard_map/ppermute | solution.py:239
  2.6 12.1 %collective-permute-start.4 = (bf16[128,1024]{1,0:T(8,128)(2,1)S(1)}, bf16[128,1024]{1,0:T(8,128)(2,1)S(1)}, u32[]{:S(2)}, u32[]{:S(2)}) collective-permute-start(bf16[128,1024]{1,0:T(8,128)(2,1)S(1)} %get-tuple-element.23.x_ref), channel_id=1, source_target_pairs={{0,16},{1,17},{2,18},{3,19},{4,20},{5,21},{6,22},{7,23},{8,24},{9,... | collective-permute-start | bytes 786440 | tf_op jit(solution)/shard_map/ppermute | solution.py:239
  3.9 8.4 %collective-permute-start = (bf16[64,1024]{1,0:T(8,128)(2,1)S(1)}, bf16[64,1024]{1,0:T(8,128)(2,1)S(1)}, u32[]{:S(2)}, u32[]{:S(2)}) collective-permute-start(bf16[64,1024]{1,0:T(8,128)(2,1)S(1)} %get-tuple-element.24), channel_id=1, source_target_pairs={{0,1},{1,2},{2,3},{3,4},{4,5},{5,6},{6,7},{7,8},{8,9},{9,10},{10,1... | collective-permute-start | bytes 393224 | tf_op jit(solution)/shard_map/ppermute | solution.py:239
  5.1 6.1 %copy-start.6 = (s32[1,1,128,2]{2,3,1,0:T(2,128)S(1)}, s32[1,1,128,2]{2,3,1,0:T(2,128)}, u32[]{:S(2)}) copy-start(s32[1,1,128,2]{2,3,1,0:T(2,128)} %param.14) | copy-start | bytes 3076
  5.1 6.1 %copy-start.7 = (s32[2]{0:T(128)S(1)}, s32[2]{0:T(128)}, u32[]{:S(2)}) copy-start(s32[2]{0:T(128)} %shifts_ref) | copy-start | bytes 28
  5.1 7.2 %collective-permute-start.1 = (bf16[64,1024]{1,0:T(8,128)(2,1)S(1)}, bf16[64,1024]{1,0:T(8,128)(2,1)S(1)}, u32[]{:S(2)}, u32[]{:S(2)}) collective-permute-start(bf16[64,1024]{1,0:T(8,128)(2,1)S(1)} %get-tuple-element.25), channel_id=1, source_target_pairs={{0,15},{1,0},{2,1},{3,2},{4,3},{5,4},{6,5},{7,6},{8,7},{9,8},{10,9... | collective-permute-start | bytes 393224 | tf_op jit(solution)/shard_map/ppermute | solution.py:239
  12.4 4.9 %collective-permute-start.3 = (bf16[64,1024]{1,0:T(8,128)(2,1)S(1)}, bf16[64,1024]{1,0:T(8,128)(2,1)S(1)}, u32[]{:S(2)}, u32[]{:S(2)}) collective-permute-start(bf16[64,1024]{1,0:T(8,128)(2,1)S(1)} %side.1.side_ref), channel_id=1, source_target_pairs={{0,112},{1,113},{2,114},{3,115},{4,116},{5,117},{6,118},{7,119},{8... | collective-permute-start | bytes 393224 | tf_op jit(solution)/shard_map/ppermute | solution.py:239
  14.4 3.0 %collective-permute-start.2 = (bf16[64,1024]{1,0:T(8,128)(2,1)S(1)}, bf16[64,1024]{1,0:T(8,128)(2,1)S(1)}, u32[]{:S(2)}, u32[]{:S(2)}) collective-permute-start(bf16[64,1024]{1,0:T(8,128)(2,1)S(1)} %side.1.side_ref), channel_id=1, source_target_pairs={{0,16},{1,17},{2,18},{3,19},{4,20},{5,21},{6,22},{7,23},{8,24},{9,... | collective-permute-start | bytes 393224 | tf_op jit(solution)/shard_map/ppermute | solution.py:239
  14.6 2.8 %copy-start = (bf16[1024,1024]{1,0:T(8,128)(2,1)S(1)}, bf16[1024,1024]{1,0:T(8,128)(2,1)}, u32[]{:S(2)}) copy-start(bf16[1024,1024]{1,0:T(8,128)(2,1)} %wo_ref.1) | copy-start | bytes 6291460
  14.6 2.8 %copy-start.1 = (bf16[1024,64]{0,1:T(8,128)(2,1)S(1)}, bf16[1024,64]{0,1:T(8,128)(2,1)}, u32[]{:S(2)}) copy-start(bf16[1024,64]{0,1:T(8,128)(2,1)} %param.13) | copy-start | bytes 393220
  20.1 34.8 %copy-start.2 = (bf16[1024,512]{1,0:T(8,128)(2,1)S(1)}, bf16[1024,512]{1,0:T(8,128)(2,1)}, u32[]{:S(2)}) copy-start(bf16[1024,512]{1,0:T(8,128)(2,1)} %wg_ref.1) | copy-start | bytes 3145732
  20.1 34.8 %copy-start.3 = (bf16[1024,512]{1,0:T(8,128)(2,1)S(1)}, bf16[1024,512]{1,0:T(8,128)(2,1)}, u32[]{:S(2)}) copy-start(bf16[1024,512]{1,0:T(8,128)(2,1)} %wu_ref.1) | copy-start | bytes 3145732
  20.1 34.8 %copy-start.4 = (bf16[512,1024]{1,0:T(8,128)(2,1)S(1)}, bf16[512,1024]{1,0:T(8,128)(2,1)}, u32[]{:S(2)}) copy-start(bf16[512,1024]{1,0:T(8,128)(2,1)} %wd_ref.1) | copy-start | bytes 3145732

commit v5 on v4

--- a/solution.py
+++ b/solution.py
@@ -59,9 +59,11 @@
     return lax.dot_general(a, b, (((1,), (1,)), ((), ())), preferred_element_type=F32)
 
 
-def split_kernel(tokens_ref, x_ref, low_ref, high_ref):
+def split_kernel(tokens_ref, x_ref, low_ref, high_ref, up_ref, down_ref):
     x = tokens_ref[...]
     x_ref[...] = x
+    up_ref[...] = x
+    down_ref[...] = x
     halves = x.astype(F32).reshape(-1, 2, WIN, D)
     low_ref[...] = halves[:, 0].reshape(-1, D).astype(BF16)
     high_ref[...] = halves[:, 1].reshape(-1, D).astype(BF16)
@@ -245,15 +247,15 @@
     experts = router.shape[1]
     shape = jax.ShapeDtypeStruct
     half = shape((n // 2, width), BF16)
-    x, low, high = vmem_call(
+    x, low, high, for_up, for_down = vmem_call(
         split_kernel,
         "split",
-        [shape((n, width), BF16), half, half],
+        [shape((n, width), BF16), half, half, *[shape((n, width), BF16)] * 2],
         (tokens.reshape(n, width),),
         3 << 30,
     )
-    up = moved(x, 1, 0)
-    down = moved(x, -1, 0)
+    up = moved(for_up, 1, 0)
+    down = moved(for_down, -1, 0)
     left = moved(high, 0, 1)
     right = moved(low, 0, -1)
     whole = shape((n, width), BF16)

time: 87.4 us -> 86.3 us (0.987)
  blocking collectives: 63.2 us -> 61.3 us
  starting transfers between devices: 10.9 us -> 11.9 us
    all_to_all x1, blocking collectives: 34.8 us -> 32.9 us  [body(): lax.all_to_all(send, AXES, split_axis=0, concat_axis=0, tiled=True)]
    ppermute x6, starting transfers between devices: 10.9 us -> 11.9 us  [moved(): return lax.ppermute(x, AXES, pairs)]
  transfers between devices with their start and end apart: 6 -> 6, of which waited for: 2 -> 1; matrix products, arithmetic and copies ran while one was open for 0% -> 0% of each run, Pallas kernels for 6% -> 6%
where the time goes in v5:
time: 86.3 us; the launch traced here: 86.1 us
  blocking collectives  61.3 us (71%)
  starting transfers between devices  11.9 us (14%)
  Pallas kernels  11.4 us (13%)
  local copies, waits for them, and re-layouts  1.15 us (1%)
    all_to_all x1, blocking collectives, body(): lax.all_to_all(send, AXES, split_axis=0, concat_axis=0, tiled=True)  32.9 us
    all_to_all x1, blocking collectives, body(): back = lax.all_to_all(part, AXES, split_axis=0, concat_axis=0, tiled=True)  28.4 us
    ppermute x6, starting transfers between devices, moved(): return lax.ppermute(x, AXES, pairs)  11.9 us
    pallas_call x8, Pallas kernels, vmem_call(): pl.pallas_call(kernel, in_specs=specs, out_specs=outs, out_shape=out_shap...  11.4 us
  transfers between devices with their start and end apart: 6, of which 1 were waited for; matrix products, arithmetic and copies ran while one was open for 0% of the time, Pallas kernels for 6%

profile of v5, /device:TPU:1, one launch (start us, length us, event | category | flops | bytes accessed | tf_op | source)
XLA Modules:
  0.0 86.1 jit_solution(17738726621679695803)
XLA Ops:
  0.0 0.0 slice-start
  0.0 0.0 copy-start.5
  0.0 1.1 %copy-done.5 = bf16[8,16,1024]{2,1,0:T(8,128)(2,1)S(1)} copy-done((bf16[8,16,1024]{2,1,0:T(8,128)(2,1)S(1)}, bf16[8,16,1024]{2,1,0:T(8,128)(2,1)}, u32[]{:S(2)}) %copy-start.5) | copy-done | bytes 262168
  1.1 0.0 slice-start.1
  1.1 0.1 split.1
  1.2 2.7 %collective-permute-start.4 = (bf16[128,1024]{1,0:T(8,128)(2,1)S(1)}, bf16[128,1024]{1,0:T(8,128)(2,1)S(1)}, u32[]{:S(2)}, u32[]{:S(2)}) collective-permute-start(bf16[128,1024]{1,0:T(8,128)(2,1)S(1)} %get-tuple-element.34), channel_id=1, source_target_pairs={{0,16},{1,17},{2,18},{3,19},{4,20},{5,21},{6,22},{7,23},{8,24},{9,... | collective-permute-start | bytes 786440 | tf_op jit(solution)/shard_map/ppermute | solution.py:241
  3.9 0.0 collective-permute-start.5
  3.9 1.2 %collective-permute-start = (bf16[64,1024]{1,0:T(8,128)(2,1)S(1)}, bf16[64,1024]{1,0:T(8,128)(2,1)S(1)}, u32[]{:S(2)}, u32[]{:S(2)}) collective-permute-start(bf16[64,1024]{1,0:T(8,128)(2,1)S(1)} %get-tuple-element.26), channel_id=1, source_target_pairs={{0,1},{1,2},{2,3},{3,4},{4,5},{5,6},{6,7},{7,8},{8,9},{9,10},{10,1... | collective-permute-start | bytes 393224 | tf_op jit(solution)/shard_map/ppermute | solution.py:241
  5.1 4.7 %collective-permute-start.1 = (bf16[64,1024]{1,0:T(8,128)(2,1)S(1)}, bf16[64,1024]{1,0:T(8,128)(2,1)S(1)}, u32[]{:S(2)}, u32[]{:S(2)}) collective-permute-start(bf16[64,1024]{1,0:T(8,128)(2,1)S(1)} %get-tuple-element.27), channel_id=1, source_target_pairs={{0,15},{1,0},{2,1},{3,2},{4,3},{5,4},{6,5},{7,6},{8,7},{9,8},{10,9... | collective-permute-start | bytes 393224 | tf_op jit(solution)/shard_map/ppermute | solution.py:241
  9.8 0.0 slice-done
  9.8 0.0 slice-done.1
  9.8 0.0 copy-start.6
  9.8 0.0 copy-start.7
  9.9 1.3 %own.1 = (bf16[256,1024]{1,0:T(8,128)(2,1)S(1)}, bf16[128,1024]{1,0:T(8,128)(2,1)S(1)}, bf16[128,1024]{1,0:T(8,128)(2,1)S(1)}) custom-call(bf16[128,1024]{1,0:T(8,128)(2,1)S(1)} %get-tuple-element.25.x_ref, bf16[1024,3072]{1,0:T(8,128)(2,1)S(1)} %bitcast.8), custom_call_target="tpu_custom_call" | custom-call | flops 805306368 | bytes 6553600 | tf_op jit(solution)/shard_map/own/pallas_call | solution.py:46
  11.2 0.0 copy-done.6
  11.2 0.0 copy-done.7
  11.2 1.0 %plan.1 = (bf16[384,128]{1,0:T(8,128)(2,1)S(1)}, f32[128,8]{1,0:T(8,128)S(1)}, bf16[256,384]{1,0:T(8,128)(2,1)S(1)}, bf16[256,768]{1,0:T(8,128)(2,1)S(1)}) custom-call(s32[2]{0:T(128)S(1)} %copy-done.7, s32[2,128]{1,0:T(2,128)S(1)} %bitcast.12), custom_call_target="tpu_custom_call" | custom-call | flops 1073741824 | bytes 1032 | tf_op jit(solution)/shard_map/plan/pallas_call | solution.py:46
  12.3 0.0 collective-permute-done.left_ref
  12.3 0.0 collective-permute-done.1.right_ref
  12.3 0.1 side.1.side_ref
  12.4 2.5 %collective-permute-start.3 = (bf16[64,1024]{1,0:T(8,128)(2,1)S(1)}, bf16[64,1024]{1,0:T(8,128)(2,1)S(1)}, u32[]{:S(2)}, u32[]{:S(2)}) collective-permute-start(bf16[64,1024]{1,0:T(8,128)(2,1)S(1)} %side.1.side_ref), channel_id=1, source_target_pairs={{0,112},{1,113},{2,114},{3,115},{4,116},{5,117},{6,118},{7,119},{8... | collective-permute-start | bytes 393224 | tf_op jit(solution)/shard_map/ppermute | solution.py:241
  14.9 0.7 collective-permute-start.2
  15.6 0.0 collective-permute-done.4.up_ref
  15.6 0.0 collective-permute-done.5.down_ref
  15.6 0.0 copy-start
  15.6 0.0 copy-start.1
  15.6 2.3 %near.1 = (f32[128,1024]{1,0:T(8,128)S(1)}, f32[128,1024]{1,0:T(8,128)S(1)}) custom-call(bf16[128,1024]{1,0:T(8,128)(2,1)S(1)} %collective-permute-done.4.up_ref, bf16[128,1024]{1,0:T(8,128)(2,1)S(1)} %collective-permute-done.5.down_ref, bf16[64,1024]{1,0:T(8,128)(2,1)S(1)} %side.1.side_ref, bf16[1024,3072]{1,0:T(8,128)(2,1)S(1)} %bitcast.8, ...), custom_call_target="tpu_custom_call" | custom-call | flops 1073741824 | bytes 8196096 | tf_op jit(solution)/shard_map/near/pallas_call | solution.py:46
  18.0 0.3 collective-permute-done.3.down_ref
  18.2 0.0 collective-permute-done.2.up_ref
  18.2 0.0 copy-done
  18.2 0.0 copy-done.1
  18.2 2.6 %last.1 = (bf16[128,1024]{1,0:T(8,128)(2,1)S(1)}, f32[128,128]{1,0:T(8,128)S(1)}, bf16[64,2,6,8,128]{4,3,2,1,0:T(8,128)(2,1)S(1)}) custom-call(bf16[128,1024]{1,0:T(8,128)(2,1)S(1)} %get-tuple-element.25.x_ref, bf16[64,1024]{1,0:T(8,128)(2,1)S(1)} %collective-permute-done.2.up_ref, bf16[64,1024]{1,0:T(8,128)(2,1)S(1)} %collective-permute-done.3.down_ref, ...), custom_call_target="tpu_custom_call" | custom-call | flops 805306368 | bytes 10915840 | tf_op jit(solution)/shard_map/last/pallas_call | solution.py:46
  20.9 0.0 copy-start.2
  20.9 0.0 copy-start.3
  20.9 0.0 copy-start.4
  20.9 32.9 %all_to_all.10.rows_ref = bf16[768,8,128]{2,1,0:T(8,128)(2,1)S(1)} all-to-all(bf16[768,8,128]{2,1,0:T(8,128)(2,1)S(1)} %bitcast.9), channel_id=1, replica_groups=mesh['lat'=8,'lon'=16] {'lat','lon'}, dimensions={0} | all-to-all | bytes 3145728 | tf_op jit(solution)/shard_map/all_to_all | solution.py:305
  53.8 0.0 copy-done.2
  53.8 0.0 copy-done.3
  53.8 0.0 copy-done.4
  53.8 2.6 %experts.1 = bf16[768,8,128]{2,1,0:T(8,128)(2,1)S(1)} custom-call(bf16[768,8,128]{2,1,0:T(8,128)(2,1)S(1)} %all_to_all.10.rows_ref, bf16[1024,512]{1,0:T(8,128)(2,1)S(1)} %copy-done.2, bf16[1024,512]{1,0:T(8,128)(2,1)S(1)} %copy-done.3, bf16[512,1024]{1,0:T(8,128)(2,1)S(1)} %copy-done.4), custom_call_target="tpu_custom_call" | custom-call | flops 4294967296 | bytes 4718592 | tf_op jit(solution)/shard_map/experts/pallas_call | solution.py:46
  56.4 28.4 %all_to_all.11.back_ref = bf16[768,8,128]{2,1,0:T(8,128)(2,1)S(1)} all-to-all(bf16[768,8,128]{2,1,0:T(8,128)(2,1)S(1)} %experts.1), channel_id=1, replica_groups=mesh['lat'=8,'lon'=16] {'lat','lon'}, dimensions={0} | all-to-all | bytes 3145728 | tf_op jit(solution)/shard_map/all_to_all | solution.py:309
  84.8 1.3 %combine.1 = bf16[128,1024]{1,0:T(8,128)(2,1)} custom-call(bf16[768,8,128]{2,1,0:T(8,128)(2,1)S(1)} %all_to_all.11.back_ref, bf16[256,768]{1,0:T(8,128)(2,1)S(1)} %get-tuple-element.42.pick_ref, f32[128,128]{1,0:T(8,128)S(1)} %get-tuple-element.43.gates_ref, bf16[128,1024]{1,0:T(8,128)(2,1)S(1)} %get-tuple-element.44.mixed_ref), custom_call_target="tpu_custom_call" | custom-call | flops 1073741824 | bytes 2293760 | tf_op jit(solution)/shard_map/combine/pallas_call | solution.py:46
  (1 shorter events, 0.0 us)
Async XLA Ops:
  0.0 9.8 %slice-start = ((s8[6291456]{0:T(1024)(128)(4,1)}), s8[4194304]{0:T(1024)(128)(4,1)S(1)}, s32[]{:S(2)}) async-start(s8[6291456]{0:T(1024)(128)(4,1)} %bitcast.7), calls=%async_computation.2 | async-start | bytes 8388608
  0.0 1.1 %copy-start.5 = (bf16[8,16,1024]{2,1,0:T(8,128)(2,1)S(1)}, bf16[8,16,1024]{2,1,0:T(8,128)(2,1)}, u32[]{:S(2)}) copy-start(bf16[8,16,1024]{2,1,0:T(8,128)(2,1)} %param.9) | copy-start | bytes 786436
  1.1 8.7 %slice-start.1 = ((s8[6291456]{0:T(1024)(128)(4,1)}), s8[2097152]{0:T(1024)(128)(4,1)S(1)}, s32[]{:S(2)}) async-start(s8[6291456]{0:T(1024)(128)(4,1)} %bitcast.7), calls=%async_computation.3 | async-start | bytes 4194304
  1.2 14.4 %collective-permute-start.4 = (bf16[128,1024]{1,0:T(8,128)(2,1)S(1)}, bf16[128,1024]{1,0:T(8,128)(2,1)S(1)}, u32[]{:S(2)}, u32[]{:S(2)}) collective-permute-start(bf16[128,1024]{1,0:T(8,128)(2,1)S(1)} %get-tuple-element.34), channel_id=1, source_target_pairs={{0,16},{1,17},{2,18},{3,19},{4,20},{5,21},{6,22},{7,23},{8,24},{9,... | collective-permute-start | bytes 786440 | tf_op jit(solution)/shard_map/ppermute | solution.py:241
  3.9 11.7 %collective-permute-start.5 = (bf16[128,1024]{1,0:T(8,128)(2,1)S(1)}, bf16[128,1024]{1,0:T(8,128)(2,1)S(1)}, u32[]{:S(2)}, u32[]{:S(2)}) collective-permute-start(bf16[128,1024]{1,0:T(8,128)(2,1)S(1)} %get-tuple-element.35), channel_id=1, source_target_pairs={{0,112},{1,113},{2,114},{3,115},{4,116},{5,117},{6,118},{7,119},{8... | collective-permute-start | bytes 786440 | tf_op jit(solution)/shard_map/ppermute | solution.py:241
  3.9 8.4 %collective-permute-start = (bf16[64,1024]{1,0:T(8,128)(2,1)S(1)}, bf16[64,1024]{1,0:T(8,128)(2,1)S(1)}, u32[]{:S(2)}, u32[]{:S(2)}) collective-permute-start(bf16[64,1024]{1,0:T(8,128)(2,1)S(1)} %get-tuple-element.26), channel_id=1, source_target_pairs={{0,1},{1,2},{2,3},{3,4},{4,5},{5,6},{6,7},{7,8},{8,9},{9,10},{10,1... | collective-permute-start | bytes 393224 | tf_op jit(solution)/shard_map/ppermute | solution.py:241
  5.1 7.2 %collective-permute-start.1 = (bf16[64,1024]{1,0:T(8,128)(2,1)S(1)}, bf16[64,1024]{1,0:T(8,128)(2,1)S(1)}, u32[]{:S(2)}, u32[]{:S(2)}) collective-permute-start(bf16[64,1024]{1,0:T(8,128)(2,1)S(1)} %get-tuple-element.27), channel_id=1, source_target_pairs={{0,15},{1,0},{2,1},{3,2},{4,3},{5,4},{6,5},{7,6},{8,7},{9,8},{10,9... | collective-permute-start | bytes 393224 | tf_op jit(solution)/shard_map/ppermute | solution.py:241
  9.8 1.4 %copy-start.6 = (s32[1,1,128,2]{2,3,1,0:T(2,128)S(1)}, s32[1,1,128,2]{2,3,1,0:T(2,128)}, u32[]{:S(2)}) copy-start(s32[1,1,128,2]{2,3,1,0:T(2,128)} %param.14) | copy-start | bytes 3076
  9.8 1.4 %copy-start.7 = (s32[2]{0:T(128)S(1)}, s32[2]{0:T(128)}, u32[]{:S(2)}) copy-start(s32[2]{0:T(128)} %shifts_ref) | copy-start | bytes 28
  12.4 5.8 %collective-permute-start.3 = (bf16[64,1024]{1,0:T(8,128)(2,1)S(1)}, bf16[64,1024]{1,0:T(8,128)(2,1)S(1)}, u32[]{:S(2)}, u32[]{:S(2)}) collective-permute-start(bf16[64,1024]{1,0:T(8,128)(2,1)S(1)} %side.1.side_ref), channel_id=1, source_target_pairs={{0,112},{1,113},{2,114},{3,115},{4,116},{5,117},{6,118},{7,119},{8... | collective-permute-start | bytes 393224 | tf_op jit(solution)/shard_map/ppermute | solution.py:241
  14.9 3.3 %collective-permute-start.2 = (bf16[64,1024]{1,0:T(8,128)(2,1)S(1)}, bf16[64,1024]{1,0:T(8,128)(2,1)S(1)}, u32[]{:S(2)}, u32[]{:S(2)}) collective-permute-start(bf16[64,1024]{1,0:T(8,128)(2,1)S(1)} %side.1.side_ref), channel_id=1, source_target_pairs={{0,16},{1,17},{2,18},{3,19},{4,20},{5,21},{6,22},{7,23},{8,24},{9,... | collective-permute-start | bytes 393224 | tf_op jit(solution)/shard_map/ppermute | solution.py:241
  15.6 2.6 %copy-start = (bf16[1024,1024]{1,0:T(8,128)(2,1)S(1)}, bf16[1024,1024]{1,0:T(8,128)(2,1)}, u32[]{:S(2)}) copy-start(bf16[1024,1024]{1,0:T(8,128)(2,1)} %wo_ref.1) | copy-start | bytes 6291460
  15.6 2.6 %copy-start.1 = (bf16[1024,64]{0,1:T(8,128)(2,1)S(1)}, bf16[1024,64]{0,1:T(8,128)(2,1)}, u32[]{:S(2)}) copy-start(bf16[1024,64]{0,1:T(8,128)(2,1)} %param.13) | copy-start | bytes 393220
  20.9 32.9 %copy-start.2 = (bf16[1024,512]{1,0:T(8,128)(2,1)S(1)}, bf16[1024,512]{1,0:T(8,128)(2,1)}, u32[]{:S(2)}) copy-start(bf16[1024,512]{1,0:T(8,128)(2,1)} %wg_ref.1) | copy-start | bytes 3145732
  20.9 32.9 %copy-start.3 = (bf16[1024,512]{1,0:T(8,128)(2,1)S(1)}, bf16[1024,512]{1,0:T(8,128)(2,1)}, u32[]{:S(2)}) copy-start(bf16[1024,512]{1,0:T(8,128)(2,1)} %wu_ref.1) | copy-start | bytes 3145732
  20.9 32.9 %copy-start.4 = (bf16[512,1024]{1,0:T(8,128)(2,1)S(1)}, bf16[512,1024]{1,0:T(8,128)(2,1)}, u32[]{:S(2)}) copy-start(bf16[512,1024]{1,0:T(8,128)(2,1)} %wd_ref.1) | copy-start | bytes 3145732

commit v6 on v5

--- a/solution.py
+++ b/solution.py
@@ -59,10 +59,9 @@
     return lax.dot_general(a, b, (((1,), (1,)), ((), ())), preferred_element_type=F32)
 
 
-def split_kernel(tokens_ref, x_ref, low_ref, high_ref, up_ref, down_ref):
+def split_kernel(tokens_ref, x_ref, low_ref, high_ref, down_ref):
     x = tokens_ref[...]
     x_ref[...] = x
-    up_ref[...] = x
     down_ref[...] = x
     halves = x.astype(F32).reshape(-1, 2, WIN, D)
     low_ref[...] = halves[:, 0].reshape(-1, D).astype(BF16)
@@ -125,12 +124,19 @@
     return jnp.concatenate([head_norm(keys[:, lanes]) for lanes in blocks(BLK)], axis=1), values
 
 
-def attend_keys(queries_ref, keys, values, mask):
+def attend_keys(queries_ref, keys, values, mask, scale=None):
     n = queries_ref.shape[0] // 2
     low_half = iota((1, 128), 1) < HEAD
     pairs = blocks(128)
     ones = jnp.ones((keys.shape[0], 128), BF16)
     scores = [contract_last(queries_ref[:, lanes], keys[:, lanes]) for lanes in pairs]
+    if scale is not None:
+        scores = [
+            jnp.concatenate(
+                [score[0:n] * scale[2 * i : 2 * i + 1], score[n:] * scale[2 * i + 1 : 2 * i + 2]], axis=0
+            )
+            for i, score in enumerate(scores)
+        ]
     weights = [jnp.exp(score).astype(BF16) * mask for score in scores]
     sums = [
         dot(weight, jnp.concatenate([values[:, lanes], ones], axis=1))
@@ -190,8 +196,14 @@
     m = up_ref.shape[0]
     past = cells_ref[0:m, 6:7] > 0.5
     corner = jnp.where(past, up_ref[...].astype(F32), down_ref[...].astype(F32))
-    keys, values = keys_values(rms(corner).astype(BF16), w_ref)
-    sums = attend_keys(qq_ref, keys, values, mask_ref[:, 3 * n - m :])
+    x = rms(corner).astype(BF16)
+    keys = dot(x, w_ref[:, D : 2 * D]).astype(BF16)
+    values = dot(x, w_ref[:, 2 * D :]).astype(BF16)
+    heads = D // HEAD
+    head = jnp.where(iota((heads, D), 0) == iota((heads, D), 1) // HEAD, 1.0, 0.0).astype(BF16)
+    square = keys.astype(F32) * keys.astype(F32)
+    scale = lax.rsqrt(contract_last(head, square.astype(BF16)) * (1.0 / HEAD) + 1e-05)
+    sums = attend_keys(qq_ref, keys, values, mask_ref[:, 3 * n - m :], scale)
     attended = [
         ((num_ref[:, lanes] + num) / (den_ref[:, lanes] + den)).astype(BF16)
         for lanes, (num, den) in zip(blocks(128), sums, strict=True)
@@ -247,17 +259,18 @@
     experts = router.shape[1]
     shape = jax.ShapeDtypeStruct
     half = shape((n // 2, width), BF16)
-    x, low, high, for_up, for_down = vmem_call(
+    x, low, high, for_down = vmem_call(
         split_kernel,
         "split",
-        [shape((n, width), BF16), half, half, *[shape((n, width), BF16)] * 2],
+        [shape((n, width), BF16), half, half, shape((n, width), BF16)],
         (tokens.reshape(n, width),),
         3 << 30,
     )
-    up = moved(for_up, 1, 0)
-    down = moved(for_down, -1, 0)
     left = moved(high, 0, 1)
     right = moved(low, 0, -1)
+    later, _, _ = lax.optimization_barrier((tokens.reshape(n, width), high, low))
+    up = moved(later, 1, 0)
+    down = moved(for_down, -1, 0)
     whole = shape((n, width), BF16)
     qq, keys, values = vmem_call(
         own_kernel,

time: 86.3 us -> 86.2 us (level)
  local copies, waits for them, and re-layouts: 1.15 us -> 0.05 us
  Pallas kernels: 11.4 us -> 12.4 us
    unnamed x20 -> x18, local copies, waits for them, and re-layouts: 1.15 us -> 0.05 us
    pallas_call x8, Pallas kernels: 11.4 us -> 12.4 us  [vmem_call(): pl.pallas_call(kernel, in_specs=specs, out_specs=outs, out_shape=out_shap...]
where the time goes in v6:
time: 86.2 us; the launch traced here: 86 us
  blocking collectives  61.3 us (71%)
  Pallas kernels  12.4 us (14%)
  starting transfers between devices  11.9 us (14%)
    all_to_all x1, blocking collectives, body(): lax.all_to_all(send, AXES, split_axis=0, concat_axis=0, tiled=True)  32.9 us
    all_to_all x1, blocking collectives, body(): back = lax.all_to_all(part, AXES, split_axis=0, concat_axis=0, tiled=True)  28.4 us
    pallas_call x8, Pallas kernels, vmem_call(): pl.pallas_call(kernel, in_specs=specs, out_specs=outs, out_shape=out_shap...  12.4 us
    ppermute x6, starting transfers between devices, moved(): return lax.ppermute(x, AXES, pairs)  11.9 us
  transfers between devices with their start and end apart: 6, of which 1 were waited for; matrix products, arithmetic and copies ran while one was open for 0% of the time, Pallas kernels for 6%

profile of v6, /device:TPU:1, one launch (start us, length us, event | category | flops | bytes accessed | tf_op | source)
XLA Modules:
  0.0 86.0 jit_solution(2493571916300548933)
XLA Ops:
  0.0 0.0 slice-start
  0.0 0.0 slice-start.1
  0.0 1.2 %split.1 = (bf16[128,1024]{1,0:T(8,128)(2,1)S(1)}, bf16[64,1024]{1,0:T(8,128)(2,1)S(1)}, bf16[64,1024]{1,0:T(8,128)(2,1)S(1)}, bf16[128,1024]{1,0:T(8,128)(2,1)S(1)}) custom-call(bf16[128,1024]{1,0:T(8,128)(2,1)} %bitcast.tokens_ref), custom_call_target="tpu_custom_call" | custom-call | flops 3221225472 | bytes 262144 | tf_op jit(solution)/shard_map/split/pallas_call | solution.py:46
  1.2 2.7 %collective-permute-start.4 = (bf16[128,1024]{1,0:T(8,128)(2,1)}, bf16[128,1024]{1,0:T(8,128)(2,1)S(1)}, u32[]{:S(2)}, u32[]{:S(2)}) collective-permute-start(bf16[128,1024]{1,0:T(8,128)(2,1)} %bitcast.tokens_ref), channel_id=1, source_target_pairs={{0,16},{1,17},{2,18},{3,19},{4,20},{5,21},{6,22},{7,23},{8,24},{9,... | collective-permute-start | bytes 786440 | tf_op jit(solution)/shard_map/ppermute | solution.py:253
  3.9 0.0 collective-permute-start.5
  3.9 1.2 %collective-permute-start = (bf16[64,1024]{1,0:T(8,128)(2,1)S(1)}, bf16[64,1024]{1,0:T(8,128)(2,1)S(1)}, u32[]{:S(2)}, u32[]{:S(2)}) collective-permute-start(bf16[64,1024]{1,0:T(8,128)(2,1)S(1)} %get-tuple-element.26), channel_id=1, source_target_pairs={{0,1},{1,2},{2,3},{3,4},{4,5},{5,6},{6,7},{7,8},{8,9},{9,10},{10,1... | collective-permute-start | bytes 393224 | tf_op jit(solution)/shard_map/ppermute | solution.py:253
  5.1 4.7 %collective-permute-start.1 = (bf16[64,1024]{1,0:T(8,128)(2,1)S(1)}, bf16[64,1024]{1,0:T(8,128)(2,1)S(1)}, u32[]{:S(2)}, u32[]{:S(2)}) collective-permute-start(bf16[64,1024]{1,0:T(8,128)(2,1)S(1)} %get-tuple-element.27), channel_id=1, source_target_pairs={{0,15},{1,0},{2,1},{3,2},{4,3},{5,4},{6,5},{7,6},{8,7},{9,8},{10,9... | collective-permute-start | bytes 393224 | tf_op jit(solution)/shard_map/ppermute | solution.py:253
  9.8 0.0 slice-done
  9.8 0.0 slice-done.1
  9.8 0.0 copy-start.5
  9.8 0.0 copy-start.6
  9.8 1.3 %own.1 = (bf16[256,1024]{1,0:T(8,128)(2,1)S(1)}, bf16[128,1024]{1,0:T(8,128)(2,1)S(1)}, bf16[128,1024]{1,0:T(8,128)(2,1)S(1)}) custom-call(bf16[128,1024]{1,0:T(8,128)(2,1)S(1)} %get-tuple-element.25.x_ref, bf16[1024,3072]{1,0:T(8,128)(2,1)S(1)} %bitcast.8), custom_call_target="tpu_custom_call" | custom-call | flops 805306368 | bytes 6553600 | tf_op jit(solution)/shard_map/own/pallas_call | solution.py:46
  11.2 0.0 copy-done.5
  11.2 0.0 copy-done.6
  11.2 1.0 %plan.1 = (bf16[384,128]{1,0:T(8,128)(2,1)S(1)}, f32[128,8]{1,0:T(8,128)S(1)}, bf16[256,384]{1,0:T(8,128)(2,1)S(1)}, bf16[256,768]{1,0:T(8,128)(2,1)S(1)}) custom-call(s32[2]{0:T(128)S(1)} %copy-done.6, s32[2,128]{1,0:T(2,128)S(1)} %bitcast.11), custom_call_target="tpu_custom_call" | custom-call | flops 1073741824 | bytes 1032 | tf_op jit(solution)/shard_map/plan/pallas_call | solution.py:46
  12.2 0.0 collective-permute-done.left_ref
  12.3 0.0 collective-permute-done.1.right_ref
  12.3 0.1 side.1.side_ref
  12.4 2.6 %collective-permute-start.3 = (bf16[64,1024]{1,0:T(8,128)(2,1)S(1)}, bf16[64,1024]{1,0:T(8,128)(2,1)S(1)}, u32[]{:S(2)}, u32[]{:S(2)}) collective-permute-start(bf16[64,1024]{1,0:T(8,128)(2,1)S(1)} %side.1.side_ref), channel_id=1, source_target_pairs={{0,112},{1,113},{2,114},{3,115},{4,116},{5,117},{6,118},{7,119},{8... | collective-permute-start | bytes 393224 | tf_op jit(solution)/shard_map/ppermute | solution.py:253
  14.9 0.7 collective-permute-start.2
  15.6 0.0 collective-permute-done.4.up_ref
  15.6 0.0 collective-permute-done.5.down_ref
  15.6 0.0 copy-start
  15.6 0.0 copy-start.1
  15.6 2.3 %near.1 = (f32[128,1024]{1,0:T(8,128)S(1)}, f32[128,1024]{1,0:T(8,128)S(1)}) custom-call(bf16[128,1024]{1,0:T(8,128)(2,1)S(1)} %collective-permute-done.4.up_ref, bf16[128,1024]{1,0:T(8,128)(2,1)S(1)} %collective-permute-done.5.down_ref, bf16[64,1024]{1,0:T(8,128)(2,1)S(1)} %side.1.side_ref, bf16[1024,3072]{1,0:T(8,128)(2,1)S(1)} %bitcast.8, ...), custom_call_target="tpu_custom_call" | custom-call | flops 1073741824 | bytes 8196096 | tf_op jit(solution)/shard_map/near/pallas_call | solution.py:46
  18.0 0.3 collective-permute-done.3.down_ref
  18.2 0.0 collective-permute-done.2.up_ref
  18.2 0.0 copy-done
  18.2 0.0 copy-done.1
  18.2 2.6 %last.1 = (bf16[128,1024]{1,0:T(8,128)(2,1)S(1)}, f32[128,128]{1,0:T(8,128)S(1)}, bf16[64,2,6,8,128]{4,3,2,1,0:T(8,128)(2,1)S(1)}) custom-call(bf16[128,1024]{1,0:T(8,128)(2,1)S(1)} %get-tuple-element.25.x_ref, bf16[64,1024]{1,0:T(8,128)(2,1)S(1)} %collective-permute-done.2.up_ref, bf16[64,1024]{1,0:T(8,128)(2,1)S(1)} %collective-permute-done.3.down_ref, ...), custom_call_target="tpu_custom_call" | custom-call | flops 805306368 | bytes 10915840 | tf_op jit(solution)/shard_map/last/pallas_call | solution.py:46
  20.8 0.0 copy-start.2
  20.8 0.0 copy-start.3
  20.8 0.0 copy-start.4
  20.8 32.9 %all_to_all.10.rows_ref = bf16[768,8,128]{2,1,0:T(8,128)(2,1)S(1)} all-to-all(bf16[768,8,128]{2,1,0:T(8,128)(2,1)S(1)} %bitcast.9), channel_id=1, replica_groups=mesh['lat'=8,'lon'=16] {'lat','lon'}, dimensions={0} | all-to-all | bytes 3145728 | tf_op jit(solution)/shard_map/all_to_all | solution.py:318
  53.7 0.0 copy-done.2
  53.7 0.0 copy-done.3
  53.7 0.0 copy-done.4
  53.7 2.6 %experts.1 = bf16[768,8,128]{2,1,0:T(8,128)(2,1)S(1)} custom-call(bf16[768,8,128]{2,1,0:T(8,128)(2,1)S(1)} %all_to_all.10.rows_ref, bf16[1024,512]{1,0:T(8,128)(2,1)S(1)} %copy-done.2, bf16[1024,512]{1,0:T(8,128)(2,1)S(1)} %copy-done.3, bf16[512,1024]{1,0:T(8,128)(2,1)S(1)} %copy-done.4), custom_call_target="tpu_custom_call" | custom-call | flops 4294967296 | bytes 4718592 | tf_op jit(solution)/shard_map/experts/pallas_call | solution.py:46
  56.3 28.4 %all_to_all.11.back_ref = bf16[768,8,128]{2,1,0:T(8,128)(2,1)S(1)} all-to-all(bf16[768,8,128]{2,1,0:T(8,128)(2,1)S(1)} %experts.1), channel_id=1, replica_groups=mesh['lat'=8,'lon'=16] {'lat','lon'}, dimensions={0} | all-to-all | bytes 3145728 | tf_op jit(solution)/shard_map/all_to_all | solution.py:322
  84.7 1.3 %combine.1 = bf16[128,1024]{1,0:T(8,128)(2,1)} custom-call(bf16[768,8,128]{2,1,0:T(8,128)(2,1)S(1)} %all_to_all.11.back_ref, bf16[256,768]{1,0:T(8,128)(2,1)S(1)} %get-tuple-element.42.pick_ref, f32[128,128]{1,0:T(8,128)S(1)} %get-tuple-element.43.gates_ref, bf16[128,1024]{1,0:T(8,128)(2,1)S(1)} %get-tuple-element.44.mixed_ref), custom_call_target="tpu_custom_call" | custom-call | flops 1073741824 | bytes 2293760 | tf_op jit(solution)/shard_map/combine/pallas_call | solution.py:46
  (1 shorter events, 0.0 us)
Async XLA Ops:
  0.0 9.8 %slice-start = ((s8[6291456]{0:T(1024)(128)(4,1)}), s8[4194304]{0:T(1024)(128)(4,1)S(1)}, s32[]{:S(2)}) async-start(s8[6291456]{0:T(1024)(128)(4,1)} %bitcast.7), calls=%async_computation.2 | async-start | bytes 8388608
  0.0 9.8 %slice-start.1 = ((s8[6291456]{0:T(1024)(128)(4,1)}), s8[2097152]{0:T(1024)(128)(4,1)S(1)}, s32[]{:S(2)}) async-start(s8[6291456]{0:T(1024)(128)(4,1)} %bitcast.7), calls=%async_computation.3 | async-start | bytes 4194304
  1.2 14.4 %collective-permute-start.4 = (bf16[128,1024]{1,0:T(8,128)(2,1)}, bf16[128,1024]{1,0:T(8,128)(2,1)S(1)}, u32[]{:S(2)}, u32[]{:S(2)}) collective-permute-start(bf16[128,1024]{1,0:T(8,128)(2,1)} %bitcast.tokens_ref), channel_id=1, source_target_pairs={{0,16},{1,17},{2,18},{3,19},{4,20},{5,21},{6,22},{7,23},{8,24},{9,... | collective-permute-start | bytes 786440 | tf_op jit(solution)/shard_map/ppermute | solution.py:253
  3.9 11.7 %collective-permute-start.5 = (bf16[128,1024]{1,0:T(8,128)(2,1)S(1)}, bf16[128,1024]{1,0:T(8,128)(2,1)S(1)}, u32[]{:S(2)}, u32[]{:S(2)}) collective-permute-start(bf16[128,1024]{1,0:T(8,128)(2,1)S(1)} %get-tuple-element.35), channel_id=1, source_target_pairs={{0,112},{1,113},{2,114},{3,115},{4,116},{5,117},{6,118},{7,119},{8... | collective-permute-start | bytes 786440 | tf_op jit(solution)/shard_map/ppermute | solution.py:253
  3.9 8.4 %collective-permute-start = (bf16[64,1024]{1,0:T(8,128)(2,1)S(1)}, bf16[64,1024]{1,0:T(8,128)(2,1)S(1)}, u32[]{:S(2)}, u32[]{:S(2)}) collective-permute-start(bf16[64,1024]{1,0:T(8,128)(2,1)S(1)} %get-tuple-element.26), channel_id=1, source_target_pairs={{0,1},{1,2},{2,3},{3,4},{4,5},{5,6},{6,7},{7,8},{8,9},{9,10},{10,1... | collective-permute-start | bytes 393224 | tf_op jit(solution)/shard_map/ppermute | solution.py:253
  5.1 7.2 %collective-permute-start.1 = (bf16[64,1024]{1,0:T(8,128)(2,1)S(1)}, bf16[64,1024]{1,0:T(8,128)(2,1)S(1)}, u32[]{:S(2)}, u32[]{:S(2)}) collective-permute-start(bf16[64,1024]{1,0:T(8,128)(2,1)S(1)} %get-tuple-element.27), channel_id=1, source_target_pairs={{0,15},{1,0},{2,1},{3,2},{4,3},{5,4},{6,5},{7,6},{8,7},{9,8},{10,9... | collective-permute-start | bytes 393224 | tf_op jit(solution)/shard_map/ppermute | solution.py:253
  9.8 1.4 %copy-start.5 = (s32[1,1,128,2]{2,3,1,0:T(2,128)S(1)}, s32[1,1,128,2]{2,3,1,0:T(2,128)}, u32[]{:S(2)}) copy-start(s32[1,1,128,2]{2,3,1,0:T(2,128)} %param.14) | copy-start | bytes 3076
  9.8 1.4 %copy-start.6 = (s32[2]{0:T(128)S(1)}, s32[2]{0:T(128)}, u32[]{:S(2)}) copy-start(s32[2]{0:T(128)} %shifts_ref) | copy-start | bytes 28
  12.4 5.8 %collective-permute-start.3 = (bf16[64,1024]{1,0:T(8,128)(2,1)S(1)}, bf16[64,1024]{1,0:T(8,128)(2,1)S(1)}, u32[]{:S(2)}, u32[]{:S(2)}) collective-permute-start(bf16[64,1024]{1,0:T(8,128)(2,1)S(1)} %side.1.side_ref), channel_id=1, source_target_pairs={{0,112},{1,113},{2,114},{3,115},{4,116},{5,117},{6,118},{7,119},{8... | collective-permute-start | bytes 393224 | tf_op jit(solution)/shard_map/ppermute | solution.py:253
  14.9 3.3 %collective-permute-start.2 = (bf16[64,1024]{1,0:T(8,128)(2,1)S(1)}, bf16[64,1024]{1,0:T(8,128)(2,1)S(1)}, u32[]{:S(2)}, u32[]{:S(2)}) collective-permute-start(bf16[64,1024]{1,0:T(8,128)(2,1)S(1)} %side.1.side_ref), channel_id=1, source_target_pairs={{0,16},{1,17},{2,18},{3,19},{4,20},{5,21},{6,22},{7,23},{8,24},{9,... | collective-permute-start | bytes 393224 | tf_op jit(solution)/shard_map/ppermute | solution.py:253
  15.6 2.6 %copy-start = (bf16[1024,1024]{1,0:T(8,128)(2,1)S(1)}, bf16[1024,1024]{1,0:T(8,128)(2,1)}, u32[]{:S(2)}) copy-start(bf16[1024,1024]{1,0:T(8,128)(2,1)} %wo_ref.1) | copy-start | bytes 6291460
  15.6 2.6 %copy-start.1 = (bf16[1024,64]{0,1:T(8,128)(2,1)S(1)}, bf16[1024,64]{0,1:T(8,128)(2,1)}, u32[]{:S(2)}) copy-start(bf16[1024,64]{0,1:T(8,128)(2,1)} %param.13) | copy-start | bytes 393220
  20.8 32.9 %copy-start.2 = (bf16[1024,512]{1,0:T(8,128)(2,1)S(1)}, bf16[1024,512]{1,0:T(8,128)(2,1)}, u32[]{:S(2)}) copy-start(bf16[1024,512]{1,0:T(8,128)(2,1)} %wg_ref.1) | copy-start | bytes 3145732
  20.8 32.9 %copy-start.3 = (bf16[1024,512]{1,0:T(8,128)(2,1)S(1)}, bf16[1024,512]{1,0:T(8,128)(2,1)}, u32[]{:S(2)}) copy-start(bf16[1024,512]{1,0:T(8,128)(2,1)} %wu_ref.1) | copy-start | bytes 3145732
  20.8 32.9 %copy-start.4 = (bf16[512,1024]{1,0:T(8,128)(2,1)S(1)}, bf16[512,1024]{1,0:T(8,128)(2,1)}, u32[]{:S(2)}) copy-start(bf16[512,1024]{1,0:T(8,128)(2,1)} %wd_ref.1) | copy-start | bytes 3145732

commit v7 on v6

--- a/solution.py
+++ b/solution.py
@@ -59,10 +59,11 @@
     return lax.dot_general(a, b, (((1,), (1,)), ((), ())), preferred_element_type=F32)
 
 
-def split_kernel(tokens_ref, x_ref, low_ref, high_ref, down_ref):
+def split_kernel(tokens_ref, x_ref, low_ref, high_ref, *parts):
     x = tokens_ref[...]
     x_ref[...] = x
-    down_ref[...] = x
+    for i, part in enumerate(parts):
+        part[...] = x[i % 2 * WIN * WIN : (i % 2 + 1) * WIN * WIN]
     halves = x.astype(F32).reshape(-1, 2, WIN, D)
     low_ref[...] = halves[:, 0].reshape(-1, D).astype(BF16)
     high_ref[...] = halves[:, 1].reshape(-1, D).astype(BF16)
@@ -171,11 +172,12 @@
 
 
 def near_kernel(
-    up_ref, down_ref, side_ref, w_ref, mask_ref, cells_ref, qq_ref, k_ref, v_ref, num_ref, den_ref
+    up_ref, up_more_ref, down_ref, down_more_ref, side_ref, w_ref, mask_ref, cells_ref, qq_ref, k_ref,
+    v_ref, num_ref, den_ref,
 ):
-    n = up_ref.shape[0]
-    past = cells_ref[:, 4:5] > 0.5
-    band = jnp.where(past, up_ref[...].astype(F32), down_ref[...].astype(F32))
+    up = jnp.concatenate([up_ref[...], up_more_ref[...]], axis=0).astype(F32)
+    down = jnp.concatenate([down_ref[...], down_more_ref[...]], axis=0).astype(F32)
+    band = jnp.where(cells_ref[:, 4:5] > 0.5, up, down)
     x = jnp.concatenate(
         [rms(band).astype(BF16), rms(side_ref[...].astype(F32)).astype(BF16)], axis=0
     )
@@ -259,18 +261,18 @@
     experts = router.shape[1]
     shape = jax.ShapeDtypeStruct
     half = shape((n // 2, width), BF16)
-    x, low, high, for_down = vmem_call(
+    x, low, high, *parts = vmem_call(
         split_kernel,
         "split",
-        [shape((n, width), BF16), half, half, shape((n, width), BF16)],
+        [shape((n, width), BF16), *[half] * 6],
         (tokens.reshape(n, width),),
         3 << 30,
     )
+    rows_up, rows_down = parts[:2], parts[2:]
     left = moved(high, 0, 1)
     right = moved(low, 0, -1)
-    later, _, _ = lax.optimization_barrier((tokens.reshape(n, width), high, low))
-    up = moved(later, 1, 0)
-    down = moved(for_down, -1, 0)
+    above = [moved(part, 1, 0) for part in rows_up]
+    below = [moved(part, -1, 0) for part in rows_down]
     whole = shape((n, width), BF16)
     qq, keys, values = vmem_call(
         own_kernel,
@@ -300,7 +302,7 @@
         near_kernel,
         "near",
         [shape((n, width), F32)] * 2,
-        (up, down, side, w_qkv, mask, cells, qq, keys, values),
+        (*above, *below, side, w_qkv, mask, cells, qq, keys, values),
         8 * n * width * width,
     )
     mixed, gates, send = vmem_call(

time: 86.2 us -> 84.8 us (0.984)
  blocking collectives: 61.3 us -> 59.1 us
  Pallas kernels: 12.4 us -> 11.3 us
  local copies, waits for them, and re-layouts: 0.05 us -> 1.14 us
    all_to_all x1, blocking collectives: 32.9 us -> 30.7 us  [body(): lax.all_to_all(send, AXES, split_axis=0, concat_axis=0, tiled=True)]
    unnamed x18 -> x20, local copies, waits for them, and re-layouts: 0.05 us -> 1.14 us
    pallas_call x8, Pallas kernels: 12.4 us -> 11.3 us  [vmem_call(): pl.pallas_call(kernel, in_specs=specs, out_specs=outs, out_shape=out_shap...]
    ppermute x6 -> x8, starting transfers between devices: 11.9 us -> 12.6 us  [moved(): return lax.ppermute(x, AXES, pairs)]
  transfers between devices with their start and end apart: 6 -> 8, of which waited for: 1 -> 2; matrix products, arithmetic and copies ran while one was open for 0% -> 0% of each run, Pallas kernels for 6% -> 6%
where the time goes in v7:
time: 84.8 us; the launch traced here: 84.7 us
  blocking collectives  59.1 us (70%)
  starting transfers between devices  12.6 us (15%)
  Pallas kernels  11.3 us (13%)
  local copies, waits for them, and re-layouts  1.14 us (1%)
    all_to_all x1, blocking collectives, body(): lax.all_to_all(send, AXES, split_axis=0, concat_axis=0, tiled=True)  30.7 us
    all_to_all x1, blocking collectives, body(): back = lax.all_to_all(part, AXES, split_axis=0, concat_axis=0, tiled=True)  28.4 us
    ppermute x8, starting transfers between devices, moved(): return lax.ppermute(x, AXES, pairs)  12.6 us
    pallas_call x8, Pallas kernels, vmem_call(): pl.pallas_call(kernel, in_specs=specs, out_specs=outs, out_shape=out_shap...  11.3 us
  transfers between devices with their start and end apart: 8, of which 2 were waited for; matrix products, arithmetic and copies ran while one was open for 0% of the time, Pallas kernels for 6%

profile of v7, /device:TPU:1, one launch (start us, length us, event | category | flops | bytes accessed | tf_op | source)
XLA Modules:
  0.0 84.7 jit_solution(11824804128053752685)
XLA Ops:
  0.0 0.0 slice-start
  0.0 0.0 copy-start.5
  0.0 1.1 %copy-done.5 = bf16[8,16,1024]{2,1,0:T(8,128)(2,1)S(1)} copy-done((bf16[8,16,1024]{2,1,0:T(8,128)(2,1)S(1)}, bf16[8,16,1024]{2,1,0:T(8,128)(2,1)}, u32[]{:S(2)}) %copy-start.5) | copy-done | bytes 262168
  1.1 0.0 slice-start.1
  1.1 0.1 split.1
  1.2 2.1 %collective-permute-start = (bf16[64,1024]{1,0:T(8,128)(2,1)S(1)}, bf16[64,1024]{1,0:T(8,128)(2,1)S(1)}, u32[]{:S(2)}, u32[]{:S(2)}) collective-permute-start(bf16[64,1024]{1,0:T(8,128)(2,1)S(1)} %get-tuple-element.28), channel_id=1, source_target_pairs={{0,1},{1,2},{2,3},{3,4},{4,5},{5,6},{6,7},{7,8},{8,9},{9,10},{10,1... | collective-permute-start | bytes 393224 | tf_op jit(solution)/shard_map/ppermute | solution.py:255
  3.3 4.8 %collective-permute-start.1 = (bf16[64,1024]{1,0:T(8,128)(2,1)S(1)}, bf16[64,1024]{1,0:T(8,128)(2,1)S(1)}, u32[]{:S(2)}, u32[]{:S(2)}) collective-permute-start(bf16[64,1024]{1,0:T(8,128)(2,1)S(1)} %get-tuple-element.29), channel_id=1, source_target_pairs={{0,15},{1,0},{2,1},{3,2},{4,3},{5,4},{6,5},{7,6},{8,7},{9,8},{10,9... | collective-permute-start | bytes 393224 | tf_op jit(solution)/shard_map/ppermute | solution.py:255
  8.1 2.1 %collective-permute-start.4 = (bf16[64,1024]{1,0:T(8,128)(2,1)S(1)}, bf16[64,1024]{1,0:T(8,128)(2,1)S(1)}, u32[]{:S(2)}, u32[]{:S(2)}) collective-permute-start(bf16[64,1024]{1,0:T(8,128)(2,1)S(1)} %get-tuple-element.36), channel_id=1, source_target_pairs={{0,16},{1,17},{2,18},{3,19},{4,20},{5,21},{6,22},{7,23},{8,24},{9,... | collective-permute-start | bytes 393224 | tf_op jit(solution)/shard_map/ppermute | solution.py:255
  10.2 0.0 collective-permute-start.5
  10.3 0.5 collective-permute-start.6
  10.8 0.0 slice-done
  10.8 0.0 slice-done.1
  10.8 0.0 copy-start.6
  10.8 0.0 copy-start.7
  10.8 1.3 %own.1 = (bf16[256,1024]{1,0:T(8,128)(2,1)S(1)}, bf16[128,1024]{1,0:T(8,128)(2,1)S(1)}, bf16[128,1024]{1,0:T(8,128)(2,1)S(1)}) custom-call(bf16[128,1024]{1,0:T(8,128)(2,1)S(1)} %get-tuple-element.27.x_ref, bf16[1024,3072]{1,0:T(8,128)(2,1)S(1)} %bitcast.8), custom_call_target="tpu_custom_call" | custom-call | flops 805306368 | bytes 6553600 | tf_op jit(solution)/shard_map/own/pallas_call | solution.py:46
  12.1 0.0 collective-permute-done.left_ref
  12.1 1.3 %collective-permute-start.7 = (bf16[64,1024]{1,0:T(8,128)(2,1)S(1)}, bf16[64,1024]{1,0:T(8,128)(2,1)S(1)}, u32[]{:S(2)}, u32[]{:S(2)}) collective-permute-start(bf16[64,1024]{1,0:T(8,128)(2,1)S(1)} %get-tuple-element.39), channel_id=1, source_target_pairs={{0,112},{1,113},{2,114},{3,115},{4,116},{5,117},{6,118},{7,119},{8... | collective-permute-start | bytes 393224 | tf_op jit(solution)/shard_map/ppermute | solution.py:255
  13.4 0.0 copy-done.6
  13.4 0.0 copy-done.7
  13.4 1.0 %plan.1 = (bf16[384,128]{1,0:T(8,128)(2,1)S(1)}, f32[128,8]{1,0:T(8,128)S(1)}, bf16[256,384]{1,0:T(8,128)(2,1)S(1)}, bf16[256,768]{1,0:T(8,128)(2,1)S(1)}) custom-call(s32[2]{0:T(128)S(1)} %copy-done.7, s32[2,128]{1,0:T(2,128)S(1)} %bitcast.12), custom_call_target="tpu_custom_call" | custom-call | flops 1073741824 | bytes 1032 | tf_op jit(solution)/shard_map/plan/pallas_call | solution.py:46
  14.5 0.0 collective-permute-done.1.right_ref
  14.5 0.1 side.1.side_ref
  14.6 1.0 %collective-permute-start.3 = (bf16[64,1024]{1,0:T(8,128)(2,1)S(1)}, bf16[64,1024]{1,0:T(8,128)(2,1)S(1)}, u32[]{:S(2)}, u32[]{:S(2)}) collective-permute-start(bf16[64,1024]{1,0:T(8,128)(2,1)S(1)} %side.1.side_ref), channel_id=1, source_target_pairs={{0,112},{1,113},{2,114},{3,115},{4,116},{5,117},{6,118},{7,119},{8... | collective-permute-start | bytes 393224 | tf_op jit(solution)/shard_map/ppermute | solution.py:255
  15.6 0.0 collective-permute-done.4.up_ref
  15.6 0.8 collective-permute-start.2
  16.4 0.0 collective-permute-done.5.up_more_ref
  16.4 0.0 collective-permute-done.6.down_ref
  16.4 0.2 collective-permute-done.7.down_more_ref
  16.5 0.0 copy-start
  16.5 0.0 copy-start.1
  16.5 2.3 %near.1 = (f32[128,1024]{1,0:T(8,128)S(1)}, f32[128,1024]{1,0:T(8,128)S(1)}) custom-call(bf16[64,1024]{1,0:T(8,128)(2,1)S(1)} %collective-permute-done.4.up_ref, bf16[64,1024]{1,0:T(8,128)(2,1)S(1)} %collective-permute-done.5.up_more_ref, bf16[64,1024]{1,0:T(8,128)(2,1)S(1)} %collective-permute-done.6.down_ref, ...), custom_call_target="tpu_custom_call" | custom-call | flops 1073741824 | bytes 8196096 | tf_op jit(solution)/shard_map/near/pallas_call | solution.py:46
  18.9 0.2 collective-permute-done.3.down_ref
  19.0 0.0 collective-permute-done.2.up_ref
  19.0 0.0 copy-done
  19.0 0.0 copy-done.1
  19.0 2.6 %last.1 = (bf16[128,1024]{1,0:T(8,128)(2,1)S(1)}, f32[128,128]{1,0:T(8,128)S(1)}, bf16[64,2,6,8,128]{4,3,2,1,0:T(8,128)(2,1)S(1)}) custom-call(bf16[128,1024]{1,0:T(8,128)(2,1)S(1)} %get-tuple-element.27.x_ref, bf16[64,1024]{1,0:T(8,128)(2,1)S(1)} %collective-permute-done.2.up_ref, bf16[64,1024]{1,0:T(8,128)(2,1)S(1)} %collective-permute-done.3.down_ref, ...), custom_call_target="tpu_custom_call" | custom-call | flops 805306368 | bytes 10915840 | tf_op jit(solution)/shard_map/last/pallas_call | solution.py:46
  21.6 0.0 copy-start.2
  21.6 0.0 copy-start.3
  21.6 0.0 copy-start.4
  21.6 30.7 %all_to_all.10.rows_ref = bf16[768,8,128]{2,1,0:T(8,128)(2,1)S(1)} all-to-all(bf16[768,8,128]{2,1,0:T(8,128)(2,1)S(1)} %bitcast.9), channel_id=1, replica_groups=mesh['lat'=8,'lon'=16] {'lat','lon'}, dimensions={0} | all-to-all | bytes 3145728 | tf_op jit(solution)/shard_map/all_to_all | solution.py:320
  52.3 0.0 copy-done.2
  52.3 0.0 copy-done.3
  52.3 0.0 copy-done.4
  52.4 2.6 %experts.1 = bf16[768,8,128]{2,1,0:T(8,128)(2,1)S(1)} custom-call(bf16[768,8,128]{2,1,0:T(8,128)(2,1)S(1)} %all_to_all.10.rows_ref, bf16[1024,512]{1,0:T(8,128)(2,1)S(1)} %copy-done.2, bf16[1024,512]{1,0:T(8,128)(2,1)S(1)} %copy-done.3, bf16[512,1024]{1,0:T(8,128)(2,1)S(1)} %copy-done.4), custom_call_target="tpu_custom_call" | custom-call | flops 4294967296 | bytes 4718592 | tf_op jit(solution)/shard_map/experts/pallas_call | solution.py:46
  55.0 28.4 %all_to_all.11.back_ref = bf16[768,8,128]{2,1,0:T(8,128)(2,1)S(1)} all-to-all(bf16[768,8,128]{2,1,0:T(8,128)(2,1)S(1)} %experts.1), channel_id=1, replica_groups=mesh['lat'=8,'lon'=16] {'lat','lon'}, dimensions={0} | all-to-all | bytes 3145728 | tf_op jit(solution)/shard_map/all_to_all | solution.py:324
  83.4 1.3 %combine.1 = bf16[128,1024]{1,0:T(8,128)(2,1)} custom-call(bf16[768,8,128]{2,1,0:T(8,128)(2,1)S(1)} %all_to_all.11.back_ref, bf16[256,768]{1,0:T(8,128)(2,1)S(1)} %get-tuple-element.46.pick_ref, f32[128,128]{1,0:T(8,128)S(1)} %get-tuple-element.47.gates_ref, bf16[128,1024]{1,0:T(8,128)(2,1)S(1)} %get-tuple-element.48.mixed_ref), custom_call_target="tpu_custom_call" | custom-call | flops 1073741824 | bytes 2293760 | tf_op jit(solution)/shard_map/combine/pallas_call | solution.py:46
  (1 shorter events, 0.0 us)
Async XLA Ops:
  0.0 10.8 %slice-start = ((s8[6291456]{0:T(1024)(128)(4,1)}), s8[4194304]{0:T(1024)(128)(4,1)S(1)}, s32[]{:S(2)}) async-start(s8[6291456]{0:T(1024)(128)(4,1)} %bitcast.7), calls=%async_computation.2 | async-start | bytes 8388608
  0.0 1.1 %copy-start.5 = (bf16[8,16,1024]{2,1,0:T(8,128)(2,1)S(1)}, bf16[8,16,1024]{2,1,0:T(8,128)(2,1)}, u32[]{:S(2)}) copy-start(bf16[8,16,1024]{2,1,0:T(8,128)(2,1)} %param.9) | copy-start | bytes 786436
  1.1 9.7 %slice-start.1 = ((s8[6291456]{0:T(1024)(128)(4,1)}), s8[2097152]{0:T(1024)(128)(4,1)S(1)}, s32[]{:S(2)}) async-start(s8[6291456]{0:T(1024)(128)(4,1)} %bitcast.7), calls=%async_computation.3 | async-start | bytes 4194304
  1.2 10.9 %collective-permute-start = (bf16[64,1024]{1,0:T(8,128)(2,1)S(1)}, bf16[64,1024]{1,0:T(8,128)(2,1)S(1)}, u32[]{:S(2)}, u32[]{:S(2)}) collective-permute-start(bf16[64,1024]{1,0:T(8,128)(2,1)S(1)} %get-tuple-element.28), channel_id=1, source_target_pairs={{0,1},{1,2},{2,3},{3,4},{4,5},{5,6},{6,7},{7,8},{8,9},{9,10},{10,1... | collective-permute-start | bytes 393224 | tf_op jit(solution)/shard_map/ppermute | solution.py:255
  3.3 11.2 %collective-permute-start.1 = (bf16[64,1024]{1,0:T(8,128)(2,1)S(1)}, bf16[64,1024]{1,0:T(8,128)(2,1)S(1)}, u32[]{:S(2)}, u32[]{:S(2)}) collective-permute-start(bf16[64,1024]{1,0:T(8,128)(2,1)S(1)} %get-tuple-element.29), channel_id=1, source_target_pairs={{0,15},{1,0},{2,1},{3,2},{4,3},{5,4},{6,5},{7,6},{8,7},{9,8},{10,9... | collective-permute-start | bytes 393224 | tf_op jit(solution)/shard_map/ppermute | solution.py:255
  8.1 7.5 %collective-permute-start.4 = (bf16[64,1024]{1,0:T(8,128)(2,1)S(1)}, bf16[64,1024]{1,0:T(8,128)(2,1)S(1)}, u32[]{:S(2)}, u32[]{:S(2)}) collective-permute-start(bf16[64,1024]{1,0:T(8,128)(2,1)S(1)} %get-tuple-element.36), channel_id=1, source_target_pairs={{0,16},{1,17},{2,18},{3,19},{4,20},{5,21},{6,22},{7,23},{8,24},{9,... | collective-permute-start | bytes 393224 | tf_op jit(solution)/shard_map/ppermute | solution.py:255
  10.2 6.1 %collective-permute-start.5 = (bf16[64,1024]{1,0:T(8,128)(2,1)S(1)}, bf16[64,1024]{1,0:T(8,128)(2,1)S(1)}, u32[]{:S(2)}, u32[]{:S(2)}) collective-permute-start(bf16[64,1024]{1,0:T(8,128)(2,1)S(1)} %get-tuple-element.37), channel_id=1, source_target_pairs={{0,16},{1,17},{2,18},{3,19},{4,20},{5,21},{6,22},{7,23},{8,24},{9,... | collective-permute-start | bytes 393224 | tf_op jit(solution)/shard_map/ppermute | solution.py:255
  10.3 6.1 %collective-permute-start.6 = (bf16[64,1024]{1,0:T(8,128)(2,1)S(1)}, bf16[64,1024]{1,0:T(8,128)(2,1)S(1)}, u32[]{:S(2)}, u32[]{:S(2)}) collective-permute-start(bf16[64,1024]{1,0:T(8,128)(2,1)S(1)} %get-tuple-element.38), channel_id=1, source_target_pairs={{0,112},{1,113},{2,114},{3,115},{4,116},{5,117},{6,118},{7,119},{8... | collective-permute-start | bytes 393224 | tf_op jit(solution)/shard_map/ppermute | solution.py:255
  10.8 2.7 %copy-start.6 = (s32[1,1,128,2]{2,3,1,0:T(2,128)S(1)}, s32[1,1,128,2]{2,3,1,0:T(2,128)}, u32[]{:S(2)}) copy-start(s32[1,1,128,2]{2,3,1,0:T(2,128)} %param.14) | copy-start | bytes 3076
  10.8 2.7 %copy-start.7 = (s32[2]{0:T(128)S(1)}, s32[2]{0:T(128)}, u32[]{:S(2)}) copy-start(s32[2]{0:T(128)} %shifts_ref) | copy-start | bytes 28
  12.1 4.4 %collective-permute-start.7 = (bf16[64,1024]{1,0:T(8,128)(2,1)S(1)}, bf16[64,1024]{1,0:T(8,128)(2,1)S(1)}, u32[]{:S(2)}, u32[]{:S(2)}) collective-permute-start(bf16[64,1024]{1,0:T(8,128)(2,1)S(1)} %get-tuple-element.39), channel_id=1, source_target_pairs={{0,112},{1,113},{2,114},{3,115},{4,116},{5,117},{6,118},{7,119},{8... | collective-permute-start | bytes 393224 | tf_op jit(solution)/shard_map/ppermute | solution.py:255
  14.6 4.4 %collective-permute-start.3 = (bf16[64,1024]{1,0:T(8,128)(2,1)S(1)}, bf16[64,1024]{1,0:T(8,128)(2,1)S(1)}, u32[]{:S(2)}, u32[]{:S(2)}) collective-permute-start(bf16[64,1024]{1,0:T(8,128)(2,1)S(1)} %side.1.side_ref), channel_id=1, source_target_pairs={{0,112},{1,113},{2,114},{3,115},{4,116},{5,117},{6,118},{7,119},{8... | collective-permute-start | bytes 393224 | tf_op jit(solution)/shard_map/ppermute | solution.py:255
  15.6 3.5 %collective-permute-start.2 = (bf16[64,1024]{1,0:T(8,128)(2,1)S(1)}, bf16[64,1024]{1,0:T(8,128)(2,1)S(1)}, u32[]{:S(2)}, u32[]{:S(2)}) collective-permute-start(bf16[64,1024]{1,0:T(8,128)(2,1)S(1)} %side.1.side_ref), channel_id=1, source_target_pairs={{0,16},{1,17},{2,18},{3,19},{4,20},{5,21},{6,22},{7,23},{8,24},{9,... | collective-permute-start | bytes 393224 | tf_op jit(solution)/shard_map/ppermute | solution.py:255
  16.5 2.5 %copy-start = (bf16[1024,1024]{1,0:T(8,128)(2,1)S(1)}, bf16[1024,1024]{1,0:T(8,128)(2,1)}, u32[]{:S(2)}) copy-start(bf16[1024,1024]{1,0:T(8,128)(2,1)} %wo_ref.1) | copy-start | bytes 6291460
  16.5 2.5 %copy-start.1 = (bf16[1024,64]{0,1:T(8,128)(2,1)S(1)}, bf16[1024,64]{0,1:T(8,128)(2,1)}, u32[]{:S(2)}) copy-start(bf16[1024,64]{0,1:T(8,128)(2,1)} %param.13) | copy-start | bytes 393220
  21.6 30.7 %copy-start.2 = (bf16[1024,512]{1,0:T(8,128)(2,1)S(1)}, bf16[1024,512]{1,0:T(8,128)(2,1)}, u32[]{:S(2)}) copy-start(bf16[1024,512]{1,0:T(8,128)(2,1)} %wg_ref.1) | copy-start | bytes 3145732
  21.6 30.7 %copy-start.3 = (bf16[1024,512]{1,0:T(8,128)(2,1)S(1)}, bf16[1024,512]{1,0:T(8,128)(2,1)}, u32[]{:S(2)}) copy-start(bf16[1024,512]{1,0:T(8,128)(2,1)} %wu_ref.1) | copy-start | bytes 3145732
  21.6 30.7 %copy-start.4 = (bf16[512,1024]{1,0:T(8,128)(2,1)S(1)}, bf16[512,1024]{1,0:T(8,128)(2,1)}, u32[]{:S(2)}) copy-start(bf16[512,1024]{1,0:T(8,128)(2,1)} %wd_ref.1) | copy-start | bytes 3145732

commit v8 on v7

--- a/solution.py
+++ b/solution.py
@@ -164,11 +164,14 @@
         qq_ref[n:, lanes] = jnp.where(low_half, 0.0, q).astype(BF16)
 
 
-def side_kernel(left_ref, right_ref, cells_ref, side_ref):
+def side_kernel(left_ref, right_ref, cells_ref, side_ref, lower_ref, upper_ref):
     n = side_ref.shape[0]
-    side_ref[...] = jnp.where(
+    side = jnp.where(
         cells_ref[0:n, 5:6] > 0.5, left_ref[...].astype(F32), right_ref[...].astype(F32)
-    ).astype(BF16)
+    )
+    side_ref[...] = side.astype(BF16)
+    upper_ref[...] = side[0 : n - WIN].astype(BF16)
+    lower_ref[...] = side[WIN:].astype(BF16)
 
 
 def near_kernel(
@@ -191,13 +194,16 @@
 
 
 def last_kernel(
-    x_ref, up_ref, down_ref, w_ref, mask_ref, qq_ref, num_ref, den_ref,
+    x_ref, down_ref, up_ref, w_ref, mask_ref, qq_ref, num_ref, den_ref,
     wo_ref, router_ref, cells_ref, pack_ref, mixed_ref, gates_ref, send_ref,
 ):
     n = x_ref.shape[0]
-    m = up_ref.shape[0]
+    m = WIN * WIN
     past = cells_ref[0:m, 6:7] > 0.5
-    corner = jnp.where(past, up_ref[...].astype(F32), down_ref[...].astype(F32))
+    row = jnp.zeros((WIN, D), F32)
+    up = jnp.concatenate([row, up_ref[...].astype(F32)], axis=0)
+    down = jnp.concatenate([down_ref[...].astype(F32), row], axis=0)
+    corner = jnp.where(past, up, down)
     x = rms(corner).astype(BF16)
     keys = dot(x, w_ref[:, D : 2 * D]).astype(BF16)
     values = dot(x, w_ref[:, 2 * D :]).astype(BF16)
@@ -295,9 +301,12 @@
         1 << 30,
         spaces={0: pltpu.SMEM},
     )
-    side = vmem_call(side_kernel, "side", half, (left, right, cells), 1 << 10)
-    up_side = moved(side, 1, 0)
-    down_side = moved(side, -1, 0)
+    most = shape((WIN * WIN - WIN, width), BF16)
+    side, lower, upper = vmem_call(
+        side_kernel, "side", [half, most, most], (left, right, cells), 1 << 10
+    )
+    up_side = moved(lower, 1, 0)
+    down_side = moved(upper, -1, 0)
     num, den = vmem_call(
         near_kernel,
         "near",
@@ -313,7 +322,7 @@
             shape((n, 128), F32),
             shape((experts, 2, MOST, 8, width // 8), BF16),
         ],
-        (x, up_side, down_side, w_qkv, mask, qq, num, den, w_out, router.T, cells, pack),
+        (x, down_side, up_side, w_qkv, mask, qq, num, den, w_out, router.T, cells, pack),
         6 * n * width * width,
     )
     send = send.reshape(2 * experts * MOST, 8, width // 8)

time: 84.8 us -> 86 us (1.014)
  blocking collectives: 59.1 us -> 60 us
  transfers between devices with their start and end apart: 8 -> 8, of which waited for: 2 -> 1; matrix products, arithmetic and copies ran while one was open for 0% -> 0% of each run, Pallas kernels for 6% -> 6%
where the time goes in v8:
time: 86 us; the launch traced here: 85.9 us
  blocking collectives  60 us (70%)
  starting transfers between devices  12.7 us (15%)
  Pallas kernels  11.3 us (13%)
  local copies, waits for them, and re-layouts  1.15 us (1%)
    all_to_all x1, blocking collectives, body(): lax.all_to_all(send, AXES, split_axis=0, concat_axis=0, tiled=True)  31.6 us
    all_to_all x1, blocking collectives, body(): back = lax.all_to_all(part, AXES, split_axis=0, concat_axis=0, tiled=True)  28.4 us
    ppermute x8, starting transfers between devices, moved(): return lax.ppermute(x, AXES, pairs)  12.7 us
    pallas_call x8, Pallas kernels, vmem_call(): pl.pallas_call(kernel, in_specs=specs, out_specs=outs, out_shape=out_shap...  11.3 us
  transfers between devices with their start and end apart: 8, of which 1 were waited for; matrix products, arithmetic and copies ran while one was open for 0% of the time, Pallas kernels for 6%

profile of v8, /device:TPU:1, one launch (start us, length us, event | category | flops | bytes accessed | tf_op | source)
XLA Modules:
  0.0 85.9 jit_solution(18301361064427963772)
XLA Ops:
  0.0 0.0 slice-start
  0.0 0.0 copy-start.5
  0.0 1.1 %copy-done.5 = bf16[8,16,1024]{2,1,0:T(8,128)(2,1)S(1)} copy-done((bf16[8,16,1024]{2,1,0:T(8,128)(2,1)S(1)}, bf16[8,16,1024]{2,1,0:T(8,128)(2,1)}, u32[]{:S(2)}) %copy-start.5) | copy-done | bytes 262168
  1.1 0.0 slice-start.1
  1.1 0.1 split.1
  1.2 2.1 %collective-permute-start = (bf16[64,1024]{1,0:T(8,128)(2,1)S(1)}, bf16[64,1024]{1,0:T(8,128)(2,1)S(1)}, u32[]{:S(2)}, u32[]{:S(2)}) collective-permute-start(bf16[64,1024]{1,0:T(8,128)(2,1)S(1)} %get-tuple-element.31), channel_id=1, source_target_pairs={{0,1},{1,2},{2,3},{3,4},{4,5},{5,6},{6,7},{7,8},{8,9},{9,10},{10,1... | collective-permute-start | bytes 393224 | tf_op jit(solution)/shard_map/ppermute | solution.py:261
  3.3 4.8 %collective-permute-start.1 = (bf16[64,1024]{1,0:T(8,128)(2,1)S(1)}, bf16[64,1024]{1,0:T(8,128)(2,1)S(1)}, u32[]{:S(2)}, u32[]{:S(2)}) collective-permute-start(bf16[64,1024]{1,0:T(8,128)(2,1)S(1)} %get-tuple-element.32), channel_id=1, source_target_pairs={{0,15},{1,0},{2,1},{3,2},{4,3},{5,4},{6,5},{7,6},{8,7},{9,8},{10,9... | collective-permute-start | bytes 393224 | tf_op jit(solution)/shard_map/ppermute | solution.py:261
  8.1 2.1 %collective-permute-start.4 = (bf16[64,1024]{1,0:T(8,128)(2,1)S(1)}, bf16[64,1024]{1,0:T(8,128)(2,1)S(1)}, u32[]{:S(2)}, u32[]{:S(2)}) collective-permute-start(bf16[64,1024]{1,0:T(8,128)(2,1)S(1)} %get-tuple-element.41), channel_id=1, source_target_pairs={{0,16},{1,17},{2,18},{3,19},{4,20},{5,21},{6,22},{7,23},{8,24},{9,... | collective-permute-start | bytes 393224 | tf_op jit(solution)/shard_map/ppermute | solution.py:261
  10.2 0.0 collective-permute-start.5
  10.3 0.5 collective-permute-start.6
  10.8 0.5 collective-permute-done.left_ref
  11.3 1.2 %collective-permute-start.7 = (bf16[64,1024]{1,0:T(8,128)(2,1)S(1)}, bf16[64,1024]{1,0:T(8,128)(2,1)S(1)}, u32[]{:S(2)}, u32[]{:S(2)}) collective-permute-start(bf16[64,1024]{1,0:T(8,128)(2,1)S(1)} %get-tuple-element.44), channel_id=1, source_target_pairs={{0,112},{1,113},{2,114},{3,115},{4,116},{5,117},{6,118},{7,119},{8... | collective-permute-start | bytes 393224 | tf_op jit(solution)/shard_map/ppermute | solution.py:261
  12.5 0.0 slice-done
  12.5 0.0 slice-done.1
  12.5 0.0 copy-start.6
  12.5 0.0 copy-start.7
  12.5 1.3 %own.1 = (bf16[256,1024]{1,0:T(8,128)(2,1)S(1)}, bf16[128,1024]{1,0:T(8,128)(2,1)S(1)}, bf16[128,1024]{1,0:T(8,128)(2,1)S(1)}) custom-call(bf16[128,1024]{1,0:T(8,128)(2,1)S(1)} %get-tuple-element.30.x_ref, bf16[1024,3072]{1,0:T(8,128)(2,1)S(1)} %bitcast.8), custom_call_target="tpu_custom_call" | custom-call | flops 805306368 | bytes 6553600 | tf_op jit(solution)/shard_map/own/pallas_call | solution.py:46
  13.8 0.0 copy-done.6
  13.9 0.0 copy-done.7
  13.9 1.0 %plan.1 = (bf16[384,128]{1,0:T(8,128)(2,1)S(1)}, f32[128,8]{1,0:T(8,128)S(1)}, bf16[256,384]{1,0:T(8,128)(2,1)S(1)}, bf16[256,768]{1,0:T(8,128)(2,1)S(1)}) custom-call(s32[2]{0:T(128)S(1)} %copy-done.7, s32[2,128]{1,0:T(2,128)S(1)} %bitcast.12), custom_call_target="tpu_custom_call" | custom-call | flops 1073741824 | bytes 1032 | tf_op jit(solution)/shard_map/plan/pallas_call | solution.py:46
  14.9 0.0 collective-permute-done.1.right_ref
  14.9 0.1 side.1
  15.0 1.9 %collective-permute-start.2 = (bf16[56,1024]{1,0:T(8,128)(2,1)S(1)}, bf16[56,1024]{1,0:T(8,128)(2,1)S(1)}, u32[]{:S(2)}, u32[]{:S(2)}) collective-permute-start(bf16[56,1024]{1,0:T(8,128)(2,1)S(1)} %get-tuple-element.37), channel_id=1, source_target_pairs={{0,112},{1,113},{2,114},{3,115},{4,116},{5,117},{6,118},{7,119},{8... | collective-permute-start | bytes 344072 | tf_op jit(solution)/shard_map/ppermute | solution.py:261
  16.9 0.0 collective-permute-done.4.up_ref
  16.9 0.0 collective-permute-start.3
  17.0 0.0 collective-permute-done.5.up_more_ref
  17.0 0.0 collective-permute-done.6.down_ref
  17.0 0.0 collective-permute-done.7.down_more_ref
  17.0 0.0 copy-start
  17.0 0.0 copy-start.1
  17.0 2.3 %near.1 = (f32[128,1024]{1,0:T(8,128)S(1)}, f32[128,1024]{1,0:T(8,128)S(1)}) custom-call(bf16[64,1024]{1,0:T(8,128)(2,1)S(1)} %collective-permute-done.4.up_ref, bf16[64,1024]{1,0:T(8,128)(2,1)S(1)} %collective-permute-done.5.up_more_ref, bf16[64,1024]{1,0:T(8,128)(2,1)S(1)} %collective-permute-done.6.down_ref, ...), custom_call_target="tpu_custom_call" | custom-call | flops 1073741824 | bytes 8196096 | tf_op jit(solution)/shard_map/near/pallas_call | solution.py:46
  19.3 0.0 collective-permute-done.2.down_ref
  19.3 0.0 collective-permute-done.3.up_ref
  19.3 0.0 copy-done
  19.4 0.0 copy-done.1
  19.4 2.6 %last.1 = (bf16[128,1024]{1,0:T(8,128)(2,1)S(1)}, f32[128,128]{1,0:T(8,128)S(1)}, bf16[64,2,6,8,128]{4,3,2,1,0:T(8,128)(2,1)S(1)}) custom-call(bf16[128,1024]{1,0:T(8,128)(2,1)S(1)} %get-tuple-element.30.x_ref, bf16[56,1024]{1,0:T(8,128)(2,1)S(1)} %collective-permute-done.2.down_ref, bf16[56,1024]{1,0:T(8,128)(2,1)S(1)} %collective-permute-done.3.up_ref, ...), custom_call_target="tpu_custom_call" | custom-call | flops 805306368 | bytes 10883072 | tf_op jit(solution)/shard_map/last/pallas_call | solution.py:46
  21.9 0.0 copy-start.2
  21.9 0.0 copy-start.3
  22.0 0.0 copy-start.4
  22.0 31.6 %all_to_all.10.rows_ref = bf16[768,8,128]{2,1,0:T(8,128)(2,1)S(1)} all-to-all(bf16[768,8,128]{2,1,0:T(8,128)(2,1)S(1)} %bitcast.9), channel_id=1, replica_groups=mesh['lat'=8,'lon'=16] {'lat','lon'}, dimensions={0} | all-to-all | bytes 3145728 | tf_op jit(solution)/shard_map/all_to_all | solution.py:329
  53.5 0.0 copy-done.2
  53.5 0.0 copy-done.3
  53.5 0.0 copy-done.4
  53.5 2.6 %experts.1 = bf16[768,8,128]{2,1,0:T(8,128)(2,1)S(1)} custom-call(bf16[768,8,128]{2,1,0:T(8,128)(2,1)S(1)} %all_to_all.10.rows_ref, bf16[1024,512]{1,0:T(8,128)(2,1)S(1)} %copy-done.2, bf16[1024,512]{1,0:T(8,128)(2,1)S(1)} %copy-done.3, bf16[512,1024]{1,0:T(8,128)(2,1)S(1)} %copy-done.4), custom_call_target="tpu_custom_call" | custom-call | flops 4294967296 | bytes 4718592 | tf_op jit(solution)/shard_map/experts/pallas_call | solution.py:46
  56.1 28.4 %all_to_all.11.back_ref = bf16[768,8,128]{2,1,0:T(8,128)(2,1)S(1)} all-to-all(bf16[768,8,128]{2,1,0:T(8,128)(2,1)S(1)} %experts.1), channel_id=1, replica_groups=mesh['lat'=8,'lon'=16] {'lat','lon'}, dimensions={0} | all-to-all | bytes 3145728 | tf_op jit(solution)/shard_map/all_to_all | solution.py:333
  84.6 1.3 %combine.1 = bf16[128,1024]{1,0:T(8,128)(2,1)} custom-call(bf16[768,8,128]{2,1,0:T(8,128)(2,1)S(1)} %all_to_all.11.back_ref, bf16[256,768]{1,0:T(8,128)(2,1)S(1)} %get-tuple-element.52.pick_ref, f32[128,128]{1,0:T(8,128)S(1)} %get-tuple-element.53.gates_ref, bf16[128,1024]{1,0:T(8,128)(2,1)S(1)} %get-tuple-element.54.mixed_ref), custom_call_target="tpu_custom_call" | custom-call | flops 1073741824 | bytes 2293760 | tf_op jit(solution)/shard_map/combine/pallas_call | solution.py:46
  (1 shorter events, 0.0 us)
Async XLA Ops:
  0.0 12.5 %slice-start = ((s8[6291456]{0:T(1024)(128)(4,1)}), s8[4194304]{0:T(1024)(128)(4,1)S(1)}, s32[]{:S(2)}) async-start(s8[6291456]{0:T(1024)(128)(4,1)} %bitcast.7), calls=%async_computation.2 | async-start | bytes 8388608
  0.0 1.1 %copy-start.5 = (bf16[8,16,1024]{2,1,0:T(8,128)(2,1)S(1)}, bf16[8,16,1024]{2,1,0:T(8,128)(2,1)}, u32[]{:S(2)}) copy-start(bf16[8,16,1024]{2,1,0:T(8,128)(2,1)} %param.9) | copy-start | bytes 786436
  1.1 11.4 %slice-start.1 = ((s8[6291456]{0:T(1024)(128)(4,1)}), s8[2097152]{0:T(1024)(128)(4,1)S(1)}, s32[]{:S(2)}) async-start(s8[6291456]{0:T(1024)(128)(4,1)} %bitcast.7), calls=%async_computation.3 | async-start | bytes 4194304
  1.2 10.1 %collective-permute-start = (bf16[64,1024]{1,0:T(8,128)(2,1)S(1)}, bf16[64,1024]{1,0:T(8,128)(2,1)S(1)}, u32[]{:S(2)}, u32[]{:S(2)}) collective-permute-start(bf16[64,1024]{1,0:T(8,128)(2,1)S(1)} %get-tuple-element.31), channel_id=1, source_target_pairs={{0,1},{1,2},{2,3},{3,4},{4,5},{5,6},{6,7},{7,8},{8,9},{9,10},{10,1... | collective-permute-start | bytes 393224 | tf_op jit(solution)/shard_map/ppermute | solution.py:261
  3.3 11.6 %collective-permute-start.1 = (bf16[64,1024]{1,0:T(8,128)(2,1)S(1)}, bf16[64,1024]{1,0:T(8,128)(2,1)S(1)}, u32[]{:S(2)}, u32[]{:S(2)}) collective-permute-start(bf16[64,1024]{1,0:T(8,128)(2,1)S(1)} %get-tuple-element.32), channel_id=1, source_target_pairs={{0,15},{1,0},{2,1},{3,2},{4,3},{5,4},{6,5},{7,6},{8,7},{9,8},{10,9... | collective-permute-start | bytes 393224 | tf_op jit(solution)/shard_map/ppermute | solution.py:261
  8.1 8.8 %collective-permute-start.4 = (bf16[64,1024]{1,0:T(8,128)(2,1)S(1)}, bf16[64,1024]{1,0:T(8,128)(2,1)S(1)}, u32[]{:S(2)}, u32[]{:S(2)}) collective-permute-start(bf16[64,1024]{1,0:T(8,128)(2,1)S(1)} %get-tuple-element.41), channel_id=1, source_target_pairs={{0,16},{1,17},{2,18},{3,19},{4,20},{5,21},{6,22},{7,23},{8,24},{9,... | collective-permute-start | bytes 393224 | tf_op jit(solution)/shard_map/ppermute | solution.py:261
  10.2 6.7 %collective-permute-start.5 = (bf16[64,1024]{1,0:T(8,128)(2,1)S(1)}, bf16[64,1024]{1,0:T(8,128)(2,1)S(1)}, u32[]{:S(2)}, u32[]{:S(2)}) collective-permute-start(bf16[64,1024]{1,0:T(8,128)(2,1)S(1)} %get-tuple-element.42), channel_id=1, source_target_pairs={{0,16},{1,17},{2,18},{3,19},{4,20},{5,21},{6,22},{7,23},{8,24},{9,... | collective-permute-start | bytes 393224 | tf_op jit(solution)/shard_map/ppermute | solution.py:261
  10.3 6.7 %collective-permute-start.6 = (bf16[64,1024]{1,0:T(8,128)(2,1)S(1)}, bf16[64,1024]{1,0:T(8,128)(2,1)S(1)}, u32[]{:S(2)}, u32[]{:S(2)}) collective-permute-start(bf16[64,1024]{1,0:T(8,128)(2,1)S(1)} %get-tuple-element.43), channel_id=1, source_target_pairs={{0,112},{1,113},{2,114},{3,115},{4,116},{5,117},{6,118},{7,119},{8... | collective-permute-start | bytes 393224 | tf_op jit(solution)/shard_map/ppermute | solution.py:261
  11.3 5.7 %collective-permute-start.7 = (bf16[64,1024]{1,0:T(8,128)(2,1)S(1)}, bf16[64,1024]{1,0:T(8,128)(2,1)S(1)}, u32[]{:S(2)}, u32[]{:S(2)}) collective-permute-start(bf16[64,1024]{1,0:T(8,128)(2,1)S(1)} %get-tuple-element.44), channel_id=1, source_target_pairs={{0,112},{1,113},{2,114},{3,115},{4,116},{5,117},{6,118},{7,119},{8... | collective-permute-start | bytes 393224 | tf_op jit(solution)/shard_map/ppermute | solution.py:261
  12.5 1.4 %copy-start.6 = (s32[1,1,128,2]{2,3,1,0:T(2,128)S(1)}, s32[1,1,128,2]{2,3,1,0:T(2,128)}, u32[]{:S(2)}) copy-start(s32[1,1,128,2]{2,3,1,0:T(2,128)} %param.14) | copy-start | bytes 3076
  12.5 1.4 %copy-start.7 = (s32[2]{0:T(128)S(1)}, s32[2]{0:T(128)}, u32[]{:S(2)}) copy-start(s32[2]{0:T(128)} %shifts_ref) | copy-start | bytes 28
  15.0 4.3 %collective-permute-start.2 = (bf16[56,1024]{1,0:T(8,128)(2,1)S(1)}, bf16[56,1024]{1,0:T(8,128)(2,1)S(1)}, u32[]{:S(2)}, u32[]{:S(2)}) collective-permute-start(bf16[56,1024]{1,0:T(8,128)(2,1)S(1)} %get-tuple-element.37), channel_id=1, source_target_pairs={{0,112},{1,113},{2,114},{3,115},{4,116},{5,117},{6,118},{7,119},{8... | collective-permute-start | bytes 344072 | tf_op jit(solution)/shard_map/ppermute | solution.py:261
  16.9 2.4 %collective-permute-start.3 = (bf16[56,1024]{1,0:T(8,128)(2,1)S(1)}, bf16[56,1024]{1,0:T(8,128)(2,1)S(1)}, u32[]{:S(2)}, u32[]{:S(2)}) collective-permute-start(bf16[56,1024]{1,0:T(8,128)(2,1)S(1)} %get-tuple-element.38), channel_id=1, source_target_pairs={{0,16},{1,17},{2,18},{3,19},{4,20},{5,21},{6,22},{7,23},{8,24},{9,... | collective-permute-start | bytes 344072 | tf_op jit(solution)/shard_map/ppermute | solution.py:261
  17.0 2.4 %copy-start = (bf16[1024,1024]{1,0:T(8,128)(2,1)S(1)}, bf16[1024,1024]{1,0:T(8,128)(2,1)}, u32[]{:S(2)}) copy-start(bf16[1024,1024]{1,0:T(8,128)(2,1)} %wo_ref.1) | copy-start | bytes 6291460
  17.0 2.4 %copy-start.1 = (bf16[1024,64]{0,1:T(8,128)(2,1)S(1)}, bf16[1024,64]{0,1:T(8,128)(2,1)}, u32[]{:S(2)}) copy-start(bf16[1024,64]{0,1:T(8,128)(2,1)} %param.13) | copy-start | bytes 393220
  21.9 31.6 %copy-start.2 = (bf16[1024,512]{1,0:T(8,128)(2,1)S(1)}, bf16[1024,512]{1,0:T(8,128)(2,1)}, u32[]{:S(2)}) copy-start(bf16[1024,512]{1,0:T(8,128)(2,1)} %wg_ref.1) | copy-start | bytes 3145732
  21.9 31.6 %copy-start.3 = (bf16[1024,512]{1,0:T(8,128)(2,1)S(1)}, bf16[1024,512]{1,0:T(8,128)(2,1)}, u32[]{:S(2)}) copy-start(bf16[1024,512]{1,0:T(8,128)(2,1)} %wu_ref.1) | copy-start | bytes 3145732
  22.0 31.6 %copy-start.4 = (bf16[512,1024]{1,0:T(8,128)(2,1)S(1)}, bf16[512,1024]{1,0:T(8,128)(2,1)}, u32[]{:S(2)}) copy-start(bf16[512,1024]{1,0:T(8,128)(2,1)} %wd_ref.1) | copy-start | bytes 3145732
